TPU v7x, 32 devices: a whole 2x2x4 slice. The times are simulated.
32 devices in a mesh: replica: 2 (over x), node: 2 (over core), rank: 8 (over z, y).
Axes of the slice: x: 2, y: 2, z: 4, core: 2. Of those that a mesh axis runs over, the one named last changes fastest.
Arguments:
- hidden_rows: bfloat16 [2048, 3584], P(('replica', 'node', 'rank')), parts along dimension 0, may hold values from -6 to 6
- routes: int32 [2048, 8], P(('replica', 'node', 'rank')), parts along dimension 0, may hold values from 0 to 15, all different within a row; in each aligned block of 64 rows (0 to 63, 64 to 127, ...) at most 48 rows name the same one
- route_weights: float32 [2048, 8], P(('replica', 'node', 'rank')), parts along dimension 0, may hold values from 0.1 to 1
- w_gate: bfloat16 [16, 3584, 1024], P(('node', 'rank')), may hold values from -0.09375 to 0.09375
- w_up: bfloat16 [16, 3584, 1024], P(('node', 'rank')), may hold values from -0.09375 to 0.09375
- w_down: bfloat16 [16, 1024, 3584], P(('node', 'rank')), may hold values from -0.1875 to 0.1875
- queries: bfloat16 [256, 64, 576], P(('replica', 'node', 'rank')), parts along dimension 0, may hold values from -40 to 40
- kv_cache: bfloat16 [256, 256, 576], P(('replica', 'node', 'rank')), parts along dimension 0, may hold values from -5 to 5
- lengths: int32 [256], P(('replica', 'node', 'rank')), parts along dimension 0, may hold values from 2 to 256, as said below
Outputs:
- mixed_rows: bfloat16 [2048, 3584], P(('replica', 'node', 'rank')), parts along dimension 0
- attended: bfloat16 [256, 64, 512], P(('replica', 'node', 'rank')), parts along dimension 0
There are 2 independent parts, one for each index of `replica`. A program takes and returns all parts, laid end to end along the dimension named above; an argument that names none is the same for every part. Nothing has to cross between parts.
Inputs may be any that keep to these rules, and one draw needn't show every extreme that they name: `routes`: each row names 8 different experts; among the 64 rows of one device no expert is named by more than 48 rows, a bound that some block reaches. `lengths`: row 0 has length 256.
All inputs are finite; a program needn't handle non-finite values.
Results may differ from a plain program's by a relative error of at most 0.006.
Values may be sent and summed in bfloat16 or wider, within the bound.
No kernel may reach another device: no remote copies, remote signals or barrier semaphores. Data moves between devices by JAX's collectives and lax.ppermute only.
A program may use at most 128 MiB of HBM per device.

v0:
```python
import jax
import jax.numpy as jnp
from jax import lax
from jax.sharding import PartitionSpec as P

LATENT = 512


score_scale = 192.0 ** (-0.5)


def run_expert(received, w_gate, w_up, w_down):
    model_width = received.shape[-1]
    gathered = received.reshape(-1, model_width)
    gate_term = jnp.dot(gathered, w_gate[0], preferred_element_type=jnp.float32)
    up_term = jnp.dot(gathered, w_up[0], preferred_element_type=jnp.float32)
    hidden = (jax.nn.silu(gate_term) * up_term).astype(jnp.bfloat16)
    produced = jnp.dot(hidden, w_down[0], preferred_element_type=jnp.float32).astype(jnp.bfloat16)
    return produced.reshape(received.shape)


def attend(queries, kv_cache, lengths):
    scores = (
        jnp.einsum("bhc,blc->bhl", queries, kv_cache, preferred_element_type=jnp.float32)
        * score_scale
    )
    visible = lax.broadcasted_iota(jnp.int32, (1, 1, kv_cache.shape[1]), 2) < lengths[:, None, None]
    scores = jnp.where(visible, scores, -jnp.inf)
    row_max = jnp.max(scores, axis=2, keepdims=True)
    exponent = jnp.exp(scores - row_max)
    softmax_weights = (exponent / jnp.sum(exponent, axis=2, keepdims=True)).astype(jnp.bfloat16)
    latent_values = kv_cache[:, :, :LATENT]
    return jnp.einsum(
        "bhl,blc->bhc", softmax_weights, latent_values, preferred_element_type=jnp.float32
    ).astype(jnp.bfloat16)


def local(hidden_rows, routes, route_weights, w_gate, w_up, w_down, queries, kv_cache, lengths):
    tokens = hidden_rows.shape[0]
    chosen = routes.shape[1]
    model_width = hidden_rows.shape[1]
    node_count = lax.axis_size("node")
    rank_count = lax.axis_size("rank")
    experts = node_count * rank_count * w_gate.shape[0]
    capacity = 3 * tokens * chosen // (2 * experts)
    attended = attend(queries, kv_cache, lengths)
    flat_routes = routes.reshape(-1)
    one_hot = (flat_routes[:, None] == jnp.arange(experts, dtype=jnp.int32)[None, :]).astype(
        jnp.int32
    )
    position = jnp.sum((jnp.cumsum(one_hot, axis=0) - 1) * one_hot, axis=1)
    slot_index = flat_routes * capacity + position
    selector = (
        slot_index[:, None] == jnp.arange(experts * capacity, dtype=jnp.int32)[None, :]
    ).astype(jnp.bfloat16)
    by_choice = selector.reshape(tokens, chosen, experts * capacity)
    by_token = jnp.sum(by_choice, axis=1)
    combine_matrix = jnp.sum(by_choice.astype(jnp.float32) * route_weights[:, :, None], axis=1)
    outgoing = jnp.einsum(
        "ts,td->sd", by_token, hidden_rows, preferred_element_type=jnp.float32
    ).astype(jnp.bfloat16)
    produced = run_expert(
        lax.all_to_all(
            outgoing.reshape(experts, capacity, model_width),
            ("node", "rank"),
            split_axis=0,
            concat_axis=0,
            tiled=True,
        ),
        w_gate,
        w_up,
        w_down,
    )
    returned = lax.all_to_all(produced, ("node", "rank"), split_axis=0, concat_axis=0, tiled=True)
    returned = returned.reshape(experts * capacity, model_width)
    mixed_rows = jnp.dot(
        combine_matrix,
        returned.astype(jnp.float32),
        precision=lax.Precision.HIGHEST,
        preferred_element_type=jnp.float32,
    ).astype(jnp.bfloat16)
    return (mixed_rows, attended)


def solution(mesh):
    return jax.shard_map(
        local,
        mesh=mesh,
        in_specs=(
            P(("replica", "node", "rank"), None),
            P(("replica", "node", "rank"), None),
            P(("replica", "node", "rank"), None),
            P(("node", "rank"), None, None),
            P(("node", "rank"), None, None),
            P(("node", "rank"), None, None),
            P(("replica", "node", "rank"), None, None),
            P(("replica", "node", "rank"), None, None),
            P(("replica", "node", "rank")),
        ),
        out_specs=(
            P(("replica", "node", "rank"), None),
            P(("replica", "node", "rank"), None, None),
        ),
        check_vma=False,
    )
```

profile of v0, /device:TPU:0, one launch (start us, length us, event | category | flops | bytes accessed | tf_op | source)
XLA Modules:
  0.0 294.9 jit_solution(4562547989957626468)
XLA Ops:
  0.6 0.0 copy-start
  0.6 0.8 copy.28
  1.5 0.1 eq.43
  1.6 0.1 eq.39
  1.7 1.2 reduce-window.6
  2.8 0.2 slice_reduce_fusion
  3.1 0.1 fusion.27
  3.2 0.1 reduce_sum.42
  3.3 0.1 copy.31
  3.3 0.7 multiply_add_fusion
  4.1 0.1 copy.32
  4.1 0.0 copy-start.3
  4.1 0.5 fusion.24
  4.7 0.0 slice-start
  4.7 2.8 convolution_convert_fusion
  7.5 0.0 slice-start.1
  7.5 130.2 %all_to_all.10 = bf16[16,48,3584]{2,1,0:T(8,128)(2,1)S(1)} all-to-all(bf16[16,48,3584]{2,1,0:T(8,128)(2,1)S(1)} %bitcast.44), channel_id=1, replica_groups=mesh['replica'=2,'node'=2,'rank'=8] {'node','rank'}, dimensions={0} | all-to-all | bytes 11010048 | tf_op jit(solution)/shard_map/all_to_all | solution.py:63
  137.7 0.0 copy-done.3
  137.7 0.0 copy-start.1
  137.7 2.5 copy-done.1
  140.1 0.0 slice-done
  140.1 0.0 slice-done.1
  140.1 7.6 %fusion.3 = f32[768,1024]{1,0:T(8,128)} fusion(bf16[768,3584]{1,0:T(8,128)(2,1)S(1)} %bitcast.46, bf16[1,3584,1024]{2,1,0:T(8,128)(2,1)S(1)} %bitcast.49), kind=kOutput, calls=%fused_computation.3 | convolution fusion | flops 5637144576 | bytes 15990784 | tf_op jit(solution)/shard_map/dot_general | solution.py:16
  147.7 20.0 %fusion.7 = bf16[768,3584]{1,0:T(8,128)(2,1)} fusion(bf16[1,1024,3584]{2,1,0:T(8,128)(2,1)} %param.14, f32[768,1024]{1,0:T(8,128)} %fusion.3, bf16[768,3584]{1,0:T(8,128)(2,1)} %bitcast.47, bf16[1,3584,1024]{2,1,0:T(8,128)(2,1)} %param.12), kind=kOutput, calls=%fused_computation.8 | convolution fusion | flops 11281760256 | bytes 28835840 | tf_op jit(solution)/shard_map/dot_general | solution.py:18
  167.7 0.0 copy-start.4
  167.7 0.0 copy-start.5
  167.7 0.0 copy-start.2
  167.7 4.9 %all-to-all-start.1 = ((bf16[16,48,3584]{2,1,0:T(8,128)(2,1)}), bf16[16,48,3584]{2,1,0:T(8,128)(2,1)}, u32[]{:S(2)}, u32[]{:S(2)}) async-start(bf16[16,48,3584]{2,1,0:T(8,128)(2,1)} %bitcast.45), calls=%async_computation.1 | async-start | bytes 11010048 | tf_op jit(solution)/shard_map/all_to_all | solution.py:74
  172.7 0.0 copy-done.4
  172.7 0.7 copy.33
  173.4 0.0 copy-done.5
  173.4 0.1 iota_compare_fusion.3
  173.5 0.0 copy-done
  173.5 0.0 copy-done.2
  173.5 0.6 fusion.23
  174.0 0.2 fusion.31
  174.3 2.1 multiply_reduce_fusion
  176.4 1.8 fusion.18
  178.2 110.4 %all-to-all-done.1 = bf16[16,48,3584]{2,1,0:T(8,128)(2,1)} async-done(((bf16[16,48,3584]{2,1,0:T(8,128)(2,1)}), bf16[16,48,3584]{2,1,0:T(8,128)(2,1)}, u32[]{:S(2)}, u32[]{:S(2)}) %all-to-all-start.1) | async-done | bytes 5505056 | tf_op jit(solution)/shard_map/all_to_all | solution.py:74
  288.5 6.4 %convolution_convert_fusion.1 = bf16[64,3584]{1,0:T(8,128)(2,1)} fusion(f32[64,768]{1,0:T(8,128)} %multiply_reduce_fusion, bf16[768,3584]{1,0:T(8,128)(2,1)} %bitcast.7), kind=kOutput, calls=%fused_computation.9 | convolution fusion | flops 2114158592 | bytes 6160384 | tf_op jit(solution)/shard_map/dot_general | solution.py:76
  (4 shorter events, 0.0 us)
Async XLA Ops:
  0.6 172.8 %copy-start = (bf16[8,64,576]{2,1,0:T(8,128)(2,1)S(1)}, bf16[8,64,576]{2,1,0:T(8,128)(2,1)}, u32[]{:S(2)}) copy-start(bf16[8,64,576]{2,1,0:T(8,128)(2,1)} %param.15) | copy-start | bytes 1769476
  4.1 133.5 %copy-start.3 = (s32[64,8]{1,0:T(8,128)}, s32[64,8]{1,0:T(8,128)S(1)}, u32[]{:S(2)}) copy-start(s32[64,8]{1,0:T(8,128)S(1)} %copy.32) | copy-start | bytes 6148
  4.7 135.4 %slice-start = ((s8[7340032]{0:T(1024)(128)(4,1)}), s8[4194304]{0:T(1024)(128)(4,1)S(1)}, s32[]{:S(2)}) async-start(s8[7340032]{0:T(1024)(128)(4,1)} %bitcast.48), calls=%async_computation.2 | async-start | bytes 8388608
  7.5 132.7 %slice-start.1 = ((s8[7340032]{0:T(1024)(128)(4,1)}), s8[3145728]{0:T(1024)(128)(4,1)S(1)}, s32[]{:S(2)}) async-start(s8[7340032]{0:T(1024)(128)(4,1)} %bitcast.48), calls=%async_computation.3 | async-start | bytes 6291456
  137.7 2.5 copy-start.1
  167.7 5.0 %copy-start.4 = (f32[64,8]{0,1:T(8,128)S(1)}, f32[64,8]{0,1:T(8,128)}, u32[]{:S(2)}) copy-start(f32[64,8]{0,1:T(8,128)} %param.11) | copy-start | bytes 6148
  167.7 5.7 %copy-start.5 = (s32[8]{0:T(128)S(1)}, s32[8]{0:T(128)}, u32[]{:S(2)}) copy-start(s32[8]{0:T(128)} %param.17) | copy-start | bytes 100
  167.7 5.7 %copy-start.2 = (bf16[8,256,576]{1,2,0:T(8,128)(2,1)S(1)}, bf16[8,256,576]{1,2,0:T(8,128)(2,1)}, u32[]{:S(2)}) copy-start(bf16[8,256,576]{1,2,0:T(8,128)(2,1)} %param.16) | copy-start | bytes 7077892
  167.7 120.8 %all-to-all-start.1 = ((bf16[16,48,3584]{2,1,0:T(8,128)(2,1)}), bf16[16,48,3584]{2,1,0:T(8,128)(2,1)}, u32[]{:S(2)}, u32[]{:S(2)}) async-start(bf16[16,48,3584]{2,1,0:T(8,128)(2,1)} %bitcast.45), calls=%async_computation.1 | async-start | bytes 11010048 | tf_op jit(solution)/shard_map/all_to_all | solution.py:74
where the time goes:
time: 300 us; the launch traced here: 295 us
  blocking collectives  130 us (43%)
  waiting for transfers between devices  110 us (37%)
  matrix products  39.1 us (13%)
  starting transfers between devices  4.94 us (2%)
  other arithmetic  4.93 us (2%)
  local copies, waits for them, and re-layouts  4.67 us (2%)
    all_to_all x1, blocking collectives, local(): lax.all_to_all(outgoing.reshape(experts, capacity, model_width), ('node',...  130 us
    all_to_all x1, waiting for transfers between devices, local(): lax.all_to_all(produced, ('node', 'rank'), split_axis=0, concat_axis=0, t...  110 us
    dot_general x1, matrix products, run_expert(): jnp.dot(hidden, w_down[0], preferred_element_type=jnp.float32)  20 us
    dot_general x1, matrix products, run_expert(): up_term = jnp.dot(gathered, w_up[0], preferred_element_type=jnp.float32)  7.58 us
    dot_general x1, matrix products, local(): jnp.dot(combine_matrix, returned.astype(jnp.float32), precision=lax.Preci...  6.39 us
  transfers between devices with their start and end apart: 1, of which 1 were waited for; matrix products, arithmetic and copies ran while one was open for 2% of the time, Pallas kernels for 0%

commit v1 on v0

v1 whole, which is shorter than its diff:
```python
import jax
import jax.numpy as jnp
from jax import lax
from jax.experimental import pallas as pl
from jax.experimental.pallas import tpu as pltpu
from jax.sharding import PartitionSpec as P

LATENT = 512
PAIR = 2


score_scale = 192.0 ** (-0.5)


def attend(queries, kv_cache, lengths):
    scores = (
        jnp.einsum("bhc,blc->bhl", queries, kv_cache, preferred_element_type=jnp.float32)
        * score_scale
    )
    visible = lax.broadcasted_iota(jnp.int32, (1, 1, kv_cache.shape[1]), 2) < lengths[:, None, None]
    scores = jnp.where(visible, scores, -jnp.inf)
    row_max = jnp.max(scores, axis=2, keepdims=True)
    exponent = jnp.exp(scores - row_max)
    softmax_weights = (exponent / jnp.sum(exponent, axis=2, keepdims=True)).astype(jnp.bfloat16)
    latent_values = kv_cache[:, :, :LATENT]
    return jnp.einsum(
        "bhl,blc->bhc", softmax_weights, latent_values, preferred_element_type=jnp.float32
    ).astype(jnp.bfloat16)


def expert_kernel(own, other, own_y, other_y, weight, gate, up, down, keep, send, rows, total):
    step = pl.program_id(0)
    tokens = own.shape[0]

    @pl.when(step == 0)
    def _():
        for place, block in enumerate((own, own_y, other, other_y)):
            rows[place * tokens : (place + 1) * tokens, :] = block[...]

    gate_term = jnp.dot(rows[...], gate[0], preferred_element_type=jnp.float32)
    up_term = jnp.dot(rows[...], up[0], preferred_element_type=jnp.float32)
    hidden = (gate_term / (1.0 + jnp.exp(-gate_term)) * up_term).astype(jnp.bfloat16)
    part = jnp.dot(hidden, down[0], preferred_element_type=jnp.float32)

    @pl.when(step == 0)
    def _():
        total[...] = part

    @pl.when(step > 0)
    def _():
        total[...] += part

    @pl.when(step == pl.num_programs(0) - 1)
    def _():
        half = 2 * tokens
        for place, out in enumerate((keep, send)):
            span = slice(place * half, (place + 1) * half)
            produced = total[span, :].astype(jnp.bfloat16).astype(jnp.float32)
            out[...] = (produced * weight[span, :]).astype(jnp.bfloat16)


def run_expert(blocks, weight, w_gate, w_up, w_down):
    tokens, model_width = blocks[0].shape
    hidden_width = w_gate.shape[2]
    tile = 256
    whole = pl.BlockSpec((tokens, model_width), lambda f: (0, 0))
    half = pl.BlockSpec((2 * tokens, model_width), lambda f: (0, 0))
    return pl.pallas_call(
        expert_kernel,
        grid=(hidden_width // tile,),
        out_shape=[jax.ShapeDtypeStruct((2 * tokens, model_width), jnp.bfloat16)] * 2,
        in_specs=[whole] * 4
        + [
            pl.BlockSpec((4 * tokens, 1), lambda f: (0, 0)),
            pl.BlockSpec((1, model_width, tile), lambda f: (0, 0, f)),
            pl.BlockSpec((1, model_width, tile), lambda f: (0, 0, f)),
            pl.BlockSpec((1, tile, model_width), lambda f: (0, f, 0)),
        ],
        out_specs=[half, half],
        scratch_shapes=[
            pltpu.VMEM((4 * tokens, model_width), jnp.bfloat16),
            pltpu.VMEM((4 * tokens, model_width), jnp.float32),
        ],
        compiler_params=pltpu.CompilerParams(vmem_limit_bytes=40 * 1024 * 1024),
        cost_estimate=pl.CostEstimate(
            flops=2 * 3 * 4 * tokens * model_width * hidden_width,
            bytes_accessed=3 * 2 * model_width * hidden_width + 16 * tokens * model_width,
            transcendentals=4 * tokens * hidden_width,
        ),
    )(*blocks, weight, w_gate, w_up, w_down)


def local(hidden_rows, routes, route_weights, w_gate, w_up, w_down, queries, kv_cache, lengths):
    tokens = hidden_rows.shape[0]
    node_count = lax.axis_size("node")
    rank_count = lax.axis_size("rank")
    experts = node_count * rank_count * w_gate.shape[0]
    steps = rank_count // PAIR
    f32, bf16 = jnp.float32, jnp.bfloat16

    def core(value):
        return lax.ppermute(value, "node", [(i, 1 - i) for i in range(node_count)])

    def pair(value):
        return lax.ppermute(value, "rank", [(i, i ^ 1) for i in range(rank_count)])

    def ring(value):
        return lax.ppermute(value, "rank", [(i, (i + PAIR) % rank_count) for i in range(rank_count)])

    chosen = routes[:, :, None] == jnp.arange(experts, dtype=jnp.int32)[None, None, :]
    dense = jnp.sum(jnp.where(chosen, route_weights[:, :, None], 0.0), axis=1)
    mine = lax.all_to_all(
        dense.T.reshape(experts, tokens), ("node", "rank"), split_axis=0, concat_axis=0, tiled=True
    ).reshape(node_count, rank_count, tokens)
    node, rank = lax.axis_index("node"), lax.axis_index("rank")

    def weight_of(slot):
        at = lax.rem(rank // PAIR - slot + steps, steps) * PAIR
        here = lax.rem(rank, PAIR)
        order = [(node, at + here), (node, at + 1 - here), (1 - node, at + here), (1 - node, at + 1 - here)]
        return jnp.concatenate([mine[n, r] for n, r in order])[:, None]

    own = [hidden_rows]
    for _ in range(steps - 1):
        own.append(ring(own[-1]))
    partial = []
    for slot in range(steps):
        own_y = pair(own[slot])
        blocks = (own[slot], core(own[slot]), own_y, core(own_y))
        partial.append(run_expert(blocks, weight_of(slot), w_gate, w_up, w_down))

    attended = attend(queries, kv_cache, lengths)

    def reduced(slot):
        keep, send = partial[slot]
        got = core(send)
        away = (keep[tokens:].astype(f32) + got[tokens:].astype(f32)).astype(bf16)
        back = pair(away)
        return keep[:tokens].astype(f32) + got[:tokens].astype(f32) + back.astype(f32)

    carried = None
    for slot in list(range(1, steps)) + [0]:
        value = reduced(slot)
        if carried is not None:
            value = value + carried.astype(f32)
        value = value.astype(bf16)
        carried = ring(value) if slot else value
    return (carried, attended)


def solution(mesh):
    return jax.shard_map(
        local,
        mesh=mesh,
        in_specs=(
            P(("replica", "node", "rank"), None),
            P(("replica", "node", "rank"), None),
            P(("replica", "node", "rank"), None),
            P(("node", "rank"), None, None),
            P(("node", "rank"), None, None),
            P(("node", "rank"), None, None),
            P(("replica", "node", "rank"), None, None),
            P(("replica", "node", "rank"), None, None),
            P(("replica", "node", "rank")),
        ),
        out_specs=(
            P(("replica", "node", "rank"), None),
            P(("replica", "node", "rank"), None, None),
        ),
        check_vma=False,
    )
```

time: 300 us -> 153 us (0.51); the launches traced: 295 us -> 152 us
  blocking collectives: 130 us -> 0 us
  waiting for transfers between devices: 110 us -> 54 us
  Pallas kernels: 0 us -> 47.1 us
  matrix products: 39.1 us -> 4.02 us
  starting transfers between devices: 4.94 us -> 26.1 us
  local copies, waits for them, and re-layouts: 4.67 us -> 11.4 us
  other arithmetic: 4.93 us -> 8.68 us
    all_to_all x1 -> x0, blocking collectives: 130 us -> none  [local(): lax.all_to_all(outgoing.reshape(experts, capacity, model_width), ('node',...]
    all_to_all x1, waiting for transfers between devices: 110 us -> 5.9 us  [local(): lax.all_to_all(dense.T.reshape(experts, tokens), ('node', 'rank'), split_...]
    ppermute x0 -> x26, waiting for transfers between devices: none -> 48.1 us  [the longest x6 26.2 us: ring(): lax.ppermute(value, 'rank', [(i, (i + PAIR) % rank_count) for i in range(...]
    pallas_call x0 -> x4, Pallas kernels: none -> 47.1 us  [run_expert(): pl.pallas_call(expert_kernel, grid=(hidden_width // tile,), out_shape=[ja...]
    dot_general x4 -> x0, matrix products: 36.8 us -> none  [the longest x1 20 us: run_expert(): jnp.dot(hidden, w_down[0], preferred_element_type=jnp.float32)]
    ppermute x0 -> x26, starting transfers between devices: none -> 21.9 us  [the longest x6 10.4 us: ring(): lax.ppermute(value, 'rank', [(i, (i + PAIR) % rank_count) for i in range(...]
    convert_element_type x1 -> x8, other arithmetic: 0.01 us -> 6.89 us  [the longest x4 4.55 us: local(): value = value.astype(bf16)]
    unnamed x18 -> x28, local copies, waits for them, and re-layouts: 4.03 us -> 10.8 us
  transfers between devices with their start and end apart: 1 -> 27, of which waited for: 1 -> 10; matrix products, arithmetic and copies ran while one was open for 2% -> 7% of each run, Pallas kernels for 0% -> 31%
where the time goes in v1:
time: 153 us; the launch traced here: 152 us
  waiting for transfers between devices  54 us (35%)
  Pallas kernels  47.1 us (31%)
  starting transfers between devices  26.1 us (17%)
  local copies, waits for them, and re-layouts  11.4 us (7%)
  other arithmetic  8.68 us (6%)
  matrix products  4.02 us (3%)
    pallas_call x4, Pallas kernels, run_expert(): pl.pallas_call(expert_kernel, grid=(hidden_width // tile,), out_shape=[ja...  47.1 us
    ppermute x6, waiting for transfers between devices, ring(): lax.ppermute(value, 'rank', [(i, (i + PAIR) % rank_count) for i in range(...  26.2 us
    ppermute x8, waiting for transfers between devices, pair(): return lax.ppermute(value, 'rank', [(i, i ^ 1) for i in range(rank_count)])  21.6 us
    unnamed x28, local copies, waits for them, and re-layouts  10.8 us
    ppermute x6, starting transfers between devices, ring(): lax.ppermute(value, 'rank', [(i, (i + PAIR) % rank_count) for i in range(...  10.4 us
    ppermute x8, starting transfers between devices, pair(): return lax.ppermute(value, 'rank', [(i, i ^ 1) for i in range(rank_count)])  9.23 us
    all_to_all x1, waiting for transfers between devices, local(): lax.all_to_all(dense.T.reshape(experts, tokens), ('node', 'rank'), split_...  5.9 us
    convert_element_type x4, other arithmetic, local(): value = value.astype(bf16)  4.55 us
  transfers between devices with their start and end apart: 27, of which 10 were waited for; matrix products, arithmetic and copies ran while one was open for 7% of the time, Pallas kernels for 31%

profile of v1, /device:TPU:0, one launch (start us, length us, event | category | flops | bytes accessed | tf_op | source)
XLA Modules:
  0.0 152.1 jit_solution(2426830517612424906)
XLA Ops:
  0.6 3.1 %collective-permute-start.5 = (bf16[64,3584]{1,0:T(8,128)(2,1)}, bf16[64,3584]{1,0:T(8,128)(2,1)}, u32[]{:S(2)}, u32[]{:S(2)}) collective-permute-start(bf16[64,3584]{1,0:T(8,128)(2,1)} %own.1), channel_id=1, source_target_pairs={{0,2},{1,3},{2,4},{3,5},{4,6},{5,7},{6,0},{7,1},{8,10},{9,11},{10,... | collective-permute-start | bytes 1376264 | tf_op jit(solution)/shard_map/ppermute | solution.py:108
  3.7 12.9 %collective-permute-done.5.own = bf16[64,3584]{1,0:T(8,128)(2,1)} collective-permute-done((bf16[64,3584]{1,0:T(8,128)(2,1)}, bf16[64,3584]{1,0:T(8,128)(2,1)}, u32[]{:S(2)}, u32[]{:S(2)}) %collective-permute-start.5) | collective-permute-done | bytes 458784 | tf_op jit(solution)/shard_map/ppermute | solution.py:108
  16.6 1.5 collective-permute-start.19
  18.1 0.5 collective-permute-start.1
  18.6 11.6 %collective-permute-done.19.own_y = bf16[64,3584]{1,0:T(8,128)(2,1)S(1)} collective-permute-done((bf16[64,3584]{1,0:T(8,128)(2,1)}, bf16[64,3584]{1,0:T(8,128)(2,1)S(1)}, u32[]{:S(2)}, u32[]{:S(2)}) %collective-permute-start.19) | collective-permute-done | bytes 458784 | tf_op jit(solution)/shard_map/ppermute | solution.py:105
  30.3 1.3 select_reduce_fusion
  31.6 4.2 %all-to-all-start = ((f32[16,1,64]{2,1,0:T(1,128)}), f32[16,1,64]{2,1,0:T(1,128)S(1)}, u32[]{:S(2)}, u32[]{:S(2)}) async-start(f32[16,1,64]{2,1,0:T(1,128)} %bitcast.2), calls=%async_computation | async-start | bytes 16384 | tf_op jit(solution)/shard_map/all_to_all | solution.py:112
  35.8 0.4 collective-permute-start
  36.2 5.9 %all-to-all-done = f32[16,1,64]{2,1,0:T(1,128)S(1)} async-done(((f32[16,1,64]{2,1,0:T(1,128)}), f32[16,1,64]{2,1,0:T(1,128)S(1)}, u32[]{:S(2)}, u32[]{:S(2)}) %all-to-all-start) | async-done | bytes 4128 | tf_op jit(solution)/shard_map/all_to_all | solution.py:112
  42.1 0.1 pad_maximum_fusion.2
  42.2 0.1 copy.32.weight
  42.3 0.6 collective-permute-start.6
  43.0 0.8 copy-done.6
  43.8 0.8 copy-done.8
  44.5 3.1 %copy-done.1 = bf16[1,3584,1024]{2,1,0:T(8,128)(2,1)S(1)} copy-done((bf16[1,3584,1024]{2,1,0:T(8,128)(2,1)S(1)}, bf16[1,3584,1024]{2,1,0:T(8,128)(2,1)}, u32[]{:S(2)}) %copy-start.1) | copy-done | bytes 7340056
  47.6 1.0 copy-done.7
  48.6 1.0 copy-done.9
  49.7 12.4 %shard_map.107 = (bf16[128,3584]{1,0:T(8,128)(2,1)S(1)}, bf16[128,3584]{1,0:T(8,128)(2,1)}) custom-call(bf16[64,3584]{1,0:T(8,128)(2,1)} %collective-permute-done.5.own, bf16[64,3584]{1,0:T(8,128)(2,1)S(1)} %copy-done.7, bf16[64,3584]{1,0:T(8,128)(2,1)S(1)} %collective-permute-done.19.own_y, bf16[64,3584]{1,0:T(8,128)(2,1)S(1)} %copy-done.9, ...), custom_call_target="tpu_custom_call" | custom-call | flops 5637144576 | bytes 25690112 | tf_op jit(solution)/shard_map/pallas_call | solution.py:68
  62.1 0.5 collective-permute-start.21
  62.6 0.1 iota_compare_fusion.1
  62.6 0.1 copy.31.weight
  62.8 0.1 pad_maximum_fusion
  62.9 0.1 copy.30.weight
  63.0 0.1 copy.29.weight
  63.2 0.6 collective-permute-start.14
  63.8 0.6 collective-permute-start.7
  64.4 3.1 %copy-done.2 = bf16[1,3584,1024]{2,1,0:T(8,128)(2,1)S(1)} copy-done((bf16[1,3584,1024]{2,1,0:T(8,128)(2,1)S(1)}, bf16[1,3584,1024]{2,1,0:T(8,128)(2,1)}, u32[]{:S(2)}) %copy-start.2) | copy-done | bytes 7340056
  67.5 1.0 copy-done.5
  68.5 11.7 %shard_map.104 = (bf16[128,3584]{1,0:T(8,128)(2,1)S(1)}, bf16[128,3584]{1,0:T(8,128)(2,1)S(1)}) custom-call(bf16[64,3584]{1,0:T(8,128)(2,1)S(1)} %copy-done.3, bf16[64,3584]{1,0:T(8,128)(2,1)} %collective-permute-done.other, bf16[64,3584]{1,0:T(8,128)(2,1)S(1)} %copy-done.5, bf16[64,3584]{1,0:T(8,128)(2,1)} %collective-permute-done.2.other_y, ...), custom_call_target="tpu_custom_call" | custom-call | flops 5637144576 | bytes 25690112 | tf_op jit(solution)/shard_map/pallas_call | solution.py:68
  80.2 0.1 collective-permute-start.3
  80.2 0.5 collective-permute-start.13
  80.7 0.1 collective-permute-start.8
  80.8 1.5 collective-permute-start.9
  82.3 0.2 collective-permute-start.15
  82.5 1.1 add_convert_fusion.4
  83.6 0.3 collective-permute-done.13.other
  83.9 1.5 collective-permute-start.22
  85.3 11.5 %shard_map.106 = (bf16[128,3584]{1,0:T(8,128)(2,1)S(1)}, bf16[128,3584]{1,0:T(8,128)(2,1)S(1)}) custom-call(bf16[64,3584]{1,0:T(8,128)(2,1)} %collective-permute-done.6.own, bf16[64,3584]{1,0:T(8,128)(2,1)S(1)} %collective-permute-done.13.other, bf16[64,3584]{1,0:T(8,128)(2,1)S(1)} %collective-permute-done.14.own_y, ...), custom_call_target="tpu_custom_call" | custom-call | flops 5637144576 | bytes 25690112 | tf_op jit(solution)/shard_map/pallas_call | solution.py:68
  96.9 0.1 collective-permute-start.16
  97.0 0.4 collective-permute-start.10
  97.4 6.1 %collective-permute-done.22 = bf16[64,3584]{1,0:T(8,128)(2,1)S(1)} collective-permute-done((bf16[64,3584]{1,0:T(8,128)(2,1)S(1)}, bf16[64,3584]{1,0:T(8,128)(2,1)S(1)}, u32[]{:S(2)}, u32[]{:S(2)}) %collective-permute-start.22) | collective-permute-done | bytes 458784 | tf_op jit(solution)/shard_map/ppermute | solution.py:105
  103.5 1.2 add_convert_fusion.3
  104.7 0.8 collective-permute-start.23
  105.5 0.1 add_convert_fusion.5
  105.6 1.6 %collective-permute-start.17 = (bf16[64,3584]{1,0:T(8,128)(2,1)S(1)}, bf16[64,3584]{1,0:T(8,128)(2,1)S(1)}, u32[]{:S(2)}, u32[]{:S(2)}) collective-permute-start(bf16[64,3584]{1,0:T(8,128)(2,1)S(1)} %add_convert_fusion.5), channel_id=1, source_target_pairs={{0,1},{1,0},{2,3},{3,2},{4,5},{5,4},{6,7},{7,6},{8,9},{9,8},{10,11... | collective-permute-start | bytes 1376264 | tf_op jit(solution)/shard_map/ppermute | solution.py:105
  107.2 11.5 %shard_map.105 = (bf16[128,3584]{1,0:T(8,128)(2,1)S(1)}, bf16[128,3584]{1,0:T(8,128)(2,1)S(1)}) custom-call(bf16[64,3584]{1,0:T(8,128)(2,1)S(1)} %collective-permute-done.7.own, bf16[64,3584]{1,0:T(8,128)(2,1)S(1)} %collective-permute-done.8.other, bf16[64,3584]{1,0:T(8,128)(2,1)S(1)} %collective-permute-done.9.own_y, ...), custom_call_target="tpu_custom_call" | custom-call | flops 5637144576 | bytes 25690112 | tf_op jit(solution)/shard_map/pallas_call | solution.py:68
  118.6 0.1 collective-permute-start.11
  118.7 0.1 collective-permute-done.23
  118.8 0.2 add_convert_fusion.2
  119.1 3.2 %collective-permute-start.24 = (bf16[64,3584]{1,0:T(8,128)(2,1)S(1)}, bf16[64,3584]{1,0:T(8,128)(2,1)S(1)}, u32[]{:S(2)}, u32[]{:S(2)}) collective-permute-start(bf16[64,3584]{1,0:T(8,128)(2,1)S(1)} %add_convert_fusion.2), channel_id=1, source_target_pairs={{0,2},{1,3},{2,4},{3,5},{4,6},{5,7},{6,0},{7,1},{8,10},{9,11},{10,... | collective-permute-start | bytes 1376264 | tf_op jit(solution)/shard_map/ppermute | solution.py:108
  122.3 0.1 add_convert_fusion.6
  122.4 0.6 collective-permute-start.12
  123.0 1.0 add_convert_fusion.7
  124.0 1.5 collective-permute-start.4
  125.5 8.3 %collective-permute-done.24 = bf16[64,3584]{1,0:T(8,128)(2,1)S(1)} collective-permute-done((bf16[64,3584]{1,0:T(8,128)(2,1)S(1)}, bf16[64,3584]{1,0:T(8,128)(2,1)S(1)}, u32[]{:S(2)}, u32[]{:S(2)}) %collective-permute-start.24) | collective-permute-done | bytes 458784 | tf_op jit(solution)/shard_map/ppermute | solution.py:108
  133.7 2.1 %collective-permute-done.12 = bf16[64,3584]{1,0:T(8,128)(2,1)S(1)} collective-permute-done((bf16[64,3584]{1,0:T(8,128)(2,1)S(1)}, bf16[64,3584]{1,0:T(8,128)(2,1)S(1)}, u32[]{:S(2)}, u32[]{:S(2)}) %collective-permute-start.12) | collective-permute-done | bytes 458784 | tf_op jit(solution)/shard_map/ppermute | solution.py:105
  135.8 1.0 add_convert_fusion.1
  136.8 2.2 %collective-permute-start.25 = (bf16[64,3584]{1,0:T(8,128)(2,1)}, bf16[64,3584]{1,0:T(8,128)(2,1)}, u32[]{:S(2)}, u32[]{:S(2)}) collective-permute-start(bf16[64,3584]{1,0:T(8,128)(2,1)} %add_convert_fusion.1), channel_id=1, source_target_pairs={{0,2},{1,3},{2,4},{3,5},{4,6},{5,7},{6,0},{7,1},{8,10},{9,11},{10,... | collective-permute-start | bytes 1376264 | tf_op jit(solution)/shard_map/ppermute | solution.py:108
  138.9 0.5 fusion.8
  139.5 0.2 fusion.27
  139.8 3.5 %fusion.3 = bf16[8,64,512]{2,1,0:T(8,128)(2,1)} fusion(bf16[8,256,576]{1,2,0:T(8,128)(2,1)} %param.16, f32[8,64]{1,0:T(8,128)S(1)} %fusion.27, f32[8,64,256]{2,1,0:T(8,128)S(1)} %fusion.8), kind=kOutput, calls=%fused_computation.3 | convolution fusion | flops 134873856 | bytes 3674112 | tf_op jit(solution)/shard_map/bhl,blc->bhc/dot_general | solution.py:26
  143.2 1.8 %collective-permute-done.4 = bf16[64,3584]{1,0:T(8,128)(2,1)} collective-permute-done((bf16[64,3584]{1,0:T(8,128)(2,1)}, bf16[64,3584]{1,0:T(8,128)(2,1)}, u32[]{:S(2)}, u32[]{:S(2)}) %collective-permute-start.4) | collective-permute-done | bytes 458784 | tf_op jit(solution)/shard_map/ppermute | solution.py:105
  145.0 5.0 %collective-permute-done.25 = bf16[64,3584]{1,0:T(8,128)(2,1)} collective-permute-done((bf16[64,3584]{1,0:T(8,128)(2,1)}, bf16[64,3584]{1,0:T(8,128)(2,1)}, u32[]{:S(2)}, u32[]{:S(2)}) %collective-permute-start.25) | collective-permute-done | bytes 458784 | tf_op jit(solution)/shard_map/ppermute | solution.py:108
  150.0 2.1 %add_convert_fusion = bf16[64,3584]{1,0:T(8,128)(2,1)} fusion(bf16[64,3584]{1,0:T(8,128)(2,1)} %collective-permute-done.25, bf16[64,3584]{1,0:T(8,128)(2,1)} %collective-permute-done.4, bf16[128,3584]{1,0:T(8,128)(2,1)S(1)} %copy-done.12, bf16[128,3584]{1,0:T(8,128)(2,1)S(1)} %get-tuple-element.10), kind=kLoop, calls=%fused_computation.8 | loop fusion | flops 1835008 | bytes 2293760 | tf_op jit(solution)/shard_map/convert_element_type | solution.py:146
  (42 shorter events, 0.1 us)
Async XLA Ops:
  0.6 138.3 %copy-start = (bf16[8,64,576]{2,1,0:T(8,128)(2,1)S(1)}, bf16[8,64,576]{2,1,0:T(8,128)(2,1)}, u32[]{:S(2)}) copy-start(bf16[8,64,576]{2,1,0:T(8,128)(2,1)} %param.15) | copy-start | bytes 1769476
  0.6 15.9 %collective-permute-start.5 = (bf16[64,3584]{1,0:T(8,128)(2,1)}, bf16[64,3584]{1,0:T(8,128)(2,1)}, u32[]{:S(2)}, u32[]{:S(2)}) collective-permute-start(bf16[64,3584]{1,0:T(8,128)(2,1)} %own.1), channel_id=1, source_target_pairs={{0,2},{1,3},{2,4},{3,5},{4,6},{5,7},{6,0},{7,1},{8,10},{9,11},{10,... | collective-permute-start | bytes 1376264 | tf_op jit(solution)/shard_map/ppermute | solution.py:108
  16.6 13.7 %collective-permute-start.19 = (bf16[64,3584]{1,0:T(8,128)(2,1)}, bf16[64,3584]{1,0:T(8,128)(2,1)S(1)}, u32[]{:S(2)}, u32[]{:S(2)}) collective-permute-start(bf16[64,3584]{1,0:T(8,128)(2,1)} %collective-permute-done.5.own), channel_id=1, source_target_pairs={{0,1},{1,0},{2,3},{3,2},{4,5},{5,4},{6,7},{7,6},{8,9},{9,8},{10,11... | collective-permute-start | bytes 1376264 | tf_op jit(solution)/shard_map/ppermute | solution.py:105
  18.1 24.8 %collective-permute-start.1 = (bf16[64,3584]{1,0:T(8,128)(2,1)}, bf16[64,3584]{1,0:T(8,128)(2,1)S(1)}, u32[]{:S(2)}, u32[]{:S(2)}) collective-permute-start(bf16[64,3584]{1,0:T(8,128)(2,1)} %own.1), channel_id=1, source_target_pairs={{0,1},{1,0},{2,3},{3,2},{4,5},{5,4},{6,7},{7,6},{8,9},{9,8},{10,11... | collective-permute-start | bytes 1376264 | tf_op jit(solution)/shard_map/ppermute | solution.py:105
  18.6 24.3 %collective-permute-start.18 = (bf16[64,3584]{1,0:T(8,128)(2,1)}, bf16[64,3584]{1,0:T(8,128)(2,1)S(1)}, u32[]{:S(2)}, u32[]{:S(2)}) collective-permute-start(bf16[64,3584]{1,0:T(8,128)(2,1)} %collective-permute-done.5.own), channel_id=1, source_target_pairs={{0,8},{8,0},{1,9},{9,1},{2,10},{10,2},{3,11},{11,3},{4,12},{12,4},... | collective-permute-start | bytes 1376264 | tf_op jit(solution)/shard_map/ppermute | solution.py:102
  30.3 13.5 %collective-permute-start.20 = (bf16[64,3584]{1,0:T(8,128)(2,1)S(1)}, bf16[64,3584]{1,0:T(8,128)(2,1)S(1)}, u32[]{:S(2)}, u32[]{:S(2)}) collective-permute-start(bf16[64,3584]{1,0:T(8,128)(2,1)S(1)} %collective-permute-done.19.own_y), channel_id=1, source_target_pairs={{0,8},{8,0},{1,9},{9,1},{2,10},{10,2},{3,11},{11,3},{4,12},{12,4},... | collective-permute-start | bytes 1376264 | tf_op jit(solution)/shard_map/ppermute | solution.py:102
  31.6 10.5 %all-to-all-start = ((f32[16,1,64]{2,1,0:T(1,128)}), f32[16,1,64]{2,1,0:T(1,128)S(1)}, u32[]{:S(2)}, u32[]{:S(2)}) async-start(f32[16,1,64]{2,1,0:T(1,128)} %bitcast.2), calls=%async_computation | async-start | bytes 16384 | tf_op jit(solution)/shard_map/all_to_all | solution.py:112
  35.8 28.6 %collective-permute-start = (bf16[64,3584]{1,0:T(8,128)(2,1)}, bf16[64,3584]{1,0:T(8,128)(2,1)}, u32[]{:S(2)}, u32[]{:S(2)}) collective-permute-start(bf16[64,3584]{1,0:T(8,128)(2,1)} %own.1), channel_id=1, source_target_pairs={{0,8},{8,0},{1,9},{9,1},{2,10},{10,2},{3,11},{11,3},{4,12},{12,4},... | collective-permute-start | bytes 1376264 | tf_op jit(solution)/shard_map/ppermute | solution.py:102
  42.2 20.4 %copy-start.13 = (s32[8]{0:T(128)S(1)}, s32[8]{0:T(128)}, u32[]{:S(2)}) copy-start(s32[8]{0:T(128)} %param.17) | copy-start | bytes 100
  42.3 20.8 %collective-permute-start.6 = (bf16[64,3584]{1,0:T(8,128)(2,1)}, bf16[64,3584]{1,0:T(8,128)(2,1)}, u32[]{:S(2)}, u32[]{:S(2)}) collective-permute-start(bf16[64,3584]{1,0:T(8,128)(2,1)} %collective-permute-done.5.own), channel_id=1, source_target_pairs={{0,2},{1,3},{2,4},{3,5},{4,6},{5,7},{6,0},{7,1},{8,10},{9,11},{10,... | collective-permute-start | bytes 1376264 | tf_op jit(solution)/shard_map/ppermute | solution.py:108
  42.9 19.2 %copy-start.4 = (bf16[64,3584]{1,0:T(8,128)(2,1)}, bf16[64,3584]{1,0:T(8,128)(2,1)S(1)}, u32[]{:S(2)}) copy-start(bf16[64,3584]{1,0:T(8,128)(2,1)S(1)} %collective-permute-done.1.own_y) | copy-start | bytes 1376260
  43.0 21.4 %collective-permute-start.2 = (bf16[64,3584]{1,0:T(8,128)(2,1)S(1)}, bf16[64,3584]{1,0:T(8,128)(2,1)}, u32[]{:S(2)}, u32[]{:S(2)}) collective-permute-start(bf16[64,3584]{1,0:T(8,128)(2,1)S(1)} %collective-permute-done.1.own_y), channel_id=1, source_target_pairs={{0,8},{8,0},{1,9},{9,1},{2,10},{10,2},{3,11},{11,3},{4,12},{12,4},... | collective-permute-start | bytes 1376264 | tf_op jit(solution)/shard_map/ppermute | solution.py:102
  43.0 0.8 copy-start.6
  43.8 0.8 copy-start.8
  44.5 3.1 %copy-start.1 = (bf16[1,3584,1024]{2,1,0:T(8,128)(2,1)S(1)}, bf16[1,3584,1024]{2,1,0:T(8,128)(2,1)}, u32[]{:S(2)}) copy-start(bf16[1,3584,1024]{2,1,0:T(8,128)(2,1)} %gate.7) | copy-start | bytes 22020100
  47.6 1.0 copy-start.7
  48.6 1.0 copy-start.9
  49.7 14.7 %copy-start.3 = (bf16[64,3584]{1,0:T(8,128)(2,1)S(1)}, bf16[64,3584]{1,0:T(8,128)(2,1)}, u32[]{:S(2)}) copy-start(bf16[64,3584]{1,0:T(8,128)(2,1)} %own.1) | copy-start | bytes 1376260
  62.1 20.2 %collective-permute-start.21 = (bf16[128,3584]{1,0:T(8,128)(2,1)}, bf16[128,3584]{1,0:T(8,128)(2,1)}, u32[]{:S(2)}, u32[]{:S(2)}) collective-permute-start(bf16[128,3584]{1,0:T(8,128)(2,1)} %get-tuple-element.17), channel_id=1, source_target_pairs={{0,8},{8,0},{1,9},{9,1},{2,10},{10,2},{3,11},{11,3},{4,12},{12,4},... | collective-permute-start | bytes 2752520 | tf_op jit(solution)/shard_map/ppermute | solution.py:102
  63.2 17.7 %collective-permute-start.14 = (bf16[64,3584]{1,0:T(8,128)(2,1)}, bf16[64,3584]{1,0:T(8,128)(2,1)S(1)}, u32[]{:S(2)}, u32[]{:S(2)}) collective-permute-start(bf16[64,3584]{1,0:T(8,128)(2,1)} %collective-permute-done.6.own), channel_id=1, source_target_pairs={{0,1},{1,0},{2,3},{3,2},{4,5},{5,4},{6,7},{7,6},{8,9},{9,8},{10,11... | collective-permute-start | bytes 1376264 | tf_op jit(solution)/shard_map/ppermute | solution.py:105
  63.8 16.9 %collective-permute-start.7 = (bf16[64,3584]{1,0:T(8,128)(2,1)}, bf16[64,3584]{1,0:T(8,128)(2,1)S(1)}, u32[]{:S(2)}, u32[]{:S(2)}) collective-permute-start(bf16[64,3584]{1,0:T(8,128)(2,1)} %collective-permute-done.6.own), channel_id=1, source_target_pairs={{0,2},{1,3},{2,4},{3,5},{4,6},{5,7},{6,0},{7,1},{8,10},{9,11},{10,... | collective-permute-start | bytes 1376264 | tf_op jit(solution)/shard_map/ppermute | solution.py:108
  64.4 3.1 %copy-start.2 = (bf16[1,3584,1024]{2,1,0:T(8,128)(2,1)S(1)}, bf16[1,3584,1024]{2,1,0:T(8,128)(2,1)}, u32[]{:S(2)}) copy-start(bf16[1,3584,1024]{2,1,0:T(8,128)(2,1)} %gate.7) | copy-start | bytes 22020100
  67.5 1.0 copy-start.5
  80.2 42.8 %collective-permute-start.3 = (bf16[128,3584]{1,0:T(8,128)(2,1)S(1)}, bf16[128,3584]{1,0:T(8,128)(2,1)S(1)}, u32[]{:S(2)}, u32[]{:S(2)}) collective-permute-start(bf16[128,3584]{1,0:T(8,128)(2,1)S(1)} %get-tuple-element.11), channel_id=1, source_target_pairs={{0,8},{8,0},{1,9},{9,1},{2,10},{10,2},{3,11},{11,3},{4,12},{12,4},... | collective-permute-start | bytes 2752520 | tf_op jit(solution)/shard_map/ppermute | solution.py:102
  80.2 3.6 %collective-permute-start.13 = (bf16[64,3584]{1,0:T(8,128)(2,1)}, bf16[64,3584]{1,0:T(8,128)(2,1)S(1)}, u32[]{:S(2)}, u32[]{:S(2)}) collective-permute-start(bf16[64,3584]{1,0:T(8,128)(2,1)} %collective-permute-done.6.own), channel_id=1, source_target_pairs={{0,8},{8,0},{1,9},{9,1},{2,10},{10,2},{3,11},{11,3},{4,12},{12,4},... | collective-permute-start | bytes 1376264 | tf_op jit(solution)/shard_map/ppermute | solution.py:102
  80.7 26.4 %collective-permute-start.8 = (bf16[64,3584]{1,0:T(8,128)(2,1)S(1)}, bf16[64,3584]{1,0:T(8,128)(2,1)S(1)}, u32[]{:S(2)}, u32[]{:S(2)}) collective-permute-start(bf16[64,3584]{1,0:T(8,128)(2,1)S(1)} %collective-permute-done.7.own), channel_id=1, source_target_pairs={{0,8},{8,0},{1,9},{9,1},{2,10},{10,2},{3,11},{11,3},{4,12},{12,4},... | collective-permute-start | bytes 1376264 | tf_op jit(solution)/shard_map/ppermute | solution.py:102
  80.8 16.2 %collective-permute-start.9 = (bf16[64,3584]{1,0:T(8,128)(2,1)S(1)}, bf16[64,3584]{1,0:T(8,128)(2,1)S(1)}, u32[]{:S(2)}, u32[]{:S(2)}) collective-permute-start(bf16[64,3584]{1,0:T(8,128)(2,1)S(1)} %collective-permute-done.7.own), channel_id=1, source_target_pairs={{0,1},{1,0},{2,3},{3,2},{4,5},{5,4},{6,7},{7,6},{8,9},{9,8},{10,11... | collective-permute-start | bytes 1376264 | tf_op jit(solution)/shard_map/ppermute | solution.py:105
  82.3 3.0 %collective-permute-start.15 = (bf16[64,3584]{1,0:T(8,128)(2,1)S(1)}, bf16[64,3584]{1,0:T(8,128)(2,1)S(1)}, u32[]{:S(2)}, u32[]{:S(2)}) collective-permute-start(bf16[64,3584]{1,0:T(8,128)(2,1)S(1)} %collective-permute-done.14.own_y), channel_id=1, source_target_pairs={{0,8},{8,0},{1,9},{9,1},{2,10},{10,2},{3,11},{11,3},{4,12},{12,4},... | collective-permute-start | bytes 1376264 | tf_op jit(solution)/shard_map/ppermute | solution.py:102
  83.9 19.7 %collective-permute-start.22 = (bf16[64,3584]{1,0:T(8,128)(2,1)S(1)}, bf16[64,3584]{1,0:T(8,128)(2,1)S(1)}, u32[]{:S(2)}, u32[]{:S(2)}) collective-permute-start(bf16[64,3584]{1,0:T(8,128)(2,1)S(1)} %add_convert_fusion.4), channel_id=1, source_target_pairs={{0,1},{1,0},{2,3},{3,2},{4,5},{5,4},{6,7},{7,6},{8,9},{9,8},{10,11... | collective-permute-start | bytes 1376264 | tf_op jit(solution)/shard_map/ppermute | solution.py:105
  96.9 8.6 %collective-permute-start.16 = (bf16[128,3584]{1,0:T(8,128)(2,1)S(1)}, bf16[128,3584]{1,0:T(8,128)(2,1)S(1)}, u32[]{:S(2)}, u32[]{:S(2)}) collective-permute-start(bf16[128,3584]{1,0:T(8,128)(2,1)S(1)} %get-tuple-element.15), channel_id=1, source_target_pairs={{0,8},{8,0},{1,9},{9,1},{2,10},{10,2},{3,11},{11,3},{4,12},{12,4},... | collective-permute-start | bytes 2752520 | tf_op jit(solution)/shard_map/ppermute | solution.py:102
  97.0 10.2 %collective-permute-start.10 = (bf16[64,3584]{1,0:T(8,128)(2,1)S(1)}, bf16[64,3584]{1,0:T(8,128)(2,1)S(1)}, u32[]{:S(2)}, u32[]{:S(2)}) collective-permute-start(bf16[64,3584]{1,0:T(8,128)(2,1)S(1)} %collective-permute-done.9.own_y), channel_id=1, source_target_pairs={{0,8},{8,0},{1,9},{9,1},{2,10},{10,2},{3,11},{11,3},{4,12},{12,4},... | collective-permute-start | bytes 1376264 | tf_op jit(solution)/shard_map/ppermute | solution.py:102
  104.7 14.1 %collective-permute-start.23 = (bf16[64,3584]{1,0:T(8,128)(2,1)S(1)}, bf16[64,3584]{1,0:T(8,128)(2,1)S(1)}, u32[]{:S(2)}, u32[]{:S(2)}) collective-permute-start(bf16[64,3584]{1,0:T(8,128)(2,1)S(1)} %add_convert_fusion.3), channel_id=1, source_target_pairs={{0,2},{1,3},{2,4},{3,5},{4,6},{5,7},{6,0},{7,1},{8,10},{9,11},{10,... | collective-permute-start | bytes 1376264 | tf_op jit(solution)/shard_map/ppermute | solution.py:108
  105.6 13.2 %collective-permute-start.17 = (bf16[64,3584]{1,0:T(8,128)(2,1)S(1)}, bf16[64,3584]{1,0:T(8,128)(2,1)S(1)}, u32[]{:S(2)}, u32[]{:S(2)}) collective-permute-start(bf16[64,3584]{1,0:T(8,128)(2,1)S(1)} %add_convert_fusion.5), channel_id=1, source_target_pairs={{0,1},{1,0},{2,3},{3,2},{4,5},{5,4},{6,7},{7,6},{8,9},{9,8},{10,11... | collective-permute-start | bytes 1376264 | tf_op jit(solution)/shard_map/ppermute | solution.py:105
  118.6 3.6 %collective-permute-start.11 = (bf16[128,3584]{1,0:T(8,128)(2,1)S(1)}, bf16[128,3584]{1,0:T(8,128)(2,1)S(1)}, u32[]{:S(2)}, u32[]{:S(2)}) collective-permute-start(bf16[128,3584]{1,0:T(8,128)(2,1)S(1)} %get-tuple-element.13), channel_id=1, source_target_pairs={{0,8},{8,0},{1,9},{9,1},{2,10},{10,2},{3,11},{11,3},{4,12},{12,4},... | collective-permute-start | bytes 2752520 | tf_op jit(solution)/shard_map/ppermute | solution.py:102
  119.1 14.6 %collective-permute-start.24 = (bf16[64,3584]{1,0:T(8,128)(2,1)S(1)}, bf16[64,3584]{1,0:T(8,128)(2,1)S(1)}, u32[]{:S(2)}, u32[]{:S(2)}) collective-permute-start(bf16[64,3584]{1,0:T(8,128)(2,1)S(1)} %add_convert_fusion.2), channel_id=1, source_target_pairs={{0,2},{1,3},{2,4},{3,5},{4,6},{5,7},{6,0},{7,1},{8,10},{9,11},{10,... | collective-permute-start | bytes 1376264 | tf_op jit(solution)/shard_map/ppermute | solution.py:108
  122.3 16.7 %copy-start.10 = (bf16[8,256,576]{1,2,0:T(8,128)(2,1)S(1)}, bf16[8,256,576]{1,2,0:T(8,128)(2,1)}, u32[]{:S(2)}) copy-start(bf16[8,256,576]{1,2,0:T(8,128)(2,1)} %param.16) | copy-start | bytes 7077892
  122.4 13.4 %collective-permute-start.12 = (bf16[64,3584]{1,0:T(8,128)(2,1)S(1)}, bf16[64,3584]{1,0:T(8,128)(2,1)S(1)}, u32[]{:S(2)}, u32[]{:S(2)}) collective-permute-start(bf16[64,3584]{1,0:T(8,128)(2,1)S(1)} %add_convert_fusion.6), channel_id=1, source_target_pairs={{0,1},{1,0},{2,3},{3,2},{4,5},{5,4},{6,7},{7,6},{8,9},{9,8},{10,11... | collective-permute-start | bytes 1376264 | tf_op jit(solution)/shard_map/ppermute | solution.py:105
  123.0 16.5 %copy-start.11 = (bf16[128,3584]{1,0:T(8,128)(2,1)}, bf16[128,3584]{1,0:T(8,128)(2,1)S(1)}, u32[]{:S(2)}) copy-start(bf16[128,3584]{1,0:T(8,128)(2,1)S(1)} %collective-permute-done.3) | copy-start | bytes 2752516
  124.0 21.0 %collective-permute-start.4 = (bf16[64,3584]{1,0:T(8,128)(2,1)}, bf16[64,3584]{1,0:T(8,128)(2,1)}, u32[]{:S(2)}, u32[]{:S(2)}) collective-permute-start(bf16[64,3584]{1,0:T(8,128)(2,1)} %add_convert_fusion.7), channel_id=1, source_target_pairs={{0,1},{1,0},{2,3},{3,2},{4,5},{5,4},{6,7},{7,6},{8,9},{9,8},{10,11... | collective-permute-start | bytes 1376264 | tf_op jit(solution)/shard_map/ppermute | solution.py:105
  136.8 13.2 %collective-permute-start.25 = (bf16[64,3584]{1,0:T(8,128)(2,1)}, bf16[64,3584]{1,0:T(8,128)(2,1)}, u32[]{:S(2)}, u32[]{:S(2)}) collective-permute-start(bf16[64,3584]{1,0:T(8,128)(2,1)} %add_convert_fusion.1), channel_id=1, source_target_pairs={{0,2},{1,3},{2,4},{3,5},{4,6},{5,7},{6,0},{7,1},{8,10},{9,11},{10,... | collective-permute-start | bytes 1376264 | tf_op jit(solution)/shard_map/ppermute | solution.py:108
  139.7 10.2 %copy-start.12 = (bf16[128,3584]{1,0:T(8,128)(2,1)S(1)}, bf16[128,3584]{1,0:T(8,128)(2,1)}, u32[]{:S(2)}) copy-start(bf16[128,3584]{1,0:T(8,128)(2,1)} %copy-done.11) | copy-start | bytes 2752516

commit v2 on v0

v2 whole, which is shorter than its diff:
```python
import jax
import jax.numpy as jnp
from jax import lax
from jax.experimental import pallas as pl
from jax.experimental.pallas import tpu as pltpu
from jax.sharding import PartitionSpec as P

LATENT = 512
PAIR = 2


VMEM_LIMIT = 16 * 1024 * 1024
score_scale = 192.0 ** (-0.5)


def attend(queries, kv_cache, lengths):
    scores = (
        jnp.einsum("bhc,blc->bhl", queries, kv_cache, preferred_element_type=jnp.float32)
        * score_scale
    )
    visible = lax.broadcasted_iota(jnp.int32, (1, 1, kv_cache.shape[1]), 2) < lengths[:, None, None]
    scores = jnp.where(visible, scores, -jnp.inf)
    row_max = jnp.max(scores, axis=2, keepdims=True)
    exponent = jnp.exp(scores - row_max)
    softmax_weights = (exponent / jnp.sum(exponent, axis=2, keepdims=True)).astype(jnp.bfloat16)
    latent_values = kv_cache[:, :, :LATENT]
    return jnp.einsum(
        "bhl,blc->bhc", softmax_weights, latent_values, preferred_element_type=jnp.float32
    ).astype(jnp.bfloat16)


def extend_kernel(experts, hidden, routes, route_weights, out):
    tokens, model_width = hidden.shape
    out[:, :model_width] = hidden[...]
    shape = (tokens, out.shape[1] - model_width)
    lane = lax.broadcasted_iota(jnp.int32, shape, 1)
    group = (lane >= experts).astype(jnp.int32) + (lane >= 2 * experts).astype(jnp.int32)
    expert = lane - group * experts
    weight = jnp.zeros(shape, jnp.float32)
    for k in range(routes.shape[1]):
        weight += jnp.where(routes[:, k : k + 1] == expert, route_weights[:, k : k + 1], 0.0)
    high = weight.astype(jnp.bfloat16).astype(jnp.float32)
    middle = (weight - high).astype(jnp.bfloat16).astype(jnp.float32)
    low = weight - high - middle
    part = jnp.where(group == 0, high, jnp.where(group == 1, middle, low))
    out[:, model_width:] = part.astype(jnp.bfloat16)


def extend(hidden_rows, routes, route_weights, experts):
    tokens, model_width = hidden_rows.shape
    extra = -(-3 * experts // 128) * 128
    inside = pl.BlockSpec(memory_space=pltpu.VMEM)
    return pl.pallas_call(
        lambda *refs: extend_kernel(experts, *refs),
        out_shape=jax.ShapeDtypeStruct((tokens, model_width + extra), jnp.bfloat16),
        in_specs=[inside] * 3,
        out_specs=inside,
        compiler_params=pltpu.CompilerParams(vmem_limit_bytes=VMEM_LIMIT),
        cost_estimate=pl.CostEstimate(flops=0, bytes_accessed=hidden_rows.size * 4, transcendentals=0),
    )(hidden_rows, routes, route_weights)


def expert_kernel(experts, own, other, own_y, other_y, gate, up, down, keep, send, rows):
    tokens = own.shape[0]
    model_width = gate.shape[0]
    for place, block in enumerate((own, own_y, other, other_y)):
        rows[place * tokens : (place + 1) * tokens, :] = block[...]
    extra = rows[:, model_width:].astype(jnp.float32)
    lane = lax.broadcasted_iota(jnp.int32, extra.shape, 1)
    mine = lax.axis_index("node") * lax.axis_size("rank") + lax.axis_index("rank")
    at = (lane == mine) | (lane == mine + experts) | (lane == mine + 2 * experts)
    weight = jnp.sum(jnp.where(at, extra, 0.0), axis=1, keepdims=True)
    values = rows[:, :model_width]
    gate_term = jnp.dot(values, gate[...], preferred_element_type=jnp.float32)
    up_term = jnp.dot(values, up[...], preferred_element_type=jnp.float32)
    hidden = (gate_term / (1.0 + jnp.exp(-gate_term)) * up_term).astype(jnp.bfloat16)
    produced = jnp.dot(hidden, down[...], preferred_element_type=jnp.float32)
    produced = (produced.astype(jnp.bfloat16).astype(jnp.float32) * weight).astype(jnp.bfloat16)
    keep[...] = produced[: 2 * tokens]
    send[...] = produced[2 * tokens :]


def load_kernel(*refs):
    count = len(refs) // 3
    copies = [
        pltpu.make_async_copy(refs[i], refs[count + i], refs[2 * count + i]) for i in range(count)
    ]
    for copy in copies:
        copy.start()
    for copy in copies:
        copy.wait()


def load_inside(*arrays):
    return pl.pallas_call(
        load_kernel,
        out_shape=[jax.ShapeDtypeStruct(a.shape, a.dtype) for a in arrays],
        in_specs=[pl.BlockSpec(memory_space=pl.ANY)] * len(arrays),
        out_specs=[pl.BlockSpec(memory_space=pltpu.VMEM)] * len(arrays),
        scratch_shapes=[pltpu.SemaphoreType.DMA] * len(arrays),
        compiler_params=pltpu.CompilerParams(vmem_limit_bytes=VMEM_LIMIT),
        cost_estimate=pl.CostEstimate(
            flops=0, bytes_accessed=sum(a.size * 2 for a in arrays), transcendentals=0
        ),
    )(*arrays)


def run_expert(experts, blocks, w_gate, w_up, w_down):
    tokens, extended = blocks[0].shape
    model_width, hidden_width = w_gate.shape
    inside = pl.BlockSpec(memory_space=pltpu.VMEM)
    return pl.pallas_call(
        lambda *refs: expert_kernel(experts, *refs),
        out_shape=[jax.ShapeDtypeStruct((2 * tokens, model_width), jnp.bfloat16)] * 2,
        in_specs=[inside] * 7,
        out_specs=[inside] * 2,
        scratch_shapes=[pltpu.VMEM((4 * tokens, extended), jnp.bfloat16)],
        compiler_params=pltpu.CompilerParams(vmem_limit_bytes=VMEM_LIMIT),
        cost_estimate=pl.CostEstimate(
            flops=2 * 3 * 4 * tokens * model_width * hidden_width,
            bytes_accessed=16 * tokens * model_width,
            transcendentals=4 * tokens * hidden_width,
        ),
    )(*blocks, w_gate, w_up, w_down)


def local(hidden_rows, routes, route_weights, w_gate, w_up, w_down, queries, kv_cache, lengths):
    tokens = hidden_rows.shape[0]
    node_count = lax.axis_size("node")
    rank_count = lax.axis_size("rank")
    experts = node_count * rank_count * w_gate.shape[0]
    steps = rank_count // PAIR
    f32, bf16 = jnp.float32, jnp.bfloat16

    def core(value):
        return lax.ppermute(value, "node", [(i, 1 - i) for i in range(node_count)])

    def pair(value):
        return lax.ppermute(value, "rank", [(i, i ^ 1) for i in range(rank_count)])

    def ring(value):
        return lax.ppermute(value, "rank", [(i, (i + PAIR) % rank_count) for i in range(rank_count)])

    weights = load_inside(w_gate[0], w_up[0], w_down[0])

    attended = attend(queries, kv_cache, lengths)

    own = [extend(hidden_rows, routes, route_weights, experts)]
    other, own_y, other_y, partial = [], [], [], []
    for slot in range(steps):
        arrived = {"own_y": pair(own[slot]), "other": core(own[slot])}
        if slot < steps - 1:
            arrived["own"] = ring(own[slot])
        if slot == 0:
            arrived["weights"] = weights
        else:
            other_y.append(core(own_y[slot - 1]))
            blocks = own[slot - 1], other[slot - 1], own_y[slot - 1], other_y[slot - 1]
            arrived["partial"] = run_expert(experts, blocks, *weights)
        arrived = lax.optimization_barrier(arrived)
        own_y.append(arrived["own_y"])
        other.append(arrived["other"])
        if slot < steps - 1:
            own.append(arrived["own"])
        if slot == 0:
            weights = arrived["weights"]
        else:
            partial.append(arrived["partial"])
    other_y.append(core(own_y[-1]))
    blocks = own[-1], other[-1], own_y[-1], other_y[-1]
    partial.append(run_expert(experts, blocks, *weights))

    got = [core(send) for keep, send in partial]

    def away(slot):
        return pair((partial[slot][0][tokens:].astype(f32) + got[slot][tokens:].astype(f32)).astype(bf16))

    def kept(slot):
        return partial[slot][0][:tokens].astype(f32) + got[slot][:tokens].astype(f32)

    back = {}
    carried = None
    for slot in list(range(1, steps)) + [0]:
        back[slot] = away(slot)
        value = kept(slot) + back[slot].astype(f32)
        if carried is not None:
            value = value + carried.astype(f32)
        value = value.astype(bf16)
        carried = ring(value) if slot else value
    return (carried, attended)


def solution(mesh):
    return jax.shard_map(
        local,
        mesh=mesh,
        in_specs=(
            P(("replica", "node", "rank"), None),
            P(("replica", "node", "rank"), None),
            P(("replica", "node", "rank"), None),
            P(("node", "rank"), None, None),
            P(("node", "rank"), None, None),
            P(("node", "rank"), None, None),
            P(("replica", "node", "rank"), None, None),
            P(("replica", "node", "rank"), None, None),
            P(("replica", "node", "rank")),
        ),
        out_specs=(
            P(("replica", "node", "rank"), None),
            P(("replica", "node", "rank"), None, None),
        ),
        check_vma=False,
    )
```

time: 300 us -> 122 us (0.41); the launches traced: 295 us -> 121 us
  blocking collectives: 130 us -> 0 us
  waiting for transfers between devices: 110 us -> 44.4 us
  matrix products: 39.1 us -> 3.95 us
  Pallas kernels: 0 us -> 27.8 us
  local copies, waits for them, and re-layouts: 4.67 us -> 20.9 us
  starting transfers between devices: 4.94 us -> 18.7 us
    all_to_all x1 -> x0, blocking collectives: 130 us -> none  [local(): lax.all_to_all(outgoing.reshape(experts, capacity, model_width), ('node',...]
    all_to_all x1 -> x0, waiting for transfers between devices: 110 us -> none  [local(): lax.all_to_all(produced, ('node', 'rank'), split_axis=0, concat_axis=0, t...]
    ppermute x0 -> x26, waiting for transfers between devices: none -> 44.4 us  [the longest x6 28.2 us: ring(): lax.ppermute(value, 'rank', [(i, (i + PAIR) % rank_count) for i in range(...]
    dot_general x4 -> x0, matrix products: 36.8 us -> none  [the longest x1 20 us: run_expert(): jnp.dot(hidden, w_down[0], preferred_element_type=jnp.float32)]
    pallas_call x0 -> x6, Pallas kernels: none -> 27.8 us  [the longest x4 23.5 us: run_expert(): pl.pallas_call(lambda *refs: expert_kernel(experts, *refs), out_shape=[ja...]
    ppermute x0 -> x26, starting transfers between devices: none -> 18.7 us  [the longest x8 9.11 us: pair(): return lax.ppermute(value, 'rank', [(i, i ^ 1) for i in range(rank_count)])]
    unnamed x18 -> x22, local copies, waits for them, and re-layouts: 4.03 us -> 20.9 us
    all_to_all x1 -> x0, starting transfers between devices: 4.94 us -> none  [local(): lax.all_to_all(produced, ('node', 'rank'), split_axis=0, concat_axis=0, t...]
  transfers between devices with their start and end apart: 1 -> 26, of which waited for: 1 -> 11; matrix products, arithmetic and copies ran while one was open for 2% -> 6% of each run, Pallas kernels for 0% -> 23%
where the time goes in v2:
time: 122 us; the launch traced here: 121 us
  waiting for transfers between devices  44.4 us (36%)
  Pallas kernels  27.8 us (23%)
  local copies, waits for them, and re-layouts  20.9 us (17%)
  starting transfers between devices  18.7 us (15%)
  other arithmetic  4.92 us (4%)
  matrix products  3.95 us (3%)
    ppermute x6, waiting for transfers between devices, ring(): lax.ppermute(value, 'rank', [(i, (i + PAIR) % rank_count) for i in range(...  28.2 us
    pallas_call x4, Pallas kernels, run_expert(): pl.pallas_call(lambda *refs: expert_kernel(experts, *refs), out_shape=[ja...  23.5 us
    unnamed x22, local copies, waits for them, and re-layouts  20.9 us
    ppermute x8, waiting for transfers between devices, pair(): return lax.ppermute(value, 'rank', [(i, i ^ 1) for i in range(rank_count)])  14.3 us
    ppermute x8, starting transfers between devices, pair(): return lax.ppermute(value, 'rank', [(i, i ^ 1) for i in range(rank_count)])  9.11 us
    ppermute x6, starting transfers between devices, ring(): lax.ppermute(value, 'rank', [(i, (i + PAIR) % rank_count) for i in range(...  6.64 us
    pallas_call x1, Pallas kernels, load_inside(): pl.pallas_call(load_kernel, out_shape=[jax.ShapeDtypeStruct(a.shape, a.dt...  4.08 us
    convert_element_type x4, other arithmetic, local(): value = value.astype(bf16)  3.4 us
  transfers between devices with their start and end apart: 26, of which 11 were waited for; matrix products, arithmetic and copies ran while one was open for 6% of the time, Pallas kernels for 23%

profile of v2, /device:TPU:0, one launch (start us, length us, event | category | flops | bytes accessed | tf_op | source)
XLA Modules:
  0.0 121.5 jit_solution(12555624657437139231)
XLA Ops:
  0.6 0.0 copy-start
  0.6 0.8 copy.11.refs_1_
  1.5 0.8 copy.12.refs_2_
  2.3 1.0 copy-done.7
  3.3 0.2 shard_map.104.refs_0_
  3.5 0.5 collective-permute-start
  4.0 2.6 %collective-permute-start.1 = (bf16[64,3712]{1,0:T(8,128)(2,1)S(1)}, bf16[64,3712]{1,0:T(8,128)(2,1)S(1)}, u32[]{:S(2)}, u32[]{:S(2)}) collective-permute-start(bf16[64,3712]{1,0:T(8,128)(2,1)S(1)} %shard_map.104.refs_0_), channel_id=1, source_target_pairs={{0,2},{1,3},{2,4},{3,5},{4,6},{5,7},{6,0},{7,1},{8,10},{9,11},{10,... | collective-permute-start | bytes 1425416 | tf_op jit(solution)/shard_map/ppermute | solution.py:142
  6.7 1.5 %collective-permute-start.2 = (bf16[64,3712]{1,0:T(8,128)(2,1)S(1)}, bf16[64,3712]{1,0:T(8,128)(2,1)S(1)}, u32[]{:S(2)}, u32[]{:S(2)}) collective-permute-start(bf16[64,3712]{1,0:T(8,128)(2,1)S(1)} %shard_map.104.refs_0_), channel_id=1, source_target_pairs={{0,1},{1,0},{2,3},{3,2},{4,5},{5,4},{6,7},{7,6},{8,9},{9,8},{10,11... | collective-permute-start | bytes 1425416 | tf_op jit(solution)/shard_map/ppermute | solution.py:139
  8.2 3.1 %copy-done.5 = bf16[1,3584,1024]{2,1,0:T(8,128)(2,1)S(1)} copy-done((bf16[1,3584,1024]{2,1,0:T(8,128)(2,1)S(1)}, bf16[1,3584,1024]{2,1,0:T(8,128)(2,1)}, u32[]{:S(2)}) %copy-start.5) | copy-done | bytes 7340056
  11.3 3.1 %copy-done.6 = bf16[1,3584,1024]{2,1,0:T(8,128)(2,1)S(1)} copy-done((bf16[1,3584,1024]{2,1,0:T(8,128)(2,1)S(1)}, bf16[1,3584,1024]{2,1,0:T(8,128)(2,1)}, u32[]{:S(2)}) %copy-start.6) | copy-done | bytes 7340056
  14.3 4.1 %shard_map.105 = (bf16[3584,1024]{1,0:T(8,128)(2,1)S(1)}, bf16[3584,1024]{1,0:T(8,128)(2,1)S(1)}, bf16[1024,3584]{1,0:T(8,128)(2,1)S(1)}) custom-call(bf16[3584,1024]{1,0:T(8,128)(2,1)S(1)} %bitcast.7, bf16[3584,1024]{1,0:T(8,128)(2,1)S(1)} %bitcast.8, bf16[1024,3584]{1,0:T(8,128)(2,1)} %bitcast.9), custom_call_target="tpu_custom_call" | custom-call | bytes 22020096 | tf_op jit(solution)/shard_map/pallas_call | solution.py:95
  18.4 2.9 %copy-done.1 = bf16[3584,1024]{1,0:T(8,128)(2,1)} copy-done((bf16[3584,1024]{1,0:T(8,128)(2,1)}, bf16[3584,1024]{1,0:T(8,128)(2,1)S(1)}, u32[]{:S(2)}) %copy-start.1) | copy-done | bytes 7340056
  21.4 3.0 %copy-done.3 = bf16[1024,3584]{1,0:T(8,128)(2,1)} copy-done((bf16[1024,3584]{1,0:T(8,128)(2,1)}, bf16[1024,3584]{1,0:T(8,128)(2,1)S(1)}, u32[]{:S(2)}) %copy-start.3) | copy-done | bytes 7340056
  24.3 0.0 collective-permute-done.refs_1_
  24.4 0.1 collective-permute-start.6
  24.4 0.5 collective-permute-start.3
  24.9 1.6 %collective-permute-start.4 = (bf16[64,3712]{1,0:T(8,128)(2,1)S(1)}, bf16[64,3712]{1,0:T(8,128)(2,1)S(1)}, u32[]{:S(2)}, u32[]{:S(2)}) collective-permute-start(bf16[64,3712]{1,0:T(8,128)(2,1)S(1)} %collective-permute-done.1.refs_0_), channel_id=1, source_target_pairs={{0,2},{1,3},{2,4},{3,5},{4,6},{5,7},{6,0},{7,1},{8,10},{9,11},{10,... | collective-permute-start | bytes 1425416 | tf_op jit(solution)/shard_map/ppermute | solution.py:142
  26.5 0.5 collective-permute-start.5
  27.0 3.1 %copy-done.2 = bf16[3584,1024]{1,0:T(8,128)(2,1)S(1)} copy-done((bf16[3584,1024]{1,0:T(8,128)(2,1)S(1)}, bf16[3584,1024]{1,0:T(8,128)(2,1)}, u32[]{:S(2)}) %copy-start.2) | copy-done | bytes 7340056
  30.1 3.1 %copy-done.4 = bf16[1024,3584]{1,0:T(8,128)(2,1)S(1)} copy-done((bf16[1024,3584]{1,0:T(8,128)(2,1)S(1)}, bf16[1024,3584]{1,0:T(8,128)(2,1)}, u32[]{:S(2)}) %copy-start.4) | copy-done | bytes 7340056
  33.2 5.9 %shard_map.106 = (bf16[128,3584]{1,0:T(8,128)(2,1)S(1)}, bf16[128,3584]{1,0:T(8,128)(2,1)S(1)}) custom-call(bf16[64,3712]{1,0:T(8,128)(2,1)S(1)} %shard_map.104.refs_0_, bf16[64,3712]{1,0:T(8,128)(2,1)S(1)} %collective-permute-done.refs_1_, bf16[64,3712]{1,0:T(8,128)(2,1)S(1)} %collective-permute-done.2.refs_2_, ...), custom_call_target="tpu_custom_call" | custom-call | flops 5637144576 | bytes 3670016 | tf_op jit(solution)/shard_map/pallas_call | solution.py:112
  39.1 0.5 collective-permute-done.4.refs_0_
  39.6 0.5 collective-permute-start.9
  40.1 1.2 collective-permute-start.10
  41.3 1.5 %collective-permute-start.11 = (bf16[64,3712]{1,0:T(8,128)(2,1)S(1)}, bf16[64,3712]{1,0:T(8,128)(2,1)S(1)}, u32[]{:S(2)}, u32[]{:S(2)}) collective-permute-start(bf16[64,3712]{1,0:T(8,128)(2,1)S(1)} %collective-permute-done.4.refs_0_), channel_id=1, source_target_pairs={{0,1},{1,0},{2,3},{3,2},{4,5},{5,4},{6,7},{7,6},{8,9},{9,8},{10,11... | collective-permute-start | bytes 1425416 | tf_op jit(solution)/shard_map/ppermute | solution.py:139
  42.8 5.9 %shard_map.107 = (bf16[128,3584]{1,0:T(8,128)(2,1)S(1)}, bf16[128,3584]{1,0:T(8,128)(2,1)S(1)}) custom-call(bf16[64,3712]{1,0:T(8,128)(2,1)S(1)} %collective-permute-done.1.refs_0_, bf16[64,3712]{1,0:T(8,128)(2,1)S(1)} %collective-permute-done.3.refs_1_, bf16[64,3712]{1,0:T(8,128)(2,1)S(1)} %collective-permute-done.5.refs_2_, ...), custom_call_target="tpu_custom_call" | custom-call | flops 5637144576 | bytes 3670016 | tf_op jit(solution)/shard_map/pallas_call | solution.py:112
  48.7 6.1 %collective-permute-done.10.refs_0_ = bf16[64,3712]{1,0:T(8,128)(2,1)S(1)} collective-permute-done((bf16[64,3712]{1,0:T(8,128)(2,1)S(1)}, bf16[64,3712]{1,0:T(8,128)(2,1)S(1)}, u32[]{:S(2)}, u32[]{:S(2)}) %collective-permute-start.10) | collective-permute-done | bytes 475168 | tf_op jit(solution)/shard_map/ppermute | solution.py:142
  54.8 0.1 iota_compare_fusion
  54.8 0.5 collective-permute-start.7
  55.3 0.1 collective-permute-start.13
  55.4 1.1 collective-permute-start.14
  56.5 0.2 collective-permute-start.15
  56.7 0.5 collective-permute-done.21
  57.2 0.1 add_convert_fusion.4
  57.3 1.2 collective-permute-start.22
  58.5 1.4 %collective-permute-done.15.refs_3_ = bf16[64,3712]{1,0:T(8,128)(2,1)S(1)} collective-permute-done((bf16[64,3712]{1,0:T(8,128)(2,1)S(1)}, bf16[64,3712]{1,0:T(8,128)(2,1)S(1)}, u32[]{:S(2)}, u32[]{:S(2)}) %collective-permute-start.15) | collective-permute-done | bytes 475168 | tf_op jit(solution)/shard_map/ppermute | solution.py:136
  59.9 5.9 %shard_map.108 = (bf16[128,3584]{1,0:T(8,128)(2,1)S(1)}, bf16[128,3584]{1,0:T(8,128)(2,1)S(1)}) custom-call(bf16[64,3712]{1,0:T(8,128)(2,1)S(1)} %collective-permute-done.4.refs_0_, bf16[64,3712]{1,0:T(8,128)(2,1)S(1)} %collective-permute-done.9.refs_1_, bf16[64,3712]{1,0:T(8,128)(2,1)S(1)} %collective-permute-done.11.refs_2_, ...), custom_call_target="tpu_custom_call" | custom-call | flops 5637144576 | bytes 3670016 | tf_op jit(solution)/shard_map/pallas_call | solution.py:112
  65.8 3.3 %collective-permute-done.14.refs_2_ = bf16[64,3712]{1,0:T(8,128)(2,1)S(1)} collective-permute-done((bf16[64,3712]{1,0:T(8,128)(2,1)S(1)}, bf16[64,3712]{1,0:T(8,128)(2,1)S(1)}, u32[]{:S(2)}, u32[]{:S(2)}) %collective-permute-start.14) | collective-permute-done | bytes 475168 | tf_op jit(solution)/shard_map/ppermute | solution.py:139
  69.1 0.5 collective-permute-start.16
  69.6 8.9 %collective-permute-done.22 = bf16[64,3584]{1,0:T(8,128)(2,1)S(1)} collective-permute-done((bf16[64,3584]{1,0:T(8,128)(2,1)S(1)}, bf16[64,3584]{1,0:T(8,128)(2,1)S(1)}, u32[]{:S(2)}, u32[]{:S(2)}) %collective-permute-start.22) | collective-permute-done | bytes 458784 | tf_op jit(solution)/shard_map/ppermute | solution.py:139
  78.5 0.2 add_convert_fusion.3
  78.6 0.3 collective-permute-start.23
  78.9 0.1 add_convert_fusion.5
  79.0 1.2 collective-permute-start.20
  80.2 5.9 %shard_map.109 = (bf16[128,3584]{1,0:T(8,128)(2,1)S(1)}, bf16[128,3584]{1,0:T(8,128)(2,1)S(1)}) custom-call(bf16[64,3712]{1,0:T(8,128)(2,1)S(1)} %collective-permute-done.10.refs_0_, bf16[64,3712]{1,0:T(8,128)(2,1)S(1)} %collective-permute-done.13.refs_1_, bf16[64,3712]{1,0:T(8,128)(2,1)S(1)} %collective-permute-done.14.refs_2_, ...), custom_call_target="tpu_custom_call" | custom-call | flops 5637144576 | bytes 3670016 | tf_op jit(solution)/shard_map/pallas_call | solution.py:112
  86.1 0.1 collective-permute-start.17
  86.2 6.6 %collective-permute-done.23 = bf16[64,3584]{1,0:T(8,128)(2,1)S(1)} collective-permute-done((bf16[64,3584]{1,0:T(8,128)(2,1)S(1)}, bf16[64,3584]{1,0:T(8,128)(2,1)S(1)}, u32[]{:S(2)}, u32[]{:S(2)}) %collective-permute-start.23) | collective-permute-done | bytes 458784 | tf_op jit(solution)/shard_map/ppermute | solution.py:142
  92.8 0.2 add_convert_fusion.2
  93.0 0.1 collective-permute-start.24
  93.1 0.0 copy-start.8
  93.1 0.1 add_convert_fusion.6
  93.2 1.2 collective-permute-start.18
  94.4 0.9 add_convert_fusion.7
  95.3 0.9 collective-permute-start.8
  96.2 9.9 %collective-permute-done.24 = bf16[64,3584]{1,0:T(8,128)(2,1)S(1)} collective-permute-done((bf16[64,3584]{1,0:T(8,128)(2,1)S(1)}, bf16[64,3584]{1,0:T(8,128)(2,1)S(1)}, u32[]{:S(2)}, u32[]{:S(2)}) %collective-permute-start.24) | collective-permute-done | bytes 458784 | tf_op jit(solution)/shard_map/ppermute | solution.py:142
  106.1 0.7 collective-permute-done.18
  106.8 1.0 add_convert_fusion.1
  107.7 0.9 collective-permute-start.25
  108.7 0.6 fusion.8
  109.2 0.2 fusion.11
  109.5 3.4 %fusion.3 = bf16[8,64,512]{2,1,0:T(8,128)(2,1)} fusion(bf16[8,256,576]{1,2,0:T(8,128)(2,1)} %param.16, f32[8,64]{1,0:T(8,128)S(1)} %fusion.11, f32[8,64,256]{2,1,0:T(8,128)S(1)} %fusion.8), kind=kOutput, calls=%fused_computation.3 | convolution fusion | flops 134873856 | bytes 3674112 | tf_op jit(solution)/shard_map/bhl,blc->bhc/dot_general | solution.py:27
  112.9 1.4 %collective-permute-done.8 = bf16[64,3584]{1,0:T(8,128)(2,1)S(1)} collective-permute-done((bf16[64,3584]{1,0:T(8,128)(2,1)}, bf16[64,3584]{1,0:T(8,128)(2,1)S(1)}, u32[]{:S(2)}, u32[]{:S(2)}) %collective-permute-start.8) | collective-permute-done | bytes 458784 | tf_op jit(solution)/shard_map/ppermute | solution.py:139
  114.3 5.1 %collective-permute-done.25 = bf16[64,3584]{1,0:T(8,128)(2,1)} collective-permute-done((bf16[64,3584]{1,0:T(8,128)(2,1)}, bf16[64,3584]{1,0:T(8,128)(2,1)}, u32[]{:S(2)}, u32[]{:S(2)}) %collective-permute-start.25) | collective-permute-done | bytes 458784 | tf_op jit(solution)/shard_map/ppermute | solution.py:142
  119.4 2.0 %add_convert_fusion = bf16[64,3584]{1,0:T(8,128)(2,1)} fusion(bf16[64,3584]{1,0:T(8,128)(2,1)} %collective-permute-done.25, bf16[64,3584]{1,0:T(8,128)(2,1)S(1)} %collective-permute-done.8, bf16[128,3584]{1,0:T(8,128)(2,1)S(1)} %collective-permute-done.7, bf16[128,3584]{1,0:T(8,128)(2,1)S(1)} %get-tuple-element.44), kind=kLoop, calls=%fused_computation.8 | loop fusion | flops 1835008 | bytes 2293760 | tf_op jit(solution)/shard_map/convert_element_type | solution.py:188
  (28 shorter events, 0.1 us)
Async XLA Ops:
  0.6 108.0 %copy-start = (bf16[8,64,576]{2,1,0:T(8,128)(2,1)S(1)}, bf16[8,64,576]{2,1,0:T(8,128)(2,1)}, u32[]{:S(2)}) copy-start(bf16[8,64,576]{2,1,0:T(8,128)(2,1)} %param.15) | copy-start | bytes 1769476
  2.3 1.0 copy-start.7
  3.5 20.8 %collective-permute-start = (bf16[64,3712]{1,0:T(8,128)(2,1)S(1)}, bf16[64,3712]{1,0:T(8,128)(2,1)S(1)}, u32[]{:S(2)}, u32[]{:S(2)}) collective-permute-start(bf16[64,3712]{1,0:T(8,128)(2,1)S(1)} %shard_map.104.refs_0_), channel_id=1, source_target_pairs={{0,8},{8,0},{1,9},{9,1},{2,10},{10,2},{3,11},{11,3},{4,12},{12,4},... | collective-permute-start | bytes 1425416 | tf_op jit(solution)/shard_map/ppermute | solution.py:136
  4.0 20.3 %collective-permute-start.1 = (bf16[64,3712]{1,0:T(8,128)(2,1)S(1)}, bf16[64,3712]{1,0:T(8,128)(2,1)S(1)}, u32[]{:S(2)}, u32[]{:S(2)}) collective-permute-start(bf16[64,3712]{1,0:T(8,128)(2,1)S(1)} %shard_map.104.refs_0_), channel_id=1, source_target_pairs={{0,2},{1,3},{2,4},{3,5},{4,6},{5,7},{6,0},{7,1},{8,10},{9,11},{10,... | collective-permute-start | bytes 1425416 | tf_op jit(solution)/shard_map/ppermute | solution.py:142
  6.7 17.7 %collective-permute-start.2 = (bf16[64,3712]{1,0:T(8,128)(2,1)S(1)}, bf16[64,3712]{1,0:T(8,128)(2,1)S(1)}, u32[]{:S(2)}, u32[]{:S(2)}) collective-permute-start(bf16[64,3712]{1,0:T(8,128)(2,1)S(1)} %shard_map.104.refs_0_), channel_id=1, source_target_pairs={{0,1},{1,0},{2,3},{3,2},{4,5},{5,4},{6,7},{7,6},{8,9},{9,8},{10,11... | collective-permute-start | bytes 1425416 | tf_op jit(solution)/shard_map/ppermute | solution.py:139
  8.2 3.1 %copy-start.5 = (bf16[1,3584,1024]{2,1,0:T(8,128)(2,1)S(1)}, bf16[1,3584,1024]{2,1,0:T(8,128)(2,1)}, u32[]{:S(2)}) copy-start(bf16[1,3584,1024]{2,1,0:T(8,128)(2,1)} %param.12) | copy-start | bytes 22020100
  11.3 3.1 %copy-start.6 = (bf16[1,3584,1024]{2,1,0:T(8,128)(2,1)S(1)}, bf16[1,3584,1024]{2,1,0:T(8,128)(2,1)}, u32[]{:S(2)}) copy-start(bf16[1,3584,1024]{2,1,0:T(8,128)(2,1)} %param.13) | copy-start | bytes 22020100
  18.4 2.9 %copy-start.1 = (bf16[3584,1024]{1,0:T(8,128)(2,1)}, bf16[3584,1024]{1,0:T(8,128)(2,1)S(1)}, u32[]{:S(2)}) copy-start(bf16[3584,1024]{1,0:T(8,128)(2,1)S(1)} %get-tuple-element.40.refs_5_) | copy-start | bytes 22020100
  21.3 3.0 %copy-start.3 = (bf16[1024,3584]{1,0:T(8,128)(2,1)}, bf16[1024,3584]{1,0:T(8,128)(2,1)S(1)}, u32[]{:S(2)}) copy-start(bf16[1024,3584]{1,0:T(8,128)(2,1)S(1)} %get-tuple-element.41.refs_6_) | copy-start | bytes 22020100
  24.4 2.7 %collective-permute-start.6 = (bf16[64,3712]{1,0:T(8,128)(2,1)S(1)}, bf16[64,3712]{1,0:T(8,128)(2,1)S(1)}, u32[]{:S(2)}, u32[]{:S(2)}) collective-permute-start(bf16[64,3712]{1,0:T(8,128)(2,1)S(1)} %collective-permute-done.2.refs_2_), channel_id=1, source_target_pairs={{0,8},{8,0},{1,9},{9,1},{2,10},{10,2},{3,11},{11,3},{4,12},{12,4},... | collective-permute-start | bytes 1425416 | tf_op jit(solution)/shard_map/ppermute | solution.py:136
  24.4 14.6 %collective-permute-start.3 = (bf16[64,3712]{1,0:T(8,128)(2,1)S(1)}, bf16[64,3712]{1,0:T(8,128)(2,1)S(1)}, u32[]{:S(2)}, u32[]{:S(2)}) collective-permute-start(bf16[64,3712]{1,0:T(8,128)(2,1)S(1)} %collective-permute-done.1.refs_0_), channel_id=1, source_target_pairs={{0,8},{8,0},{1,9},{9,1},{2,10},{10,2},{3,11},{11,3},{4,12},{12,4},... | collective-permute-start | bytes 1425416 | tf_op jit(solution)/shard_map/ppermute | solution.py:136
  24.9 14.7 %collective-permute-start.4 = (bf16[64,3712]{1,0:T(8,128)(2,1)S(1)}, bf16[64,3712]{1,0:T(8,128)(2,1)S(1)}, u32[]{:S(2)}, u32[]{:S(2)}) collective-permute-start(bf16[64,3712]{1,0:T(8,128)(2,1)S(1)} %collective-permute-done.1.refs_0_), channel_id=1, source_target_pairs={{0,2},{1,3},{2,4},{3,5},{4,6},{5,7},{6,0},{7,1},{8,10},{9,11},{10,... | collective-permute-start | bytes 1425416 | tf_op jit(solution)/shard_map/ppermute | solution.py:142
  26.5 13.1 %collective-permute-start.5 = (bf16[64,3712]{1,0:T(8,128)(2,1)S(1)}, bf16[64,3712]{1,0:T(8,128)(2,1)S(1)}, u32[]{:S(2)}, u32[]{:S(2)}) collective-permute-start(bf16[64,3712]{1,0:T(8,128)(2,1)S(1)} %collective-permute-done.1.refs_0_), channel_id=1, source_target_pairs={{0,1},{1,0},{2,3},{3,2},{4,5},{5,4},{6,7},{7,6},{8,9},{9,8},{10,11... | collective-permute-start | bytes 1425416 | tf_op jit(solution)/shard_map/ppermute | solution.py:139
  27.0 3.1 %copy-start.2 = (bf16[3584,1024]{1,0:T(8,128)(2,1)S(1)}, bf16[3584,1024]{1,0:T(8,128)(2,1)}, u32[]{:S(2)}) copy-start(bf16[3584,1024]{1,0:T(8,128)(2,1)} %copy-done.1) | copy-start | bytes 22020100
  30.1 3.1 %copy-start.4 = (bf16[1024,3584]{1,0:T(8,128)(2,1)S(1)}, bf16[1024,3584]{1,0:T(8,128)(2,1)}, u32[]{:S(2)}) copy-start(bf16[1024,3584]{1,0:T(8,128)(2,1)} %copy-done.3) | copy-start | bytes 22020100
  39.6 15.2 %copy-start.9 = (s32[8]{0:T(128)S(1)}, s32[8]{0:T(128)}, u32[]{:S(2)}) copy-start(s32[8]{0:T(128)} %param.17) | copy-start | bytes 100
  39.6 3.2 %collective-permute-start.12 = (bf16[64,3712]{1,0:T(8,128)(2,1)S(1)}, bf16[64,3712]{1,0:T(8,128)(2,1)S(1)}, u32[]{:S(2)}, u32[]{:S(2)}) collective-permute-start(bf16[64,3712]{1,0:T(8,128)(2,1)S(1)} %collective-permute-done.5.refs_2_), channel_id=1, source_target_pairs={{0,8},{8,0},{1,9},{9,1},{2,10},{10,2},{3,11},{11,3},{4,12},{12,4},... | collective-permute-start | bytes 1425416 | tf_op jit(solution)/shard_map/ppermute | solution.py:136
  39.6 9.1 %collective-permute-start.9 = (bf16[64,3712]{1,0:T(8,128)(2,1)S(1)}, bf16[64,3712]{1,0:T(8,128)(2,1)S(1)}, u32[]{:S(2)}, u32[]{:S(2)}) collective-permute-start(bf16[64,3712]{1,0:T(8,128)(2,1)S(1)} %collective-permute-done.4.refs_0_), channel_id=1, source_target_pairs={{0,8},{8,0},{1,9},{9,1},{2,10},{10,2},{3,11},{11,3},{4,12},{12,4},... | collective-permute-start | bytes 1425416 | tf_op jit(solution)/shard_map/ppermute | solution.py:136
  40.1 14.6 %collective-permute-start.10 = (bf16[64,3712]{1,0:T(8,128)(2,1)S(1)}, bf16[64,3712]{1,0:T(8,128)(2,1)S(1)}, u32[]{:S(2)}, u32[]{:S(2)}) collective-permute-start(bf16[64,3712]{1,0:T(8,128)(2,1)S(1)} %collective-permute-done.4.refs_0_), channel_id=1, source_target_pairs={{0,2},{1,3},{2,4},{3,5},{4,6},{5,7},{6,0},{7,1},{8,10},{9,11},{10,... | collective-permute-start | bytes 1425416 | tf_op jit(solution)/shard_map/ppermute | solution.py:142
  41.3 13.5 %collective-permute-start.11 = (bf16[64,3712]{1,0:T(8,128)(2,1)S(1)}, bf16[64,3712]{1,0:T(8,128)(2,1)S(1)}, u32[]{:S(2)}, u32[]{:S(2)}) collective-permute-start(bf16[64,3712]{1,0:T(8,128)(2,1)S(1)} %collective-permute-done.4.refs_0_), channel_id=1, source_target_pairs={{0,1},{1,0},{2,3},{3,2},{4,5},{5,4},{6,7},{7,6},{8,9},{9,8},{10,11... | collective-permute-start | bytes 1425416 | tf_op jit(solution)/shard_map/ppermute | solution.py:139
  54.7 2.5 %collective-permute-start.21 = (bf16[128,3584]{1,0:T(8,128)(2,1)S(1)}, bf16[128,3584]{1,0:T(8,128)(2,1)S(1)}, u32[]{:S(2)}, u32[]{:S(2)}) collective-permute-start(bf16[128,3584]{1,0:T(8,128)(2,1)S(1)} %get-tuple-element.63), channel_id=1, source_target_pairs={{0,8},{8,0},{1,9},{9,1},{2,10},{10,2},{3,11},{11,3},{4,12},{12,4},... | collective-permute-start | bytes 2752520 | tf_op jit(solution)/shard_map/ppermute | solution.py:136
  54.8 39.6 %collective-permute-start.7 = (bf16[128,3584]{1,0:T(8,128)(2,1)S(1)}, bf16[128,3584]{1,0:T(8,128)(2,1)S(1)}, u32[]{:S(2)}, u32[]{:S(2)}) collective-permute-start(bf16[128,3584]{1,0:T(8,128)(2,1)S(1)} %get-tuple-element.45), channel_id=1, source_target_pairs={{0,8},{8,0},{1,9},{9,1},{2,10},{10,2},{3,11},{11,3},{4,12},{12,4},... | collective-permute-start | bytes 2752520 | tf_op jit(solution)/shard_map/ppermute | solution.py:136
  55.3 10.4 %collective-permute-start.13 = (bf16[64,3712]{1,0:T(8,128)(2,1)S(1)}, bf16[64,3712]{1,0:T(8,128)(2,1)S(1)}, u32[]{:S(2)}, u32[]{:S(2)}) collective-permute-start(bf16[64,3712]{1,0:T(8,128)(2,1)S(1)} %collective-permute-done.10.refs_0_), channel_id=1, source_target_pairs={{0,8},{8,0},{1,9},{9,1},{2,10},{10,2},{3,11},{11,3},{4,12},{12,4},... | collective-permute-start | bytes 1425416 | tf_op jit(solution)/shard_map/ppermute | solution.py:136
  55.4 13.7 %collective-permute-start.14 = (bf16[64,3712]{1,0:T(8,128)(2,1)S(1)}, bf16[64,3712]{1,0:T(8,128)(2,1)S(1)}, u32[]{:S(2)}, u32[]{:S(2)}) collective-permute-start(bf16[64,3712]{1,0:T(8,128)(2,1)S(1)} %collective-permute-done.10.refs_0_), channel_id=1, source_target_pairs={{0,1},{1,0},{2,3},{3,2},{4,5},{5,4},{6,7},{7,6},{8,9},{9,8},{10,11... | collective-permute-start | bytes 1425416 | tf_op jit(solution)/shard_map/ppermute | solution.py:139
  56.5 3.4 %collective-permute-start.15 = (bf16[64,3712]{1,0:T(8,128)(2,1)S(1)}, bf16[64,3712]{1,0:T(8,128)(2,1)S(1)}, u32[]{:S(2)}, u32[]{:S(2)}) collective-permute-start(bf16[64,3712]{1,0:T(8,128)(2,1)S(1)} %collective-permute-done.11.refs_2_), channel_id=1, source_target_pairs={{0,8},{8,0},{1,9},{9,1},{2,10},{10,2},{3,11},{11,3},{4,12},{12,4},... | collective-permute-start | bytes 1425416 | tf_op jit(solution)/shard_map/ppermute | solution.py:136
  57.3 21.1 %collective-permute-start.22 = (bf16[64,3584]{1,0:T(8,128)(2,1)S(1)}, bf16[64,3584]{1,0:T(8,128)(2,1)S(1)}, u32[]{:S(2)}, u32[]{:S(2)}) collective-permute-start(bf16[64,3584]{1,0:T(8,128)(2,1)S(1)} %add_convert_fusion.4), channel_id=1, source_target_pairs={{0,1},{1,0},{2,3},{3,2},{4,5},{5,4},{6,7},{7,6},{8,9},{9,8},{10,11... | collective-permute-start | bytes 1376264 | tf_op jit(solution)/shard_map/ppermute | solution.py:139
  69.1 9.8 %collective-permute-start.19 = (bf16[128,3584]{1,0:T(8,128)(2,1)S(1)}, bf16[128,3584]{1,0:T(8,128)(2,1)S(1)}, u32[]{:S(2)}, u32[]{:S(2)}) collective-permute-start(bf16[128,3584]{1,0:T(8,128)(2,1)S(1)} %get-tuple-element.61), channel_id=1, source_target_pairs={{0,8},{8,0},{1,9},{9,1},{2,10},{10,2},{3,11},{11,3},{4,12},{12,4},... | collective-permute-start | bytes 2752520 | tf_op jit(solution)/shard_map/ppermute | solution.py:136
  69.1 11.1 %collective-permute-start.16 = (bf16[64,3712]{1,0:T(8,128)(2,1)S(1)}, bf16[64,3712]{1,0:T(8,128)(2,1)S(1)}, u32[]{:S(2)}, u32[]{:S(2)}) collective-permute-start(bf16[64,3712]{1,0:T(8,128)(2,1)S(1)} %collective-permute-done.14.refs_2_), channel_id=1, source_target_pairs={{0,8},{8,0},{1,9},{9,1},{2,10},{10,2},{3,11},{11,3},{4,12},{12,4},... | collective-permute-start | bytes 1425416 | tf_op jit(solution)/shard_map/ppermute | solution.py:136
  78.6 14.2 %collective-permute-start.23 = (bf16[64,3584]{1,0:T(8,128)(2,1)S(1)}, bf16[64,3584]{1,0:T(8,128)(2,1)S(1)}, u32[]{:S(2)}, u32[]{:S(2)}) collective-permute-start(bf16[64,3584]{1,0:T(8,128)(2,1)S(1)} %add_convert_fusion.3), channel_id=1, source_target_pairs={{0,2},{1,3},{2,4},{3,5},{4,6},{5,7},{6,0},{7,1},{8,10},{9,11},{10,... | collective-permute-start | bytes 1376264 | tf_op jit(solution)/shard_map/ppermute | solution.py:142
  79.0 13.7 %collective-permute-start.20 = (bf16[64,3584]{1,0:T(8,128)(2,1)S(1)}, bf16[64,3584]{1,0:T(8,128)(2,1)S(1)}, u32[]{:S(2)}, u32[]{:S(2)}) collective-permute-start(bf16[64,3584]{1,0:T(8,128)(2,1)S(1)} %add_convert_fusion.5), channel_id=1, source_target_pairs={{0,1},{1,0},{2,3},{3,2},{4,5},{5,4},{6,7},{7,6},{8,9},{9,8},{10,11... | collective-permute-start | bytes 1376264 | tf_op jit(solution)/shard_map/ppermute | solution.py:139
  86.1 7.0 %collective-permute-start.17 = (bf16[128,3584]{1,0:T(8,128)(2,1)S(1)}, bf16[128,3584]{1,0:T(8,128)(2,1)S(1)}, u32[]{:S(2)}, u32[]{:S(2)}) collective-permute-start(bf16[128,3584]{1,0:T(8,128)(2,1)S(1)} %get-tuple-element.59), channel_id=1, source_target_pairs={{0,8},{8,0},{1,9},{9,1},{2,10},{10,2},{3,11},{11,3},{4,12},{12,4},... | collective-permute-start | bytes 2752520 | tf_op jit(solution)/shard_map/ppermute | solution.py:136
  93.0 13.0 %collective-permute-start.24 = (bf16[64,3584]{1,0:T(8,128)(2,1)S(1)}, bf16[64,3584]{1,0:T(8,128)(2,1)S(1)}, u32[]{:S(2)}, u32[]{:S(2)}) collective-permute-start(bf16[64,3584]{1,0:T(8,128)(2,1)S(1)} %add_convert_fusion.2), channel_id=1, source_target_pairs={{0,2},{1,3},{2,4},{3,5},{4,6},{5,7},{6,0},{7,1},{8,10},{9,11},{10,... | collective-permute-start | bytes 1376264 | tf_op jit(solution)/shard_map/ppermute | solution.py:142
  93.1 15.6 %copy-start.8 = (bf16[8,256,576]{1,2,0:T(8,128)(2,1)S(1)}, bf16[8,256,576]{1,2,0:T(8,128)(2,1)}, u32[]{:S(2)}) copy-start(bf16[8,256,576]{1,2,0:T(8,128)(2,1)} %param.16) | copy-start | bytes 7077892
  93.2 13.5 %collective-permute-start.18 = (bf16[64,3584]{1,0:T(8,128)(2,1)S(1)}, bf16[64,3584]{1,0:T(8,128)(2,1)S(1)}, u32[]{:S(2)}, u32[]{:S(2)}) collective-permute-start(bf16[64,3584]{1,0:T(8,128)(2,1)S(1)} %add_convert_fusion.6), channel_id=1, source_target_pairs={{0,1},{1,0},{2,3},{3,2},{4,5},{5,4},{6,7},{7,6},{8,9},{9,8},{10,11... | collective-permute-start | bytes 1376264 | tf_op jit(solution)/shard_map/ppermute | solution.py:139
  95.3 19.0 %collective-permute-start.8 = (bf16[64,3584]{1,0:T(8,128)(2,1)}, bf16[64,3584]{1,0:T(8,128)(2,1)S(1)}, u32[]{:S(2)}, u32[]{:S(2)}) collective-permute-start(bf16[64,3584]{1,0:T(8,128)(2,1)} %add_convert_fusion.7), channel_id=1, source_target_pairs={{0,1},{1,0},{2,3},{3,2},{4,5},{5,4},{6,7},{7,6},{8,9},{9,8},{10,11... | collective-permute-start | bytes 1376264 | tf_op jit(solution)/shard_map/ppermute | solution.py:139
  107.7 11.7 %collective-permute-start.25 = (bf16[64,3584]{1,0:T(8,128)(2,1)}, bf16[64,3584]{1,0:T(8,128)(2,1)}, u32[]{:S(2)}, u32[]{:S(2)}) collective-permute-start(bf16[64,3584]{1,0:T(8,128)(2,1)} %add_convert_fusion.1), channel_id=1, source_target_pairs={{0,2},{1,3},{2,4},{3,5},{4,6},{5,7},{6,0},{7,1},{8,10},{9,11},{10,... | collective-permute-start | bytes 1376264 | tf_op jit(solution)/shard_map/ppermute | solution.py:142

commit v3 on v2

--- a/solution.py
+++ b/solution.py
@@ -9,7 +9,8 @@
 PAIR = 2
 
 
-VMEM_LIMIT = 16 * 1024 * 1024
+VMEM_LIMIT = 28 * 1024 * 1024
+LOAD_LIMIT = 28 * 1024 * 1024
 score_scale = 192.0 ** (-0.5)
 
 
@@ -29,21 +30,24 @@
     ).astype(jnp.bfloat16)
 
 
-def extend_kernel(experts, hidden, routes, route_weights, out):
+def extend_kernel(experts, hidden, routes, route_weights, out, sem):
     tokens, model_width = hidden.shape
-    out[:, :model_width] = hidden[...]
+    copy = pltpu.make_async_copy(hidden, out.at[:, :model_width], sem)
+    copy.start()
     shape = (tokens, out.shape[1] - model_width)
     lane = lax.broadcasted_iota(jnp.int32, shape, 1)
     group = (lane >= experts).astype(jnp.int32) + (lane >= 2 * experts).astype(jnp.int32)
     expert = lane - group * experts
     weight = jnp.zeros(shape, jnp.float32)
-    for k in range(routes.shape[1]):
-        weight += jnp.where(routes[:, k : k + 1] == expert, route_weights[:, k : k + 1], 0.0)
+    route, route_weight = routes[...].T, route_weights[...].T
+    for k in range(routes.shape[0]):
+        weight += jnp.where(route[:, k : k + 1] == expert, route_weight[:, k : k + 1], 0.0)
     high = weight.astype(jnp.bfloat16).astype(jnp.float32)
     middle = (weight - high).astype(jnp.bfloat16).astype(jnp.float32)
     low = weight - high - middle
     part = jnp.where(group == 0, high, jnp.where(group == 1, middle, low))
     out[:, model_width:] = part.astype(jnp.bfloat16)
+    copy.wait()
 
 
 def extend(hidden_rows, routes, route_weights, experts):
@@ -53,14 +57,16 @@
     return pl.pallas_call(
         lambda *refs: extend_kernel(experts, *refs),
         out_shape=jax.ShapeDtypeStruct((tokens, model_width + extra), jnp.bfloat16),
-        in_specs=[inside] * 3,
+        in_specs=[pl.BlockSpec(memory_space=pl.ANY), inside, inside],
         out_specs=inside,
-        compiler_params=pltpu.CompilerParams(vmem_limit_bytes=VMEM_LIMIT),
+        scratch_shapes=[pltpu.SemaphoreType.DMA],
+        compiler_params=pltpu.CompilerParams(vmem_limit_bytes=60 * 1024 * 1024),
         cost_estimate=pl.CostEstimate(flops=0, bytes_accessed=hidden_rows.size * 4, transcendentals=0),
-    )(hidden_rows, routes, route_weights)
-
-
-def expert_kernel(experts, own, other, own_y, other_y, gate, up, down, keep, send, rows):
+    )(hidden_rows, routes.T, route_weights.T)
+
+
+def expert_kernel(experts, own, other, own_y, other_y, gate, up, down, *refs):
+    outs, rows = refs[:-1], refs[-1]
     tokens = own.shape[0]
     model_width = gate.shape[0]
     for place, block in enumerate((own, own_y, other, other_y)):
@@ -76,8 +82,8 @@
     hidden = (gate_term / (1.0 + jnp.exp(-gate_term)) * up_term).astype(jnp.bfloat16)
     produced = jnp.dot(hidden, down[...], preferred_element_type=jnp.float32)
     produced = (produced.astype(jnp.bfloat16).astype(jnp.float32) * weight).astype(jnp.bfloat16)
-    keep[...] = produced[: 2 * tokens]
-    send[...] = produced[2 * tokens :]
+    for place, out in enumerate(outs):
+        out[...] = produced[place * tokens : (place + 1) * tokens]
 
 
 def load_kernel(*refs):
@@ -98,7 +104,7 @@
         in_specs=[pl.BlockSpec(memory_space=pl.ANY)] * len(arrays),
         out_specs=[pl.BlockSpec(memory_space=pltpu.VMEM)] * len(arrays),
         scratch_shapes=[pltpu.SemaphoreType.DMA] * len(arrays),
-        compiler_params=pltpu.CompilerParams(vmem_limit_bytes=VMEM_LIMIT),
+        compiler_params=pltpu.CompilerParams(vmem_limit_bytes=LOAD_LIMIT),
         cost_estimate=pl.CostEstimate(
             flops=0, bytes_accessed=sum(a.size * 2 for a in arrays), transcendentals=0
         ),
@@ -111,16 +117,12 @@
     inside = pl.BlockSpec(memory_space=pltpu.VMEM)
     return pl.pallas_call(
         lambda *refs: expert_kernel(experts, *refs),
-        out_shape=[jax.ShapeDtypeStruct((2 * tokens, model_width), jnp.bfloat16)] * 2,
+        out_shape=[jax.ShapeDtypeStruct((tokens, model_width), jnp.bfloat16)] * 4,
         in_specs=[inside] * 7,
-        out_specs=[inside] * 2,
+        out_specs=[inside] * 4,
         scratch_shapes=[pltpu.VMEM((4 * tokens, extended), jnp.bfloat16)],
         compiler_params=pltpu.CompilerParams(vmem_limit_bytes=VMEM_LIMIT),
-        cost_estimate=pl.CostEstimate(
-            flops=2 * 3 * 4 * tokens * model_width * hidden_width,
-            bytes_accessed=16 * tokens * model_width,
-            transcendentals=4 * tokens * hidden_width,
-        ),
+        cost_estimate=pl.CostEstimate(flops=0, bytes_accessed=0, transcendentals=0),
     )(*blocks, w_gate, w_up, w_down)
 
 
@@ -143,51 +145,71 @@
 
     weights = load_inside(w_gate[0], w_up[0], w_down[0])
 
-    attended = attend(queries, kv_cache, lengths)
-
-    own = [extend(hidden_rows, routes, route_weights, experts)]
-    other, own_y, other_y, partial = [], [], [], []
+    own, own_y, other, other_y = [extend(hidden_rows, routes, route_weights, experts)], [], [], []
+    keep, keep_y, got, got_y, back = [], [], [], [], {}
+
+    def compute(slot):
+        other_y.append(core(own_y[slot]))
+        blocks = own[slot], other[slot], own_y[slot], other_y[slot]
+        kept, kept_y, sent, sent_y = run_expert(experts, blocks, *weights)
+        keep.append(kept)
+        keep_y.append(kept_y)
+        got_y.append(core(sent_y))
+        got.append(core(sent))
+
+    def away(slot):
+        return pair((keep_y[slot].astype(f32) + got_y[slot].astype(f32)).astype(bf16))
+
+    def onward(slot, carried):
+        value = keep[slot].astype(f32) + got[slot].astype(f32) + back[slot].astype(f32)
+        if carried is not None:
+            value = value + carried.astype(f32)
+        return value.astype(bf16)
+
     for slot in range(steps):
-        arrived = {"own_y": pair(own[slot]), "other": core(own[slot])}
+        arrived = {"other": core(own[slot])}
+        if slot < steps - 1 or steps < 3:
+            arrived["own_y"] = pair(own[slot])
+        else:
+            arrived["own_y"] = ring(own_y[slot - 1])
+            arrived["back"] = away(1)
         if slot < steps - 1:
             arrived["own"] = ring(own[slot])
         if slot == 0:
             arrived["weights"] = weights
         else:
-            other_y.append(core(own_y[slot - 1]))
-            blocks = own[slot - 1], other[slot - 1], own_y[slot - 1], other_y[slot - 1]
-            arrived["partial"] = run_expert(experts, blocks, *weights)
+            compute(slot - 1)
+            arrived["keep"] = keep_y[slot - 1]
         arrived = lax.optimization_barrier(arrived)
+        other.append(arrived["other"])
         own_y.append(arrived["own_y"])
-        other.append(arrived["other"])
-        if slot < steps - 1:
+        if "own" in arrived:
             own.append(arrived["own"])
-        if slot == 0:
+        if "weights" in arrived:
             weights = arrived["weights"]
-        else:
-            partial.append(arrived["partial"])
-    other_y.append(core(own_y[-1]))
-    blocks = own[-1], other[-1], own_y[-1], other_y[-1]
-    partial.append(run_expert(experts, blocks, *weights))
-
-    got = [core(send) for keep, send in partial]
-
-    def away(slot):
-        return pair((partial[slot][0][tokens:].astype(f32) + got[slot][tokens:].astype(f32)).astype(bf16))
-
-    def kept(slot):
-        return partial[slot][0][:tokens].astype(f32) + got[slot][:tokens].astype(f32)
-
-    back = {}
+        if "keep" in arrived:
+            keep_y[slot - 1] = arrived["keep"]
+        if "back" in arrived:
+            back[1] = arrived["back"]
+
+    attended = attend(queries, kv_cache, lengths)
+
+    order = list(range(1, steps)) + [0]
+    if steps > 1 and 1 not in back:
+        back[1] = away(1)
     carried = None
-    for slot in list(range(1, steps)) + [0]:
-        back[slot] = away(slot)
-        value = kept(slot) + back[slot].astype(f32)
-        if carried is not None:
-            value = value + carried.astype(f32)
-        value = value.astype(bf16)
-        carried = ring(value) if slot else value
-    return (carried, attended)
+    for place, slot in enumerate(order[:-1]):
+        arrived = {"carried": ring(onward(slot, carried))}
+        if place == 0:
+            compute(steps - 1)
+            arrived["keep"] = keep_y[-1]
+        following = order[place + 1]
+        arrived["back"] = away(following)
+        arrived = lax.optimization_barrier(arrived)
+        carried, back[following] = arrived["carried"], arrived["back"]
+        if place == 0:
+            keep_y[-1] = arrived["keep"]
+    return (onward(0, carried), attended)
 
 
 def solution(mesh):

time: 122 us -> 112 us (0.918)
  local copies, waits for them, and re-layouts: 20.9 us -> 0.02 us
  waiting for transfers between devices: 44.4 us -> 50.4 us
  Pallas kernels: 27.8 us -> 33.4 us
    unnamed x22 -> x8, local copies, waits for them, and re-layouts: 20.9 us -> 0.02 us
    ppermute x6 -> x7, waiting for transfers between devices: 28.2 us -> 46.1 us  [ring(): lax.ppermute(value, 'rank', [(i, (i + PAIR) % rank_count) for i in range(...]
    ppermute x8 -> x7, waiting for transfers between devices: 14.3 us -> 3.34 us  [pair(): return lax.ppermute(value, 'rank', [(i, i ^ 1) for i in range(rank_count)])]
    pallas_call x1, Pallas kernels: 4.08 us -> 7.34 us  [load_inside(): pl.pallas_call(load_kernel, out_shape=[jax.ShapeDtypeStruct(a.shape, a.dt...]
    pallas_call x1, Pallas kernels: 0.22 us -> 2.57 us  [extend(): pl.pallas_call(lambda *refs: extend_kernel(experts, *refs), out_shape=jax...]
    ppermute x6 -> x7, starting transfers between devices: 6.64 us -> 5.16 us  [ring(): lax.ppermute(value, 'rank', [(i, (i + PAIR) % rank_count) for i in range(...]
    ppermute x12 -> x16, starting transfers between devices: 2.93 us -> 4.01 us  [core(): return lax.ppermute(value, 'node', [(i, 1 - i) for i in range(node_count)])]
    ppermute x8 -> x7, starting transfers between devices: 9.11 us -> 9.88 us  [pair(): return lax.ppermute(value, 'rank', [(i, i ^ 1) for i in range(rank_count)])]
  transfers between devices with their start and end apart: 26 -> 30, of which waited for: 11 -> 10; matrix products, arithmetic and copies ran while one was open for 6% -> 5% of each run, Pallas kernels for 23% -> 28%
where the time goes in v3:
time: 112 us
  waiting for transfers between devices  50.4 us (45%)
  Pallas kernels  33.4 us (30%)
  starting transfers between devices  19.1 us (17%)
  other arithmetic  4.14 us (4%)
  matrix products  3.95 us (4%)
    ppermute x7, waiting for transfers between devices, ring(): lax.ppermute(value, 'rank', [(i, (i + PAIR) % rank_count) for i in range(...  46.1 us
    pallas_call x4, Pallas kernels, run_expert(): pl.pallas_call(lambda *refs: expert_kernel(experts, *refs), out_shape=[ja...  23.5 us
    ppermute x7, starting transfers between devices, pair(): return lax.ppermute(value, 'rank', [(i, i ^ 1) for i in range(rank_count)])  9.88 us
    pallas_call x1, Pallas kernels, load_inside(): pl.pallas_call(load_kernel, out_shape=[jax.ShapeDtypeStruct(a.shape, a.dt...  7.34 us
    ppermute x7, starting transfers between devices, ring(): lax.ppermute(value, 'rank', [(i, (i + PAIR) % rank_count) for i in range(...  5.16 us
    ppermute x16, starting transfers between devices, core(): return lax.ppermute(value, 'node', [(i, 1 - i) for i in range(node_count)])  4.01 us
    convert_element_type x4, other arithmetic, onward(): return value.astype(bf16)  3.4 us
    dot_general x1, matrix products, attend(): jnp.einsum('bhl,blc->bhc', softmax_weights, latent_values, preferred_elem...  3.4 us
  transfers between devices with their start and end apart: 30, of which 10 were waited for; matrix products, arithmetic and copies ran while one was open for 5% of the time, Pallas kernels for 28%

profile of v3, /device:TPU:0, one launch (start us, length us, event | category | flops | bytes accessed | tf_op | source)
XLA Modules:
  0.0 111.8 jit_solution(12640911479186606909)
XLA Ops:
  0.6 0.0 copy-start
  0.6 2.6 %shard_map.104.refs_0_ = bf16[64,3712]{1,0:T(8,128)(2,1)} custom-call(bf16[64,3584]{1,0:T(8,128)(2,1)} %refs_0_.1, s32[8,64]{1,0:T(8,128)} %bitcast.12, f32[8,64]{1,0:T(8,128)} %bitcast.13), custom_call_target="tpu_custom_call" | custom-call | bytes 917504 | tf_op jit(solution)/shard_map/pallas_call | solution.py:57
  3.2 0.5 collective-permute-start
  3.7 2.6 %collective-permute-start.1 = (bf16[64,3712]{1,0:T(8,128)(2,1)}, bf16[64,3712]{1,0:T(8,128)(2,1)S(1)}, u32[]{:S(2)}, u32[]{:S(2)}) collective-permute-start(bf16[64,3712]{1,0:T(8,128)(2,1)} %shard_map.104.refs_0_), channel_id=1, source_target_pairs={{0,2},{1,3},{2,4},{3,5},{4,6},{5,7},{6,0},{7,1},{8,10},{9,11},{10,... | collective-permute-start | bytes 1425416 | tf_op jit(solution)/shard_map/ppermute | solution.py:144
  6.4 1.5 %collective-permute-start.2 = (bf16[64,3712]{1,0:T(8,128)(2,1)}, bf16[64,3712]{1,0:T(8,128)(2,1)S(1)}, u32[]{:S(2)}, u32[]{:S(2)}) collective-permute-start(bf16[64,3712]{1,0:T(8,128)(2,1)} %shard_map.104.refs_0_), channel_id=1, source_target_pairs={{0,1},{1,0},{2,3},{3,2},{4,5},{5,4},{6,7},{7,6},{8,9},{9,8},{10,11... | collective-permute-start | bytes 1425416 | tf_op jit(solution)/shard_map/ppermute | solution.py:141
  7.9 7.3 %shard_map.105 = (bf16[3584,1024]{1,0:T(8,128)(2,1)S(1)}, bf16[3584,1024]{1,0:T(8,128)(2,1)S(1)}, bf16[1024,3584]{1,0:T(8,128)(2,1)S(1)}) custom-call(bf16[3584,1024]{1,0:T(8,128)(2,1)} %bitcast.9, bf16[3584,1024]{1,0:T(8,128)(2,1)} %bitcast.10, bf16[1024,3584]{1,0:T(8,128)(2,1)} %bitcast.11), custom_call_target="tpu_custom_call" | custom-call | bytes 22020096 | tf_op jit(solution)/shard_map/pallas_call | solution.py:101
  15.2 0.0 collective-permute-done.refs_1_
  15.3 4.8 %collective-permute-done.1.refs_0_ = bf16[64,3712]{1,0:T(8,128)(2,1)S(1)} collective-permute-done((bf16[64,3712]{1,0:T(8,128)(2,1)}, bf16[64,3712]{1,0:T(8,128)(2,1)S(1)}, u32[]{:S(2)}, u32[]{:S(2)}) %collective-permute-start.1) | collective-permute-done | bytes 475168 | tf_op jit(solution)/shard_map/ppermute | solution.py:144
  20.1 0.0 collective-permute-done.2.refs_2_
  20.1 0.5 collective-permute-start.5
  20.6 1.0 collective-permute-start.6
  21.6 1.5 %collective-permute-start.7 = (bf16[64,3712]{1,0:T(8,128)(2,1)S(1)}, bf16[64,3712]{1,0:T(8,128)(2,1)S(1)}, u32[]{:S(2)}, u32[]{:S(2)}) collective-permute-start(bf16[64,3712]{1,0:T(8,128)(2,1)S(1)} %collective-permute-done.1.refs_0_), channel_id=1, source_target_pairs={{0,1},{1,0},{2,3},{3,2},{4,5},{5,4},{6,7},{7,6},{8,9},{9,8},{10,11... | collective-permute-start | bytes 1425416 | tf_op jit(solution)/shard_map/ppermute | solution.py:141
  23.1 5.9 %shard_map.106 = (bf16[64,3584]{1,0:T(8,128)(2,1)S(1)}, bf16[64,3584]{1,0:T(8,128)(2,1)S(1)}, bf16[64,3584]{1,0:T(8,128)(2,1)S(1)}, bf16[64,3584]{1,0:T(8,128)(2,1)S(1)}) custom-call(bf16[64,3712]{1,0:T(8,128)(2,1)S(1)} %copy-done.1, bf16[64,3712]{1,0:T(8,128)(2,1)S(1)} %collective-permute-done.refs_1_, bf16[64,3712]{1,0:T(8,128)(2,1)S(1)} %collective-permute-done.2.refs_2_, ...), custom_call_target="tpu_custom_call" | custom-call | tf_op jit(solution)/shard_map/pallas_call | solution.py:118
  29.0 6.2 %collective-permute-done.6.refs_0_ = bf16[64,3712]{1,0:T(8,128)(2,1)S(1)} collective-permute-done((bf16[64,3712]{1,0:T(8,128)(2,1)S(1)}, bf16[64,3712]{1,0:T(8,128)(2,1)S(1)}, u32[]{:S(2)}, u32[]{:S(2)}) %collective-permute-start.6) | collective-permute-done | bytes 475168 | tf_op jit(solution)/shard_map/ppermute | solution.py:144
  35.2 0.0 collective-permute-done.7.refs_2_
  35.2 0.0 collective-permute-start.10
  35.2 0.5 collective-permute-start.11
  35.7 0.5 collective-permute-start.12
  36.2 1.5 %collective-permute-start.13 = (bf16[64,3712]{1,0:T(8,128)(2,1)S(1)}, bf16[64,3712]{1,0:T(8,128)(2,1)S(1)}, u32[]{:S(2)}, u32[]{:S(2)}) collective-permute-start(bf16[64,3712]{1,0:T(8,128)(2,1)S(1)} %collective-permute-done.6.refs_0_), channel_id=1, source_target_pairs={{0,1},{1,0},{2,3},{3,2},{4,5},{5,4},{6,7},{7,6},{8,9},{9,8},{10,11... | collective-permute-start | bytes 1425416 | tf_op jit(solution)/shard_map/ppermute | solution.py:141
  37.7 5.9 %shard_map.107 = (bf16[64,3584]{1,0:T(8,128)(2,1)S(1)}, bf16[64,3584]{1,0:T(8,128)(2,1)S(1)}, bf16[64,3584]{1,0:T(8,128)(2,1)S(1)}, bf16[64,3584]{1,0:T(8,128)(2,1)S(1)}) custom-call(bf16[64,3712]{1,0:T(8,128)(2,1)S(1)} %collective-permute-done.1.refs_0_, bf16[64,3712]{1,0:T(8,128)(2,1)S(1)} %collective-permute-done.5.refs_1_, ...), custom_call_target="tpu_custom_call" | custom-call | tf_op jit(solution)/shard_map/pallas_call | solution.py:118
  43.6 0.1 collective-permute-start.14
  43.7 6.6 %collective-permute-done.12.refs_0_ = bf16[64,3712]{1,0:T(8,128)(2,1)S(1)} collective-permute-done((bf16[64,3712]{1,0:T(8,128)(2,1)S(1)}, bf16[64,3712]{1,0:T(8,128)(2,1)S(1)}, u32[]{:S(2)}, u32[]{:S(2)}) %collective-permute-start.12) | collective-permute-done | bytes 475168 | tf_op jit(solution)/shard_map/ppermute | solution.py:144
  50.3 0.0 collective-permute-start.16
  50.3 0.0 collective-permute-start.18
  50.3 0.5 collective-permute-start.17
  50.8 0.1 add_convert_fusion.6
  50.9 1.6 %collective-permute-start.15 = (bf16[64,3584]{1,0:T(8,128)(2,1)S(1)}, bf16[64,3584]{1,0:T(8,128)(2,1)S(1)}, u32[]{:S(2)}, u32[]{:S(2)}) collective-permute-start(bf16[64,3584]{1,0:T(8,128)(2,1)S(1)} %add_convert_fusion.6), channel_id=1, source_target_pairs={{0,1},{1,0},{2,3},{3,2},{4,5},{5,4},{6,7},{7,6},{8,9},{9,8},{10,11... | collective-permute-start | bytes 1376264 | tf_op jit(solution)/shard_map/ppermute | solution.py:141
  52.5 0.0 collective-permute-done.16.refs_3_
  52.5 5.9 %shard_map.108 = (bf16[64,3584]{1,0:T(8,128)(2,1)S(1)}, bf16[64,3584]{1,0:T(8,128)(2,1)S(1)}, bf16[64,3584]{1,0:T(8,128)(2,1)S(1)}, bf16[64,3584]{1,0:T(8,128)(2,1)S(1)}) custom-call(bf16[64,3712]{1,0:T(8,128)(2,1)S(1)} %collective-permute-done.6.refs_0_, bf16[64,3712]{1,0:T(8,128)(2,1)S(1)} %collective-permute-done.11.refs_1_, ...), custom_call_target="tpu_custom_call" | custom-call | tf_op jit(solution)/shard_map/pallas_call | solution.py:118
  58.4 0.0 copy-start.3
  58.4 0.6 collective-permute-start.21
  59.0 6.4 %collective-permute-done.18.refs_2_ = bf16[64,3712]{1,0:T(8,128)(2,1)S(1)} collective-permute-done((bf16[64,3712]{1,0:T(8,128)(2,1)S(1)}, bf16[64,3712]{1,0:T(8,128)(2,1)S(1)}, u32[]{:S(2)}, u32[]{:S(2)}) %collective-permute-start.18) | collective-permute-done | bytes 475168 | tf_op jit(solution)/shard_map/ppermute | solution.py:144
  65.4 0.2 add_convert_fusion.4
  65.5 0.1 collective-permute-start.24
  65.6 0.1 collective-permute-start.19
  65.7 0.0 collective-permute-done.21
  65.7 0.1 add_convert_fusion.5
  65.8 1.6 %collective-permute-start.22 = (bf16[64,3584]{1,0:T(8,128)(2,1)S(1)}, bf16[64,3584]{1,0:T(8,128)(2,1)S(1)}, u32[]{:S(2)}, u32[]{:S(2)}) collective-permute-start(bf16[64,3584]{1,0:T(8,128)(2,1)S(1)} %add_convert_fusion.5), channel_id=1, source_target_pairs={{0,1},{1,0},{2,3},{3,2},{4,5},{5,4},{6,7},{7,6},{8,9},{9,8},{10,11... | collective-permute-start | bytes 1376264 | tf_op jit(solution)/shard_map/ppermute | solution.py:141
  67.4 0.2 collective-permute-start.27
  67.6 0.1 iota_compare_fusion
  67.7 0.3 collective-permute-start.8
  68.0 0.0 collective-permute-done.19.refs_3_
  68.0 0.2 collective-permute-start.4
  68.2 5.9 %shard_map.109 = (bf16[64,3584]{1,0:T(8,128)(2,1)S(1)}, bf16[64,3584]{1,0:T(8,128)(2,1)S(1)}, bf16[64,3584]{1,0:T(8,128)(2,1)S(1)}, bf16[64,3584]{1,0:T(8,128)(2,1)S(1)}) custom-call(bf16[64,3712]{1,0:T(8,128)(2,1)S(1)} %collective-permute-done.12.refs_0_, bf16[64,3712]{1,0:T(8,128)(2,1)S(1)} %collective-permute-done.17.refs_1_, ...), custom_call_target="tpu_custom_call" | custom-call | tf_op jit(solution)/shard_map/pallas_call | solution.py:118
  74.1 5.5 %collective-permute-done.24 = bf16[64,3584]{1,0:T(8,128)(2,1)S(1)} collective-permute-done((bf16[64,3584]{1,0:T(8,128)(2,1)S(1)}, bf16[64,3584]{1,0:T(8,128)(2,1)S(1)}, u32[]{:S(2)}, u32[]{:S(2)}) %collective-permute-start.24) | collective-permute-done | bytes 458784 | tf_op jit(solution)/shard_map/ppermute | solution.py:144
  79.5 0.0 collective-permute-start.25
  79.6 0.2 add_convert_fusion.2
  79.8 0.1 collective-permute-start.28
  79.9 0.5 collective-permute-start.20
  80.4 0.9 collective-permute-done.25
  81.4 0.1 add_convert_fusion.3
  81.5 1.6 %collective-permute-start.26 = (bf16[64,3584]{1,0:T(8,128)(2,1)S(1)}, bf16[64,3584]{1,0:T(8,128)(2,1)S(1)}, u32[]{:S(2)}, u32[]{:S(2)}) collective-permute-start(bf16[64,3584]{1,0:T(8,128)(2,1)S(1)} %add_convert_fusion.3), channel_id=1, source_target_pairs={{0,1},{1,0},{2,3},{3,2},{4,5},{5,4},{6,7},{7,6},{8,9},{9,8},{10,11... | collective-permute-start | bytes 1376264 | tf_op jit(solution)/shard_map/ppermute | solution.py:141
  83.1 0.1 add_convert_fusion.7
  83.2 0.6 collective-permute-start.9
  83.7 10.8 %collective-permute-done.28 = bf16[64,3584]{1,0:T(8,128)(2,1)S(1)} collective-permute-done((bf16[64,3584]{1,0:T(8,128)(2,1)S(1)}, bf16[64,3584]{1,0:T(8,128)(2,1)S(1)}, u32[]{:S(2)}, u32[]{:S(2)}) %collective-permute-start.28) | collective-permute-done | bytes 458784 | tf_op jit(solution)/shard_map/ppermute | solution.py:144
  94.6 0.3 collective-permute-done.26
  94.9 1.0 add_convert_fusion.1
  95.9 0.8 collective-permute-start.29
  96.7 0.6 fusion.8
  97.3 0.2 fusion.11
  97.5 3.4 %fusion.3 = bf16[8,64,512]{2,1,0:T(8,128)(2,1)} fusion(bf16[8,256,576]{1,2,0:T(8,128)(2,1)} %param.16, f32[8,64]{1,0:T(8,128)S(1)} %fusion.11, f32[8,64,256]{2,1,0:T(8,128)S(1)} %fusion.8), kind=kOutput, calls=%fused_computation.3 | convolution fusion | flops 134873856 | bytes 3674112 | tf_op jit(solution)/shard_map/bhl,blc->bhc/dot_general | solution.py:28
  100.9 3.0 %collective-permute-done.9 = bf16[64,3584]{1,0:T(8,128)(2,1)S(1)} collective-permute-done((bf16[64,3584]{1,0:T(8,128)(2,1)S(1)}, bf16[64,3584]{1,0:T(8,128)(2,1)S(1)}, u32[]{:S(2)}, u32[]{:S(2)}) %collective-permute-start.9) | collective-permute-done | bytes 458784 | tf_op jit(solution)/shard_map/ppermute | solution.py:141
  103.9 5.9 %collective-permute-done.29 = bf16[64,3584]{1,0:T(8,128)(2,1)} collective-permute-done((bf16[64,3584]{1,0:T(8,128)(2,1)}, bf16[64,3584]{1,0:T(8,128)(2,1)}, u32[]{:S(2)}, u32[]{:S(2)}) %collective-permute-start.29) | collective-permute-done | bytes 458784 | tf_op jit(solution)/shard_map/ppermute | solution.py:144
  109.8 2.0 %add_convert_fusion = bf16[64,3584]{1,0:T(8,128)(2,1)} fusion(bf16[64,3584]{1,0:T(8,128)(2,1)} %collective-permute-done.29, bf16[64,3584]{1,0:T(8,128)(2,1)S(1)} %collective-permute-done.9, bf16[64,3584]{1,0:T(8,128)(2,1)S(1)} %collective-permute-done.4, bf16[64,3584]{1,0:T(8,128)(2,1)S(1)} %get-tuple-element.54), kind=kLoop, calls=%fused_computation.8 | loop fusion | flops 1835008 | bytes 2293760 | tf_op jit(solution)/shard_map/convert_element_type | solution.py:167
  (22 shorter events, 0.1 us)
Async XLA Ops:
  0.6 96.1 %copy-start = (bf16[8,64,576]{2,1,0:T(8,128)(2,1)S(1)}, bf16[8,64,576]{2,1,0:T(8,128)(2,1)}, u32[]{:S(2)}) copy-start(bf16[8,64,576]{2,1,0:T(8,128)(2,1)} %param.15) | copy-start | bytes 1769476
  3.2 12.0 %collective-permute-start = (bf16[64,3712]{1,0:T(8,128)(2,1)}, bf16[64,3712]{1,0:T(8,128)(2,1)S(1)}, u32[]{:S(2)}, u32[]{:S(2)}) collective-permute-start(bf16[64,3712]{1,0:T(8,128)(2,1)} %shard_map.104.refs_0_), channel_id=1, source_target_pairs={{0,8},{8,0},{1,9},{9,1},{2,10},{10,2},{3,11},{11,3},{4,12},{12,4},... | collective-permute-start | bytes 1425416 | tf_op jit(solution)/shard_map/ppermute | solution.py:138
  3.7 16.3 %collective-permute-start.1 = (bf16[64,3712]{1,0:T(8,128)(2,1)}, bf16[64,3712]{1,0:T(8,128)(2,1)S(1)}, u32[]{:S(2)}, u32[]{:S(2)}) collective-permute-start(bf16[64,3712]{1,0:T(8,128)(2,1)} %shard_map.104.refs_0_), channel_id=1, source_target_pairs={{0,2},{1,3},{2,4},{3,5},{4,6},{5,7},{6,0},{7,1},{8,10},{9,11},{10,... | collective-permute-start | bytes 1425416 | tf_op jit(solution)/shard_map/ppermute | solution.py:144
  6.4 13.7 %collective-permute-start.2 = (bf16[64,3712]{1,0:T(8,128)(2,1)}, bf16[64,3712]{1,0:T(8,128)(2,1)S(1)}, u32[]{:S(2)}, u32[]{:S(2)}) collective-permute-start(bf16[64,3712]{1,0:T(8,128)(2,1)} %shard_map.104.refs_0_), channel_id=1, source_target_pairs={{0,1},{1,0},{2,3},{3,2},{4,5},{5,4},{6,7},{7,6},{8,9},{9,8},{10,11... | collective-permute-start | bytes 1425416 | tf_op jit(solution)/shard_map/ppermute | solution.py:141
  7.9 15.2 %copy-start.1 = (bf16[64,3712]{1,0:T(8,128)(2,1)S(1)}, bf16[64,3712]{1,0:T(8,128)(2,1)}, u32[]{:S(2)}) copy-start(bf16[64,3712]{1,0:T(8,128)(2,1)} %shard_map.104.refs_0_) | copy-start | bytes 1425412
  20.1 3.0 %collective-permute-start.3 = (bf16[64,3712]{1,0:T(8,128)(2,1)S(1)}, bf16[64,3712]{1,0:T(8,128)(2,1)S(1)}, u32[]{:S(2)}, u32[]{:S(2)}) collective-permute-start(bf16[64,3712]{1,0:T(8,128)(2,1)S(1)} %collective-permute-done.2.refs_2_), channel_id=1, source_target_pairs={{0,8},{8,0},{1,9},{9,1},{2,10},{10,2},{3,11},{11,3},{4,12},{12,4},... | collective-permute-start | bytes 1425416 | tf_op jit(solution)/shard_map/ppermute | solution.py:138
  20.1 8.9 %collective-permute-start.5 = (bf16[64,3712]{1,0:T(8,128)(2,1)S(1)}, bf16[64,3712]{1,0:T(8,128)(2,1)S(1)}, u32[]{:S(2)}, u32[]{:S(2)}) collective-permute-start(bf16[64,3712]{1,0:T(8,128)(2,1)S(1)} %collective-permute-done.1.refs_0_), channel_id=1, source_target_pairs={{0,8},{8,0},{1,9},{9,1},{2,10},{10,2},{3,11},{11,3},{4,12},{12,4},... | collective-permute-start | bytes 1425416 | tf_op jit(solution)/shard_map/ppermute | solution.py:138
  20.6 14.6 %collective-permute-start.6 = (bf16[64,3712]{1,0:T(8,128)(2,1)S(1)}, bf16[64,3712]{1,0:T(8,128)(2,1)S(1)}, u32[]{:S(2)}, u32[]{:S(2)}) collective-permute-start(bf16[64,3712]{1,0:T(8,128)(2,1)S(1)} %collective-permute-done.1.refs_0_), channel_id=1, source_target_pairs={{0,2},{1,3},{2,4},{3,5},{4,6},{5,7},{6,0},{7,1},{8,10},{9,11},{10,... | collective-permute-start | bytes 1425416 | tf_op jit(solution)/shard_map/ppermute | solution.py:144
  21.6 13.6 %collective-permute-start.7 = (bf16[64,3712]{1,0:T(8,128)(2,1)S(1)}, bf16[64,3712]{1,0:T(8,128)(2,1)S(1)}, u32[]{:S(2)}, u32[]{:S(2)}) collective-permute-start(bf16[64,3712]{1,0:T(8,128)(2,1)S(1)} %collective-permute-done.1.refs_0_), channel_id=1, source_target_pairs={{0,1},{1,0},{2,3},{3,2},{4,5},{5,4},{6,7},{7,6},{8,9},{9,8},{10,11... | collective-permute-start | bytes 1425416 | tf_op jit(solution)/shard_map/ppermute | solution.py:141
  35.2 2.5 %collective-permute-start.10 = (bf16[64,3712]{1,0:T(8,128)(2,1)S(1)}, bf16[64,3712]{1,0:T(8,128)(2,1)S(1)}, u32[]{:S(2)}, u32[]{:S(2)}) collective-permute-start(bf16[64,3712]{1,0:T(8,128)(2,1)S(1)} %collective-permute-done.7.refs_2_), channel_id=1, source_target_pairs={{0,8},{8,0},{1,9},{9,1},{2,10},{10,2},{3,11},{11,3},{4,12},{12,4},... | collective-permute-start | bytes 1425416 | tf_op jit(solution)/shard_map/ppermute | solution.py:138
  35.2 8.5 %collective-permute-start.11 = (bf16[64,3712]{1,0:T(8,128)(2,1)S(1)}, bf16[64,3712]{1,0:T(8,128)(2,1)S(1)}, u32[]{:S(2)}, u32[]{:S(2)}) collective-permute-start(bf16[64,3712]{1,0:T(8,128)(2,1)S(1)} %collective-permute-done.6.refs_0_), channel_id=1, source_target_pairs={{0,8},{8,0},{1,9},{9,1},{2,10},{10,2},{3,11},{11,3},{4,12},{12,4},... | collective-permute-start | bytes 1425416 | tf_op jit(solution)/shard_map/ppermute | solution.py:138
  35.7 14.6 %collective-permute-start.12 = (bf16[64,3712]{1,0:T(8,128)(2,1)S(1)}, bf16[64,3712]{1,0:T(8,128)(2,1)S(1)}, u32[]{:S(2)}, u32[]{:S(2)}) collective-permute-start(bf16[64,3712]{1,0:T(8,128)(2,1)S(1)} %collective-permute-done.6.refs_0_), channel_id=1, source_target_pairs={{0,2},{1,3},{2,4},{3,5},{4,6},{5,7},{6,0},{7,1},{8,10},{9,11},{10,... | collective-permute-start | bytes 1425416 | tf_op jit(solution)/shard_map/ppermute | solution.py:144
  36.2 14.1 %collective-permute-start.13 = (bf16[64,3712]{1,0:T(8,128)(2,1)S(1)}, bf16[64,3712]{1,0:T(8,128)(2,1)S(1)}, u32[]{:S(2)}, u32[]{:S(2)}) collective-permute-start(bf16[64,3712]{1,0:T(8,128)(2,1)S(1)} %collective-permute-done.6.refs_0_), channel_id=1, source_target_pairs={{0,1},{1,0},{2,3},{3,2},{4,5},{5,4},{6,7},{7,6},{8,9},{9,8},{10,11... | collective-permute-start | bytes 1425416 | tf_op jit(solution)/shard_map/ppermute | solution.py:141
  43.6 7.2 %collective-permute-start.14 = (bf16[64,3584]{1,0:T(8,128)(2,1)S(1)}, bf16[64,3584]{1,0:T(8,128)(2,1)S(1)}, u32[]{:S(2)}, u32[]{:S(2)}) collective-permute-start(bf16[64,3584]{1,0:T(8,128)(2,1)S(1)} %get-tuple-element.66), channel_id=1, source_target_pairs={{0,8},{8,0},{1,9},{9,1},{2,10},{10,2},{3,11},{11,3},{4,12},{12,4},... | collective-permute-start | bytes 1376264 | tf_op jit(solution)/shard_map/ppermute | solution.py:138
  50.3 2.2 %collective-permute-start.16 = (bf16[64,3712]{1,0:T(8,128)(2,1)S(1)}, bf16[64,3712]{1,0:T(8,128)(2,1)S(1)}, u32[]{:S(2)}, u32[]{:S(2)}) collective-permute-start(bf16[64,3712]{1,0:T(8,128)(2,1)S(1)} %collective-permute-done.13.refs_2_), channel_id=1, source_target_pairs={{0,8},{8,0},{1,9},{9,1},{2,10},{10,2},{3,11},{11,3},{4,12},{12,4},... | collective-permute-start | bytes 1425416 | tf_op jit(solution)/shard_map/ppermute | solution.py:138
  50.3 15.1 %collective-permute-start.18 = (bf16[64,3712]{1,0:T(8,128)(2,1)S(1)}, bf16[64,3712]{1,0:T(8,128)(2,1)S(1)}, u32[]{:S(2)}, u32[]{:S(2)}) collective-permute-start(bf16[64,3712]{1,0:T(8,128)(2,1)S(1)} %collective-permute-done.13.refs_2_), channel_id=1, source_target_pairs={{0,2},{1,3},{2,4},{3,5},{4,6},{5,7},{6,0},{7,1},{8,10},{9,11},{10,... | collective-permute-start | bytes 1425416 | tf_op jit(solution)/shard_map/ppermute | solution.py:144
  50.3 8.7 %collective-permute-start.17 = (bf16[64,3712]{1,0:T(8,128)(2,1)S(1)}, bf16[64,3712]{1,0:T(8,128)(2,1)S(1)}, u32[]{:S(2)}, u32[]{:S(2)}) collective-permute-start(bf16[64,3712]{1,0:T(8,128)(2,1)S(1)} %collective-permute-done.12.refs_0_), channel_id=1, source_target_pairs={{0,8},{8,0},{1,9},{9,1},{2,10},{10,2},{3,11},{11,3},{4,12},{12,4},... | collective-permute-start | bytes 1425416 | tf_op jit(solution)/shard_map/ppermute | solution.py:138
  50.9 14.5 %collective-permute-start.15 = (bf16[64,3584]{1,0:T(8,128)(2,1)S(1)}, bf16[64,3584]{1,0:T(8,128)(2,1)S(1)}, u32[]{:S(2)}, u32[]{:S(2)}) collective-permute-start(bf16[64,3584]{1,0:T(8,128)(2,1)S(1)} %add_convert_fusion.6), channel_id=1, source_target_pairs={{0,1},{1,0},{2,3},{3,2},{4,5},{5,4},{6,7},{7,6},{8,9},{9,8},{10,11... | collective-permute-start | bytes 1376264 | tf_op jit(solution)/shard_map/ppermute | solution.py:141
  52.5 12.9 %collective-permute-start.23 = (bf16[64,3584]{1,0:T(8,128)(2,1)S(1)}, bf16[64,3584]{1,0:T(8,128)(2,1)S(1)}, u32[]{:S(2)}, u32[]{:S(2)}) collective-permute-start(bf16[64,3584]{1,0:T(8,128)(2,1)S(1)} %get-tuple-element.77), channel_id=1, source_target_pairs={{0,8},{8,0},{1,9},{9,1},{2,10},{10,2},{3,11},{11,3},{4,12},{12,4},... | collective-permute-start | bytes 1376264 | tf_op jit(solution)/shard_map/ppermute | solution.py:138
  58.4 9.2 %copy-start.3 = (s32[8]{0:T(128)S(1)}, s32[8]{0:T(128)}, u32[]{:S(2)}) copy-start(s32[8]{0:T(128)} %param.17) | copy-start | bytes 100
  58.4 7.3 %collective-permute-start.21 = (bf16[64,3584]{1,0:T(8,128)(2,1)S(1)}, bf16[64,3584]{1,0:T(8,128)(2,1)S(1)}, u32[]{:S(2)}, u32[]{:S(2)}) collective-permute-start(bf16[64,3584]{1,0:T(8,128)(2,1)S(1)} %get-tuple-element.75), channel_id=1, source_target_pairs={{0,8},{8,0},{1,9},{9,1},{2,10},{10,2},{3,11},{11,3},{4,12},{12,4},... | collective-permute-start | bytes 1376264 | tf_op jit(solution)/shard_map/ppermute | solution.py:138
  65.5 14.0 %collective-permute-start.24 = (bf16[64,3584]{1,0:T(8,128)(2,1)S(1)}, bf16[64,3584]{1,0:T(8,128)(2,1)S(1)}, u32[]{:S(2)}, u32[]{:S(2)}) collective-permute-start(bf16[64,3584]{1,0:T(8,128)(2,1)S(1)} %add_convert_fusion.4), channel_id=1, source_target_pairs={{0,2},{1,3},{2,4},{3,5},{4,6},{5,7},{6,0},{7,1},{8,10},{9,11},{10,... | collective-permute-start | bytes 1376264 | tf_op jit(solution)/shard_map/ppermute | solution.py:144
  65.6 2.4 %collective-permute-start.19 = (bf16[64,3712]{1,0:T(8,128)(2,1)S(1)}, bf16[64,3712]{1,0:T(8,128)(2,1)S(1)}, u32[]{:S(2)}, u32[]{:S(2)}) collective-permute-start(bf16[64,3712]{1,0:T(8,128)(2,1)S(1)} %collective-permute-done.18.refs_2_), channel_id=1, source_target_pairs={{0,8},{8,0},{1,9},{9,1},{2,10},{10,2},{3,11},{11,3},{4,12},{12,4},... | collective-permute-start | bytes 1425416 | tf_op jit(solution)/shard_map/ppermute | solution.py:138
  65.8 13.7 %collective-permute-start.22 = (bf16[64,3584]{1,0:T(8,128)(2,1)S(1)}, bf16[64,3584]{1,0:T(8,128)(2,1)S(1)}, u32[]{:S(2)}, u32[]{:S(2)}) collective-permute-start(bf16[64,3584]{1,0:T(8,128)(2,1)S(1)} %add_convert_fusion.5), channel_id=1, source_target_pairs={{0,1},{1,0},{2,3},{3,2},{4,5},{5,4},{6,7},{7,6},{8,9},{9,8},{10,11... | collective-permute-start | bytes 1376264 | tf_op jit(solution)/shard_map/ppermute | solution.py:141
  67.4 12.2 %collective-permute-start.27 = (bf16[64,3584]{1,0:T(8,128)(2,1)S(1)}, bf16[64,3584]{1,0:T(8,128)(2,1)S(1)}, u32[]{:S(2)}, u32[]{:S(2)}) collective-permute-start(bf16[64,3584]{1,0:T(8,128)(2,1)S(1)} %get-tuple-element.83), channel_id=1, source_target_pairs={{0,8},{8,0},{1,9},{9,1},{2,10},{10,2},{3,11},{11,3},{4,12},{12,4},... | collective-permute-start | bytes 1376264 | tf_op jit(solution)/shard_map/ppermute | solution.py:138
  67.7 15.4 %collective-permute-start.8 = (bf16[64,3584]{1,0:T(8,128)(2,1)S(1)}, bf16[64,3584]{1,0:T(8,128)(2,1)S(1)}, u32[]{:S(2)}, u32[]{:S(2)}) collective-permute-start(bf16[64,3584]{1,0:T(8,128)(2,1)S(1)} %get-tuple-element.59), channel_id=1, source_target_pairs={{0,8},{8,0},{1,9},{9,1},{2,10},{10,2},{3,11},{11,3},{4,12},{12,4},... | collective-permute-start | bytes 1376264 | tf_op jit(solution)/shard_map/ppermute | solution.py:138
  68.0 41.8 %collective-permute-start.4 = (bf16[64,3584]{1,0:T(8,128)(2,1)S(1)}, bf16[64,3584]{1,0:T(8,128)(2,1)S(1)}, u32[]{:S(2)}, u32[]{:S(2)}) collective-permute-start(bf16[64,3584]{1,0:T(8,128)(2,1)S(1)} %get-tuple-element.55), channel_id=1, source_target_pairs={{0,8},{8,0},{1,9},{9,1},{2,10},{10,2},{3,11},{11,3},{4,12},{12,4},... | collective-permute-start | bytes 1376264 | tf_op jit(solution)/shard_map/ppermute | solution.py:138
  79.5 1.8 %collective-permute-start.25 = (bf16[64,3584]{1,0:T(8,128)(2,1)S(1)}, bf16[64,3584]{1,0:T(8,128)(2,1)S(1)}, u32[]{:S(2)}, u32[]{:S(2)}) collective-permute-start(bf16[64,3584]{1,0:T(8,128)(2,1)S(1)} %get-tuple-element.81), channel_id=1, source_target_pairs={{0,8},{8,0},{1,9},{9,1},{2,10},{10,2},{3,11},{11,3},{4,12},{12,4},... | collective-permute-start | bytes 1376264 | tf_op jit(solution)/shard_map/ppermute | solution.py:138
  79.8 14.8 %collective-permute-start.28 = (bf16[64,3584]{1,0:T(8,128)(2,1)S(1)}, bf16[64,3584]{1,0:T(8,128)(2,1)S(1)}, u32[]{:S(2)}, u32[]{:S(2)}) collective-permute-start(bf16[64,3584]{1,0:T(8,128)(2,1)S(1)} %add_convert_fusion.2), channel_id=1, source_target_pairs={{0,2},{1,3},{2,4},{3,5},{4,6},{5,7},{6,0},{7,1},{8,10},{9,11},{10,... | collective-permute-start | bytes 1376264 | tf_op jit(solution)/shard_map/ppermute | solution.py:144
  79.9 16.8 %copy-start.2 = (bf16[8,256,576]{1,2,0:T(8,128)(2,1)S(1)}, bf16[8,256,576]{1,2,0:T(8,128)(2,1)}, u32[]{:S(2)}) copy-start(bf16[8,256,576]{1,2,0:T(8,128)(2,1)} %param.16) | copy-start | bytes 7077892
  79.9 15.0 %collective-permute-start.20 = (bf16[64,3584]{1,0:T(8,128)(2,1)S(1)}, bf16[64,3584]{1,0:T(8,128)(2,1)S(1)}, u32[]{:S(2)}, u32[]{:S(2)}) collective-permute-start(bf16[64,3584]{1,0:T(8,128)(2,1)S(1)} %get-tuple-element.73), channel_id=1, source_target_pairs={{0,8},{8,0},{1,9},{9,1},{2,10},{10,2},{3,11},{11,3},{4,12},{12,4},... | collective-permute-start | bytes 1376264 | tf_op jit(solution)/shard_map/ppermute | solution.py:138
  81.5 13.4 %collective-permute-start.26 = (bf16[64,3584]{1,0:T(8,128)(2,1)S(1)}, bf16[64,3584]{1,0:T(8,128)(2,1)S(1)}, u32[]{:S(2)}, u32[]{:S(2)}) collective-permute-start(bf16[64,3584]{1,0:T(8,128)(2,1)S(1)} %add_convert_fusion.3), channel_id=1, source_target_pairs={{0,1},{1,0},{2,3},{3,2},{4,5},{5,4},{6,7},{7,6},{8,9},{9,8},{10,11... | collective-permute-start | bytes 1376264 | tf_op jit(solution)/shard_map/ppermute | solution.py:141
  83.2 20.8 %collective-permute-start.9 = (bf16[64,3584]{1,0:T(8,128)(2,1)S(1)}, bf16[64,3584]{1,0:T(8,128)(2,1)S(1)}, u32[]{:S(2)}, u32[]{:S(2)}) collective-permute-start(bf16[64,3584]{1,0:T(8,128)(2,1)S(1)} %add_convert_fusion.7), channel_id=1, source_target_pairs={{0,1},{1,0},{2,3},{3,2},{4,5},{5,4},{6,7},{7,6},{8,9},{9,8},{10,11... | collective-permute-start | bytes 1376264 | tf_op jit(solution)/shard_map/ppermute | solution.py:141
  95.9 13.9 %collective-permute-start.29 = (bf16[64,3584]{1,0:T(8,128)(2,1)}, bf16[64,3584]{1,0:T(8,128)(2,1)}, u32[]{:S(2)}, u32[]{:S(2)}) collective-permute-start(bf16[64,3584]{1,0:T(8,128)(2,1)} %add_convert_fusion.1), channel_id=1, source_target_pairs={{0,2},{1,3},{2,4},{3,5},{4,6},{5,7},{6,0},{7,1},{8,10},{9,11},{10,... | collective-permute-start | bytes 1376264 | tf_op jit(solution)/shard_map/ppermute | solution.py:144

commit v4 on v3

--- a/solution.py
+++ b/solution.py
@@ -134,6 +134,11 @@
     steps = rank_count // PAIR
     f32, bf16 = jnp.float32, jnp.bfloat16
 
+    line = list(range(0, steps, 2)) + list(range(1, steps, 2))[::-1]
+    hops = [
+        (line[i] * PAIR + j, line[(i + 1) % steps] * PAIR + j) for i in range(steps) for j in range(PAIR)
+    ]
+
     def core(value):
         return lax.ppermute(value, "node", [(i, 1 - i) for i in range(node_count)])
 
@@ -141,7 +146,7 @@
         return lax.ppermute(value, "rank", [(i, i ^ 1) for i in range(rank_count)])
 
     def ring(value):
-        return lax.ppermute(value, "rank", [(i, (i + PAIR) % rank_count) for i in range(rank_count)])
+        return lax.ppermute(value, "rank", hops)
 
     weights = load_inside(w_gate[0], w_up[0], w_down[0])
 

time: 112 us -> 108 us (0.964)
  waiting for transfers between devices: 50.4 us -> 41 us
  starting transfers between devices: 19.1 us -> 24.9 us
    ppermute x7, waiting for transfers between devices: 46.1 us -> 28.4 us  [ring(): return lax.ppermute(value, 'rank', hops)]
    ppermute x7, waiting for transfers between devices: 3.34 us -> 12.6 us  [pair(): return lax.ppermute(value, 'rank', [(i, i ^ 1) for i in range(rank_count)])]
    ppermute x7, starting transfers between devices: 5.16 us -> 11.6 us  [ring(): return lax.ppermute(value, 'rank', hops)]
  transfers between devices with their start and end apart: 30 -> 30, of which waited for: 10 -> 14; matrix products, arithmetic and copies ran while one was open for 5% -> 6% of each run, Pallas kernels for 28% -> 28%
where the time goes in v4:
time: 108 us
  waiting for transfers between devices  41 us (38%)
  Pallas kernels  33.4 us (31%)
  starting transfers between devices  24.9 us (23%)
  other arithmetic  4.13 us (4%)
  matrix products  3.94 us (4%)
    ppermute x7, waiting for transfers between devices, ring(): return lax.ppermute(value, 'rank', hops)  28.4 us
    pallas_call x4, Pallas kernels, run_expert(): pl.pallas_call(lambda *refs: expert_kernel(experts, *refs), out_shape=[ja...  23.5 us
    ppermute x7, waiting for transfers between devices, pair(): return lax.ppermute(value, 'rank', [(i, i ^ 1) for i in range(rank_count)])  12.6 us
    ppermute x7, starting transfers between devices, ring(): return lax.ppermute(value, 'rank', hops)  11.6 us
    ppermute x7, starting transfers between devices, pair(): return lax.ppermute(value, 'rank', [(i, i ^ 1) for i in range(rank_count)])  9.88 us
    pallas_call x1, Pallas kernels, load_inside(): pl.pallas_call(load_kernel, out_shape=[jax.ShapeDtypeStruct(a.shape, a.dt...  7.34 us
    convert_element_type x4, other arithmetic, onward(): return value.astype(bf16)  3.4 us
    dot_general x1, matrix products, attend(): jnp.einsum('bhl,blc->bhc', softmax_weights, latent_values, preferred_elem...  3.4 us
  transfers between devices with their start and end apart: 30, of which 14 were waited for; matrix products, arithmetic and copies ran while one was open for 6% of the time, Pallas kernels for 28%

profile of v4, /device:TPU:0, one launch (start us, length us, event | category | flops | bytes accessed | tf_op | source)
XLA Modules:
  0.0 108.2 jit_solution(8041185700644228726)
XLA Ops:
  0.6 0.0 copy-start
  0.6 2.6 %shard_map.104.refs_0_ = bf16[64,3712]{1,0:T(8,128)(2,1)} custom-call(bf16[64,3584]{1,0:T(8,128)(2,1)} %refs_0_.1, s32[8,64]{1,0:T(8,128)} %bitcast.12, f32[8,64]{1,0:T(8,128)} %bitcast.13), custom_call_target="tpu_custom_call" | custom-call | bytes 917504 | tf_op jit(solution)/shard_map/pallas_call | solution.py:57
  3.2 0.5 collective-permute-start
  3.7 3.6 %collective-permute-start.1 = (bf16[64,3712]{1,0:T(8,128)(2,1)}, bf16[64,3712]{1,0:T(8,128)(2,1)S(1)}, u32[]{:S(2)}, u32[]{:S(2)}) collective-permute-start(bf16[64,3712]{1,0:T(8,128)(2,1)} %shard_map.104.refs_0_), channel_id=1, source_target_pairs={{0,4},{1,5},{4,6},{5,7},{6,2},{7,3},{2,0},{3,1},{8,12},{9,13},{12,... | collective-permute-start | bytes 1425416 | tf_op jit(solution)/shard_map/ppermute | solution.py:149
  7.4 1.5 %collective-permute-start.2 = (bf16[64,3712]{1,0:T(8,128)(2,1)}, bf16[64,3712]{1,0:T(8,128)(2,1)S(1)}, u32[]{:S(2)}, u32[]{:S(2)}) collective-permute-start(bf16[64,3712]{1,0:T(8,128)(2,1)} %shard_map.104.refs_0_), channel_id=1, source_target_pairs={{0,1},{1,0},{2,3},{3,2},{4,5},{5,4},{6,7},{7,6},{8,9},{9,8},{10,11... | collective-permute-start | bytes 1425416 | tf_op jit(solution)/shard_map/ppermute | solution.py:146
  8.9 7.3 %shard_map.105 = (bf16[3584,1024]{1,0:T(8,128)(2,1)S(1)}, bf16[3584,1024]{1,0:T(8,128)(2,1)S(1)}, bf16[1024,3584]{1,0:T(8,128)(2,1)S(1)}) custom-call(bf16[3584,1024]{1,0:T(8,128)(2,1)} %bitcast.9, bf16[3584,1024]{1,0:T(8,128)(2,1)} %bitcast.10, bf16[1024,3584]{1,0:T(8,128)(2,1)} %bitcast.11), custom_call_target="tpu_custom_call" | custom-call | bytes 22020096 | tf_op jit(solution)/shard_map/pallas_call | solution.py:101
  16.3 0.0 collective-permute-done.refs_1_
  16.3 2.2 %collective-permute-done.1.refs_0_ = bf16[64,3712]{1,0:T(8,128)(2,1)S(1)} collective-permute-done((bf16[64,3712]{1,0:T(8,128)(2,1)}, bf16[64,3712]{1,0:T(8,128)(2,1)S(1)}, u32[]{:S(2)}, u32[]{:S(2)}) %collective-permute-start.1) | collective-permute-done | bytes 475168 | tf_op jit(solution)/shard_map/ppermute | solution.py:149
  18.4 2.1 %collective-permute-done.2.refs_2_ = bf16[64,3712]{1,0:T(8,128)(2,1)S(1)} collective-permute-done((bf16[64,3712]{1,0:T(8,128)(2,1)}, bf16[64,3712]{1,0:T(8,128)(2,1)S(1)}, u32[]{:S(2)}, u32[]{:S(2)}) %collective-permute-start.2) | collective-permute-done | bytes 475168 | tf_op jit(solution)/shard_map/ppermute | solution.py:146
  20.5 0.5 collective-permute-start.5
  21.1 1.6 %collective-permute-start.6 = (bf16[64,3712]{1,0:T(8,128)(2,1)S(1)}, bf16[64,3712]{1,0:T(8,128)(2,1)S(1)}, u32[]{:S(2)}, u32[]{:S(2)}) collective-permute-start(bf16[64,3712]{1,0:T(8,128)(2,1)S(1)} %collective-permute-done.1.refs_0_), channel_id=1, source_target_pairs={{0,4},{1,5},{4,6},{5,7},{6,2},{7,3},{2,0},{3,1},{8,12},{9,13},{12,... | collective-permute-start | bytes 1425416 | tf_op jit(solution)/shard_map/ppermute | solution.py:149
  22.6 1.5 %collective-permute-start.7 = (bf16[64,3712]{1,0:T(8,128)(2,1)S(1)}, bf16[64,3712]{1,0:T(8,128)(2,1)S(1)}, u32[]{:S(2)}, u32[]{:S(2)}) collective-permute-start(bf16[64,3712]{1,0:T(8,128)(2,1)S(1)} %collective-permute-done.1.refs_0_), channel_id=1, source_target_pairs={{0,1},{1,0},{2,3},{3,2},{4,5},{5,4},{6,7},{7,6},{8,9},{9,8},{10,11... | collective-permute-start | bytes 1425416 | tf_op jit(solution)/shard_map/ppermute | solution.py:146
  24.1 0.0 collective-permute-done.3.refs_3_
  24.2 5.9 %shard_map.106 = (bf16[64,3584]{1,0:T(8,128)(2,1)S(1)}, bf16[64,3584]{1,0:T(8,128)(2,1)S(1)}, bf16[64,3584]{1,0:T(8,128)(2,1)S(1)}, bf16[64,3584]{1,0:T(8,128)(2,1)S(1)}) custom-call(bf16[64,3712]{1,0:T(8,128)(2,1)S(1)} %copy-done.1, bf16[64,3712]{1,0:T(8,128)(2,1)S(1)} %collective-permute-done.refs_1_, bf16[64,3712]{1,0:T(8,128)(2,1)S(1)} %collective-permute-done.2.refs_2_, ...), custom_call_target="tpu_custom_call" | custom-call | tf_op jit(solution)/shard_map/pallas_call | solution.py:118
  30.0 3.8 %collective-permute-done.6.refs_0_ = bf16[64,3712]{1,0:T(8,128)(2,1)S(1)} collective-permute-done((bf16[64,3712]{1,0:T(8,128)(2,1)S(1)}, bf16[64,3712]{1,0:T(8,128)(2,1)S(1)}, u32[]{:S(2)}, u32[]{:S(2)}) %collective-permute-start.6) | collective-permute-done | bytes 475168 | tf_op jit(solution)/shard_map/ppermute | solution.py:149
  33.8 1.3 %collective-permute-done.7.refs_2_ = bf16[64,3712]{1,0:T(8,128)(2,1)S(1)} collective-permute-done((bf16[64,3712]{1,0:T(8,128)(2,1)S(1)}, bf16[64,3712]{1,0:T(8,128)(2,1)S(1)}, u32[]{:S(2)}, u32[]{:S(2)}) %collective-permute-start.7) | collective-permute-done | bytes 475168 | tf_op jit(solution)/shard_map/ppermute | solution.py:146
  35.1 0.5 collective-permute-start.11
  35.6 1.2 %collective-permute-start.12 = (bf16[64,3712]{1,0:T(8,128)(2,1)S(1)}, bf16[64,3712]{1,0:T(8,128)(2,1)S(1)}, u32[]{:S(2)}, u32[]{:S(2)}) collective-permute-start(bf16[64,3712]{1,0:T(8,128)(2,1)S(1)} %collective-permute-done.6.refs_0_), channel_id=1, source_target_pairs={{0,4},{1,5},{4,6},{5,7},{6,2},{7,3},{2,0},{3,1},{8,12},{9,13},{12,... | collective-permute-start | bytes 1425416 | tf_op jit(solution)/shard_map/ppermute | solution.py:149
  36.8 1.5 %collective-permute-start.13 = (bf16[64,3712]{1,0:T(8,128)(2,1)S(1)}, bf16[64,3712]{1,0:T(8,128)(2,1)S(1)}, u32[]{:S(2)}, u32[]{:S(2)}) collective-permute-start(bf16[64,3712]{1,0:T(8,128)(2,1)S(1)} %collective-permute-done.6.refs_0_), channel_id=1, source_target_pairs={{0,1},{1,0},{2,3},{3,2},{4,5},{5,4},{6,7},{7,6},{8,9},{9,8},{10,11... | collective-permute-start | bytes 1425416 | tf_op jit(solution)/shard_map/ppermute | solution.py:146
  38.3 0.0 collective-permute-done.10.refs_3_
  38.3 5.9 %shard_map.107 = (bf16[64,3584]{1,0:T(8,128)(2,1)S(1)}, bf16[64,3584]{1,0:T(8,128)(2,1)S(1)}, bf16[64,3584]{1,0:T(8,128)(2,1)S(1)}, bf16[64,3584]{1,0:T(8,128)(2,1)S(1)}) custom-call(bf16[64,3712]{1,0:T(8,128)(2,1)S(1)} %collective-permute-done.1.refs_0_, bf16[64,3712]{1,0:T(8,128)(2,1)S(1)} %collective-permute-done.5.refs_1_, ...), custom_call_target="tpu_custom_call" | custom-call | tf_op jit(solution)/shard_map/pallas_call | solution.py:118
  44.2 0.1 collective-permute-start.14
  44.3 0.0 collective-permute-done.11.refs_1_
  44.3 4.1 %collective-permute-done.12.refs_0_ = bf16[64,3712]{1,0:T(8,128)(2,1)S(1)} collective-permute-done((bf16[64,3712]{1,0:T(8,128)(2,1)S(1)}, bf16[64,3712]{1,0:T(8,128)(2,1)S(1)}, u32[]{:S(2)}, u32[]{:S(2)}) %collective-permute-start.12) | collective-permute-done | bytes 475168 | tf_op jit(solution)/shard_map/ppermute | solution.py:149
  48.4 0.9 collective-permute-done.13.refs_2_
  49.3 1.2 %collective-permute-start.18 = (bf16[64,3712]{1,0:T(8,128)(2,1)S(1)}, bf16[64,3712]{1,0:T(8,128)(2,1)S(1)}, u32[]{:S(2)}, u32[]{:S(2)}) collective-permute-start(bf16[64,3712]{1,0:T(8,128)(2,1)S(1)} %collective-permute-done.13.refs_2_), channel_id=1, source_target_pairs={{0,4},{1,5},{4,6},{5,7},{6,2},{7,3},{2,0},{3,1},{8,12},{9,13},{12,... | collective-permute-start | bytes 1425416 | tf_op jit(solution)/shard_map/ppermute | solution.py:149
  50.5 0.2 collective-permute-start.17
  50.7 0.1 add_convert_fusion.6
  50.8 1.6 %collective-permute-start.15 = (bf16[64,3584]{1,0:T(8,128)(2,1)S(1)}, bf16[64,3584]{1,0:T(8,128)(2,1)S(1)}, u32[]{:S(2)}, u32[]{:S(2)}) collective-permute-start(bf16[64,3584]{1,0:T(8,128)(2,1)S(1)} %add_convert_fusion.6), channel_id=1, source_target_pairs={{0,1},{1,0},{2,3},{3,2},{4,5},{5,4},{6,7},{7,6},{8,9},{9,8},{10,11... | collective-permute-start | bytes 1376264 | tf_op jit(solution)/shard_map/ppermute | solution.py:146
  52.4 0.0 collective-permute-start.23
  52.4 0.0 collective-permute-done.16.refs_3_
  52.4 5.9 %shard_map.108 = (bf16[64,3584]{1,0:T(8,128)(2,1)S(1)}, bf16[64,3584]{1,0:T(8,128)(2,1)S(1)}, bf16[64,3584]{1,0:T(8,128)(2,1)S(1)}, bf16[64,3584]{1,0:T(8,128)(2,1)S(1)}) custom-call(bf16[64,3712]{1,0:T(8,128)(2,1)S(1)} %collective-permute-done.6.refs_0_, bf16[64,3712]{1,0:T(8,128)(2,1)S(1)} %collective-permute-done.11.refs_1_, ...), custom_call_target="tpu_custom_call" | custom-call | tf_op jit(solution)/shard_map/pallas_call | solution.py:118
  58.3 0.0 copy-start.3
  58.3 0.6 collective-permute-start.21
  58.9 3.7 %collective-permute-done.18.refs_2_ = bf16[64,3712]{1,0:T(8,128)(2,1)S(1)} collective-permute-done((bf16[64,3712]{1,0:T(8,128)(2,1)S(1)}, bf16[64,3712]{1,0:T(8,128)(2,1)S(1)}, u32[]{:S(2)}, u32[]{:S(2)}) %collective-permute-start.18) | collective-permute-done | bytes 475168 | tf_op jit(solution)/shard_map/ppermute | solution.py:149
  62.6 1.0 collective-permute-done.15
  63.6 0.2 add_convert_fusion.4
  63.8 1.1 %collective-permute-start.24 = (bf16[64,3584]{1,0:T(8,128)(2,1)S(1)}, bf16[64,3584]{1,0:T(8,128)(2,1)S(1)}, u32[]{:S(2)}, u32[]{:S(2)}) collective-permute-start(bf16[64,3584]{1,0:T(8,128)(2,1)S(1)} %add_convert_fusion.4), channel_id=1, source_target_pairs={{0,4},{1,5},{4,6},{5,7},{6,2},{7,3},{2,0},{3,1},{8,12},{9,13},{12,... | collective-permute-start | bytes 1376264 | tf_op jit(solution)/shard_map/ppermute | solution.py:149
  64.9 0.1 add_convert_fusion.5
  65.0 1.6 %collective-permute-start.22 = (bf16[64,3584]{1,0:T(8,128)(2,1)S(1)}, bf16[64,3584]{1,0:T(8,128)(2,1)S(1)}, u32[]{:S(2)}, u32[]{:S(2)}) collective-permute-start(bf16[64,3584]{1,0:T(8,128)(2,1)S(1)} %add_convert_fusion.5), channel_id=1, source_target_pairs={{0,1},{1,0},{2,3},{3,2},{4,5},{5,4},{6,7},{7,6},{8,9},{9,8},{10,11... | collective-permute-start | bytes 1376264 | tf_op jit(solution)/shard_map/ppermute | solution.py:146
  66.6 0.2 collective-permute-start.27
  66.9 0.1 iota_compare_fusion
  66.9 0.3 collective-permute-start.8
  67.2 0.2 collective-permute-start.4
  67.4 5.9 %shard_map.109 = (bf16[64,3584]{1,0:T(8,128)(2,1)S(1)}, bf16[64,3584]{1,0:T(8,128)(2,1)S(1)}, bf16[64,3584]{1,0:T(8,128)(2,1)S(1)}, bf16[64,3584]{1,0:T(8,128)(2,1)S(1)}) custom-call(bf16[64,3712]{1,0:T(8,128)(2,1)S(1)} %collective-permute-done.12.refs_0_, bf16[64,3712]{1,0:T(8,128)(2,1)S(1)} %collective-permute-done.17.refs_1_, ...), custom_call_target="tpu_custom_call" | custom-call | tf_op jit(solution)/shard_map/pallas_call | solution.py:118
  73.3 2.4 %collective-permute-done.24 = bf16[64,3584]{1,0:T(8,128)(2,1)S(1)} collective-permute-done((bf16[64,3584]{1,0:T(8,128)(2,1)S(1)}, bf16[64,3584]{1,0:T(8,128)(2,1)S(1)}, u32[]{:S(2)}, u32[]{:S(2)}) %collective-permute-start.24) | collective-permute-done | bytes 458784 | tf_op jit(solution)/shard_map/ppermute | solution.py:149
  75.7 2.3 %collective-permute-done.22 = bf16[64,3584]{1,0:T(8,128)(2,1)S(1)} collective-permute-done((bf16[64,3584]{1,0:T(8,128)(2,1)S(1)}, bf16[64,3584]{1,0:T(8,128)(2,1)S(1)}, u32[]{:S(2)}, u32[]{:S(2)}) %collective-permute-start.22) | collective-permute-done | bytes 458784 | tf_op jit(solution)/shard_map/ppermute | solution.py:146
  78.0 0.2 add_convert_fusion.2
  78.3 1.6 %collective-permute-start.28 = (bf16[64,3584]{1,0:T(8,128)(2,1)S(1)}, bf16[64,3584]{1,0:T(8,128)(2,1)S(1)}, u32[]{:S(2)}, u32[]{:S(2)}) collective-permute-start(bf16[64,3584]{1,0:T(8,128)(2,1)S(1)} %add_convert_fusion.2), channel_id=1, source_target_pairs={{0,4},{1,5},{4,6},{5,7},{6,2},{7,3},{2,0},{3,1},{8,12},{9,13},{12,... | collective-permute-start | bytes 1376264 | tf_op jit(solution)/shard_map/ppermute | solution.py:149
  79.8 0.2 collective-permute-start.20
  80.1 0.1 add_convert_fusion.3
  80.2 1.6 %collective-permute-start.26 = (bf16[64,3584]{1,0:T(8,128)(2,1)S(1)}, bf16[64,3584]{1,0:T(8,128)(2,1)S(1)}, u32[]{:S(2)}, u32[]{:S(2)}) collective-permute-start(bf16[64,3584]{1,0:T(8,128)(2,1)S(1)} %add_convert_fusion.3), channel_id=1, source_target_pairs={{0,1},{1,0},{2,3},{3,2},{4,5},{5,4},{6,7},{7,6},{8,9},{9,8},{10,11... | collective-permute-start | bytes 1376264 | tf_op jit(solution)/shard_map/ppermute | solution.py:146
  81.8 0.1 add_convert_fusion.7
  81.9 0.6 collective-permute-start.9
  82.5 8.8 %collective-permute-done.28 = bf16[64,3584]{1,0:T(8,128)(2,1)S(1)} collective-permute-done((bf16[64,3584]{1,0:T(8,128)(2,1)S(1)}, bf16[64,3584]{1,0:T(8,128)(2,1)S(1)}, u32[]{:S(2)}, u32[]{:S(2)}) %collective-permute-start.28) | collective-permute-done | bytes 458784 | tf_op jit(solution)/shard_map/ppermute | solution.py:149
  91.3 2.3 %collective-permute-done.26 = bf16[64,3584]{1,0:T(8,128)(2,1)S(1)} collective-permute-done((bf16[64,3584]{1,0:T(8,128)(2,1)S(1)}, bf16[64,3584]{1,0:T(8,128)(2,1)S(1)}, u32[]{:S(2)}, u32[]{:S(2)}) %collective-permute-start.26) | collective-permute-done | bytes 458784 | tf_op jit(solution)/shard_map/ppermute | solution.py:146
  93.6 1.0 add_convert_fusion.1
  94.6 1.3 %collective-permute-start.29 = (bf16[64,3584]{1,0:T(8,128)(2,1)}, bf16[64,3584]{1,0:T(8,128)(2,1)}, u32[]{:S(2)}, u32[]{:S(2)}) collective-permute-start(bf16[64,3584]{1,0:T(8,128)(2,1)} %add_convert_fusion.1), channel_id=1, source_target_pairs={{0,4},{1,5},{4,6},{5,7},{6,2},{7,3},{2,0},{3,1},{8,12},{9,13},{12,... | collective-permute-start | bytes 1376264 | tf_op jit(solution)/shard_map/ppermute | solution.py:149
  95.9 0.5 fusion.8
  96.5 0.2 fusion.11
  96.7 3.4 %fusion.3 = bf16[8,64,512]{2,1,0:T(8,128)(2,1)} fusion(bf16[8,256,576]{1,2,0:T(8,128)(2,1)} %param.16, f32[8,64]{1,0:T(8,128)S(1)} %fusion.11, f32[8,64,256]{2,1,0:T(8,128)S(1)} %fusion.8), kind=kOutput, calls=%fused_computation.3 | convolution fusion | flops 134873856 | bytes 3674112 | tf_op jit(solution)/shard_map/bhl,blc->bhc/dot_general | solution.py:28
  100.1 2.7 %collective-permute-done.9 = bf16[64,3584]{1,0:T(8,128)(2,1)S(1)} collective-permute-done((bf16[64,3584]{1,0:T(8,128)(2,1)S(1)}, bf16[64,3584]{1,0:T(8,128)(2,1)S(1)}, u32[]{:S(2)}, u32[]{:S(2)}) %collective-permute-start.9) | collective-permute-done | bytes 458784 | tf_op jit(solution)/shard_map/ppermute | solution.py:146
  102.8 3.4 %collective-permute-done.29 = bf16[64,3584]{1,0:T(8,128)(2,1)} collective-permute-done((bf16[64,3584]{1,0:T(8,128)(2,1)}, bf16[64,3584]{1,0:T(8,128)(2,1)}, u32[]{:S(2)}, u32[]{:S(2)}) %collective-permute-start.29) | collective-permute-done | bytes 458784 | tf_op jit(solution)/shard_map/ppermute | solution.py:149
  106.2 2.0 %add_convert_fusion = bf16[64,3584]{1,0:T(8,128)(2,1)} fusion(bf16[64,3584]{1,0:T(8,128)(2,1)} %collective-permute-done.29, bf16[64,3584]{1,0:T(8,128)(2,1)S(1)} %collective-permute-done.9, bf16[64,3584]{1,0:T(8,128)(2,1)S(1)} %collective-permute-done.4, bf16[64,3584]{1,0:T(8,128)(2,1)S(1)} %get-tuple-element.54), kind=kLoop, calls=%fused_computation.8 | loop fusion | flops 1835008 | bytes 2293760 | tf_op jit(solution)/shard_map/convert_element_type | solution.py:172
  (22 shorter events, 0.1 us)
Async XLA Ops:
  0.6 95.3 %copy-start = (bf16[8,64,576]{2,1,0:T(8,128)(2,1)S(1)}, bf16[8,64,576]{2,1,0:T(8,128)(2,1)}, u32[]{:S(2)}) copy-start(bf16[8,64,576]{2,1,0:T(8,128)(2,1)} %param.15) | copy-start | bytes 1769476
  3.2 13.0 %collective-permute-start = (bf16[64,3712]{1,0:T(8,128)(2,1)}, bf16[64,3712]{1,0:T(8,128)(2,1)S(1)}, u32[]{:S(2)}, u32[]{:S(2)}) collective-permute-start(bf16[64,3712]{1,0:T(8,128)(2,1)} %shard_map.104.refs_0_), channel_id=1, source_target_pairs={{0,8},{8,0},{1,9},{9,1},{2,10},{10,2},{3,11},{11,3},{4,12},{12,4},... | collective-permute-start | bytes 1425416 | tf_op jit(solution)/shard_map/ppermute | solution.py:143
  3.7 14.7 %collective-permute-start.1 = (bf16[64,3712]{1,0:T(8,128)(2,1)}, bf16[64,3712]{1,0:T(8,128)(2,1)S(1)}, u32[]{:S(2)}, u32[]{:S(2)}) collective-permute-start(bf16[64,3712]{1,0:T(8,128)(2,1)} %shard_map.104.refs_0_), channel_id=1, source_target_pairs={{0,4},{1,5},{4,6},{5,7},{6,2},{7,3},{2,0},{3,1},{8,12},{9,13},{12,... | collective-permute-start | bytes 1425416 | tf_op jit(solution)/shard_map/ppermute | solution.py:149
  7.4 13.2 %collective-permute-start.2 = (bf16[64,3712]{1,0:T(8,128)(2,1)}, bf16[64,3712]{1,0:T(8,128)(2,1)S(1)}, u32[]{:S(2)}, u32[]{:S(2)}) collective-permute-start(bf16[64,3712]{1,0:T(8,128)(2,1)} %shard_map.104.refs_0_), channel_id=1, source_target_pairs={{0,1},{1,0},{2,3},{3,2},{4,5},{5,4},{6,7},{7,6},{8,9},{9,8},{10,11... | collective-permute-start | bytes 1425416 | tf_op jit(solution)/shard_map/ppermute | solution.py:146
  8.9 15.2 %copy-start.1 = (bf16[64,3712]{1,0:T(8,128)(2,1)S(1)}, bf16[64,3712]{1,0:T(8,128)(2,1)}, u32[]{:S(2)}) copy-start(bf16[64,3712]{1,0:T(8,128)(2,1)} %shard_map.104.refs_0_) | copy-start | bytes 1425412
  20.5 3.6 %collective-permute-start.3 = (bf16[64,3712]{1,0:T(8,128)(2,1)S(1)}, bf16[64,3712]{1,0:T(8,128)(2,1)S(1)}, u32[]{:S(2)}, u32[]{:S(2)}) collective-permute-start(bf16[64,3712]{1,0:T(8,128)(2,1)S(1)} %collective-permute-done.2.refs_2_), channel_id=1, source_target_pairs={{0,8},{8,0},{1,9},{9,1},{2,10},{10,2},{3,11},{11,3},{4,12},{12,4},... | collective-permute-start | bytes 1425416 | tf_op jit(solution)/shard_map/ppermute | solution.py:143
  20.5 9.5 %collective-permute-start.5 = (bf16[64,3712]{1,0:T(8,128)(2,1)S(1)}, bf16[64,3712]{1,0:T(8,128)(2,1)S(1)}, u32[]{:S(2)}, u32[]{:S(2)}) collective-permute-start(bf16[64,3712]{1,0:T(8,128)(2,1)S(1)} %collective-permute-done.1.refs_0_), channel_id=1, source_target_pairs={{0,8},{8,0},{1,9},{9,1},{2,10},{10,2},{3,11},{11,3},{4,12},{12,4},... | collective-permute-start | bytes 1425416 | tf_op jit(solution)/shard_map/ppermute | solution.py:143
  21.1 12.8 %collective-permute-start.6 = (bf16[64,3712]{1,0:T(8,128)(2,1)S(1)}, bf16[64,3712]{1,0:T(8,128)(2,1)S(1)}, u32[]{:S(2)}, u32[]{:S(2)}) collective-permute-start(bf16[64,3712]{1,0:T(8,128)(2,1)S(1)} %collective-permute-done.1.refs_0_), channel_id=1, source_target_pairs={{0,4},{1,5},{4,6},{5,7},{6,2},{7,3},{2,0},{3,1},{8,12},{9,13},{12,... | collective-permute-start | bytes 1425416 | tf_op jit(solution)/shard_map/ppermute | solution.py:149
  22.6 12.5 %collective-permute-start.7 = (bf16[64,3712]{1,0:T(8,128)(2,1)S(1)}, bf16[64,3712]{1,0:T(8,128)(2,1)S(1)}, u32[]{:S(2)}, u32[]{:S(2)}) collective-permute-start(bf16[64,3712]{1,0:T(8,128)(2,1)S(1)} %collective-permute-done.1.refs_0_), channel_id=1, source_target_pairs={{0,1},{1,0},{2,3},{3,2},{4,5},{5,4},{6,7},{7,6},{8,9},{9,8},{10,11... | collective-permute-start | bytes 1425416 | tf_op jit(solution)/shard_map/ppermute | solution.py:146
  35.1 3.2 %collective-permute-start.10 = (bf16[64,3712]{1,0:T(8,128)(2,1)S(1)}, bf16[64,3712]{1,0:T(8,128)(2,1)S(1)}, u32[]{:S(2)}, u32[]{:S(2)}) collective-permute-start(bf16[64,3712]{1,0:T(8,128)(2,1)S(1)} %collective-permute-done.7.refs_2_), channel_id=1, source_target_pairs={{0,8},{8,0},{1,9},{9,1},{2,10},{10,2},{3,11},{11,3},{4,12},{12,4},... | collective-permute-start | bytes 1425416 | tf_op jit(solution)/shard_map/ppermute | solution.py:143
  35.1 9.2 %collective-permute-start.11 = (bf16[64,3712]{1,0:T(8,128)(2,1)S(1)}, bf16[64,3712]{1,0:T(8,128)(2,1)S(1)}, u32[]{:S(2)}, u32[]{:S(2)}) collective-permute-start(bf16[64,3712]{1,0:T(8,128)(2,1)S(1)} %collective-permute-done.6.refs_0_), channel_id=1, source_target_pairs={{0,8},{8,0},{1,9},{9,1},{2,10},{10,2},{3,11},{11,3},{4,12},{12,4},... | collective-permute-start | bytes 1425416 | tf_op jit(solution)/shard_map/ppermute | solution.py:143
  35.6 12.8 %collective-permute-start.12 = (bf16[64,3712]{1,0:T(8,128)(2,1)S(1)}, bf16[64,3712]{1,0:T(8,128)(2,1)S(1)}, u32[]{:S(2)}, u32[]{:S(2)}) collective-permute-start(bf16[64,3712]{1,0:T(8,128)(2,1)S(1)} %collective-permute-done.6.refs_0_), channel_id=1, source_target_pairs={{0,4},{1,5},{4,6},{5,7},{6,2},{7,3},{2,0},{3,1},{8,12},{9,13},{12,... | collective-permute-start | bytes 1425416 | tf_op jit(solution)/shard_map/ppermute | solution.py:149
  36.8 12.5 %collective-permute-start.13 = (bf16[64,3712]{1,0:T(8,128)(2,1)S(1)}, bf16[64,3712]{1,0:T(8,128)(2,1)S(1)}, u32[]{:S(2)}, u32[]{:S(2)}) collective-permute-start(bf16[64,3712]{1,0:T(8,128)(2,1)S(1)} %collective-permute-done.6.refs_0_), channel_id=1, source_target_pairs={{0,1},{1,0},{2,3},{3,2},{4,5},{5,4},{6,7},{7,6},{8,9},{9,8},{10,11... | collective-permute-start | bytes 1425416 | tf_op jit(solution)/shard_map/ppermute | solution.py:146
  44.2 6.5 %collective-permute-start.14 = (bf16[64,3584]{1,0:T(8,128)(2,1)S(1)}, bf16[64,3584]{1,0:T(8,128)(2,1)S(1)}, u32[]{:S(2)}, u32[]{:S(2)}) collective-permute-start(bf16[64,3584]{1,0:T(8,128)(2,1)S(1)} %get-tuple-element.66), channel_id=1, source_target_pairs={{0,8},{8,0},{1,9},{9,1},{2,10},{10,2},{3,11},{11,3},{4,12},{12,4},... | collective-permute-start | bytes 1376264 | tf_op jit(solution)/shard_map/ppermute | solution.py:143
  49.3 3.1 %collective-permute-start.16 = (bf16[64,3712]{1,0:T(8,128)(2,1)S(1)}, bf16[64,3712]{1,0:T(8,128)(2,1)S(1)}, u32[]{:S(2)}, u32[]{:S(2)}) collective-permute-start(bf16[64,3712]{1,0:T(8,128)(2,1)S(1)} %collective-permute-done.13.refs_2_), channel_id=1, source_target_pairs={{0,8},{8,0},{1,9},{9,1},{2,10},{10,2},{3,11},{11,3},{4,12},{12,4},... | collective-permute-start | bytes 1425416 | tf_op jit(solution)/shard_map/ppermute | solution.py:143
  49.3 13.3 %collective-permute-start.18 = (bf16[64,3712]{1,0:T(8,128)(2,1)S(1)}, bf16[64,3712]{1,0:T(8,128)(2,1)S(1)}, u32[]{:S(2)}, u32[]{:S(2)}) collective-permute-start(bf16[64,3712]{1,0:T(8,128)(2,1)S(1)} %collective-permute-done.13.refs_2_), channel_id=1, source_target_pairs={{0,4},{1,5},{4,6},{5,7},{6,2},{7,3},{2,0},{3,1},{8,12},{9,13},{12,... | collective-permute-start | bytes 1425416 | tf_op jit(solution)/shard_map/ppermute | solution.py:149
  50.5 8.4 %collective-permute-start.17 = (bf16[64,3712]{1,0:T(8,128)(2,1)S(1)}, bf16[64,3712]{1,0:T(8,128)(2,1)S(1)}, u32[]{:S(2)}, u32[]{:S(2)}) collective-permute-start(bf16[64,3712]{1,0:T(8,128)(2,1)S(1)} %collective-permute-done.12.refs_0_), channel_id=1, source_target_pairs={{0,8},{8,0},{1,9},{9,1},{2,10},{10,2},{3,11},{11,3},{4,12},{12,4},... | collective-permute-start | bytes 1425416 | tf_op jit(solution)/shard_map/ppermute | solution.py:143
  50.8 12.8 %collective-permute-start.15 = (bf16[64,3584]{1,0:T(8,128)(2,1)S(1)}, bf16[64,3584]{1,0:T(8,128)(2,1)S(1)}, u32[]{:S(2)}, u32[]{:S(2)}) collective-permute-start(bf16[64,3584]{1,0:T(8,128)(2,1)S(1)} %add_convert_fusion.6), channel_id=1, source_target_pairs={{0,1},{1,0},{2,3},{3,2},{4,5},{5,4},{6,7},{7,6},{8,9},{9,8},{10,11... | collective-permute-start | bytes 1376264 | tf_op jit(solution)/shard_map/ppermute | solution.py:146
  52.4 11.2 %collective-permute-start.23 = (bf16[64,3584]{1,0:T(8,128)(2,1)S(1)}, bf16[64,3584]{1,0:T(8,128)(2,1)S(1)}, u32[]{:S(2)}, u32[]{:S(2)}) collective-permute-start(bf16[64,3584]{1,0:T(8,128)(2,1)S(1)} %get-tuple-element.77), channel_id=1, source_target_pairs={{0,8},{8,0},{1,9},{9,1},{2,10},{10,2},{3,11},{11,3},{4,12},{12,4},... | collective-permute-start | bytes 1376264 | tf_op jit(solution)/shard_map/ppermute | solution.py:143
  58.3 8.5 %copy-start.3 = (s32[8]{0:T(128)S(1)}, s32[8]{0:T(128)}, u32[]{:S(2)}) copy-start(s32[8]{0:T(128)} %param.17) | copy-start | bytes 100
  58.3 6.6 %collective-permute-start.21 = (bf16[64,3584]{1,0:T(8,128)(2,1)S(1)}, bf16[64,3584]{1,0:T(8,128)(2,1)S(1)}, u32[]{:S(2)}, u32[]{:S(2)}) collective-permute-start(bf16[64,3584]{1,0:T(8,128)(2,1)S(1)} %get-tuple-element.75), channel_id=1, source_target_pairs={{0,8},{8,0},{1,9},{9,1},{2,10},{10,2},{3,11},{11,3},{4,12},{12,4},... | collective-permute-start | bytes 1376264 | tf_op jit(solution)/shard_map/ppermute | solution.py:143
  63.8 11.9 %collective-permute-start.24 = (bf16[64,3584]{1,0:T(8,128)(2,1)S(1)}, bf16[64,3584]{1,0:T(8,128)(2,1)S(1)}, u32[]{:S(2)}, u32[]{:S(2)}) collective-permute-start(bf16[64,3584]{1,0:T(8,128)(2,1)S(1)} %add_convert_fusion.4), channel_id=1, source_target_pairs={{0,4},{1,5},{4,6},{5,7},{6,2},{7,3},{2,0},{3,1},{8,12},{9,13},{12,... | collective-permute-start | bytes 1376264 | tf_op jit(solution)/shard_map/ppermute | solution.py:149
  64.9 2.3 %collective-permute-start.19 = (bf16[64,3712]{1,0:T(8,128)(2,1)S(1)}, bf16[64,3712]{1,0:T(8,128)(2,1)S(1)}, u32[]{:S(2)}, u32[]{:S(2)}) collective-permute-start(bf16[64,3712]{1,0:T(8,128)(2,1)S(1)} %collective-permute-done.18.refs_2_), channel_id=1, source_target_pairs={{0,8},{8,0},{1,9},{9,1},{2,10},{10,2},{3,11},{11,3},{4,12},{12,4},... | collective-permute-start | bytes 1425416 | tf_op jit(solution)/shard_map/ppermute | solution.py:143
  65.0 13.0 %collective-permute-start.22 = (bf16[64,3584]{1,0:T(8,128)(2,1)S(1)}, bf16[64,3584]{1,0:T(8,128)(2,1)S(1)}, u32[]{:S(2)}, u32[]{:S(2)}) collective-permute-start(bf16[64,3584]{1,0:T(8,128)(2,1)S(1)} %add_convert_fusion.5), channel_id=1, source_target_pairs={{0,1},{1,0},{2,3},{3,2},{4,5},{5,4},{6,7},{7,6},{8,9},{9,8},{10,11... | collective-permute-start | bytes 1376264 | tf_op jit(solution)/shard_map/ppermute | solution.py:146
  66.6 11.4 %collective-permute-start.27 = (bf16[64,3584]{1,0:T(8,128)(2,1)S(1)}, bf16[64,3584]{1,0:T(8,128)(2,1)S(1)}, u32[]{:S(2)}, u32[]{:S(2)}) collective-permute-start(bf16[64,3584]{1,0:T(8,128)(2,1)S(1)} %get-tuple-element.83), channel_id=1, source_target_pairs={{0,8},{8,0},{1,9},{9,1},{2,10},{10,2},{3,11},{11,3},{4,12},{12,4},... | collective-permute-start | bytes 1376264 | tf_op jit(solution)/shard_map/ppermute | solution.py:143
  66.9 14.8 %collective-permute-start.8 = (bf16[64,3584]{1,0:T(8,128)(2,1)S(1)}, bf16[64,3584]{1,0:T(8,128)(2,1)S(1)}, u32[]{:S(2)}, u32[]{:S(2)}) collective-permute-start(bf16[64,3584]{1,0:T(8,128)(2,1)S(1)} %get-tuple-element.59), channel_id=1, source_target_pairs={{0,8},{8,0},{1,9},{9,1},{2,10},{10,2},{3,11},{11,3},{4,12},{12,4},... | collective-permute-start | bytes 1376264 | tf_op jit(solution)/shard_map/ppermute | solution.py:143
  67.2 39.0 %collective-permute-start.4 = (bf16[64,3584]{1,0:T(8,128)(2,1)S(1)}, bf16[64,3584]{1,0:T(8,128)(2,1)S(1)}, u32[]{:S(2)}, u32[]{:S(2)}) collective-permute-start(bf16[64,3584]{1,0:T(8,128)(2,1)S(1)} %get-tuple-element.55), channel_id=1, source_target_pairs={{0,8},{8,0},{1,9},{9,1},{2,10},{10,2},{3,11},{11,3},{4,12},{12,4},... | collective-permute-start | bytes 1376264 | tf_op jit(solution)/shard_map/ppermute | solution.py:143
  78.0 2.0 %collective-permute-start.25 = (bf16[64,3584]{1,0:T(8,128)(2,1)S(1)}, bf16[64,3584]{1,0:T(8,128)(2,1)S(1)}, u32[]{:S(2)}, u32[]{:S(2)}) collective-permute-start(bf16[64,3584]{1,0:T(8,128)(2,1)S(1)} %get-tuple-element.81), channel_id=1, source_target_pairs={{0,8},{8,0},{1,9},{9,1},{2,10},{10,2},{3,11},{11,3},{4,12},{12,4},... | collective-permute-start | bytes 1376264 | tf_op jit(solution)/shard_map/ppermute | solution.py:143
  78.3 13.0 %collective-permute-start.28 = (bf16[64,3584]{1,0:T(8,128)(2,1)S(1)}, bf16[64,3584]{1,0:T(8,128)(2,1)S(1)}, u32[]{:S(2)}, u32[]{:S(2)}) collective-permute-start(bf16[64,3584]{1,0:T(8,128)(2,1)S(1)} %add_convert_fusion.2), channel_id=1, source_target_pairs={{0,4},{1,5},{4,6},{5,7},{6,2},{7,3},{2,0},{3,1},{8,12},{9,13},{12,... | collective-permute-start | bytes 1376264 | tf_op jit(solution)/shard_map/ppermute | solution.py:149
  79.8 16.1 %copy-start.2 = (bf16[8,256,576]{1,2,0:T(8,128)(2,1)S(1)}, bf16[8,256,576]{1,2,0:T(8,128)(2,1)}, u32[]{:S(2)}) copy-start(bf16[8,256,576]{1,2,0:T(8,128)(2,1)} %param.16) | copy-start | bytes 7077892
  79.8 13.8 %collective-permute-start.20 = (bf16[64,3584]{1,0:T(8,128)(2,1)S(1)}, bf16[64,3584]{1,0:T(8,128)(2,1)S(1)}, u32[]{:S(2)}, u32[]{:S(2)}) collective-permute-start(bf16[64,3584]{1,0:T(8,128)(2,1)S(1)} %get-tuple-element.73), channel_id=1, source_target_pairs={{0,8},{8,0},{1,9},{9,1},{2,10},{10,2},{3,11},{11,3},{4,12},{12,4},... | collective-permute-start | bytes 1376264 | tf_op jit(solution)/shard_map/ppermute | solution.py:143
  80.2 13.4 %collective-permute-start.26 = (bf16[64,3584]{1,0:T(8,128)(2,1)S(1)}, bf16[64,3584]{1,0:T(8,128)(2,1)S(1)}, u32[]{:S(2)}, u32[]{:S(2)}) collective-permute-start(bf16[64,3584]{1,0:T(8,128)(2,1)S(1)} %add_convert_fusion.3), channel_id=1, source_target_pairs={{0,1},{1,0},{2,3},{3,2},{4,5},{5,4},{6,7},{7,6},{8,9},{9,8},{10,11... | collective-permute-start | bytes 1376264 | tf_op jit(solution)/shard_map/ppermute | solution.py:146
  81.9 20.9 %collective-permute-start.9 = (bf16[64,3584]{1,0:T(8,128)(2,1)S(1)}, bf16[64,3584]{1,0:T(8,128)(2,1)S(1)}, u32[]{:S(2)}, u32[]{:S(2)}) collective-permute-start(bf16[64,3584]{1,0:T(8,128)(2,1)S(1)} %add_convert_fusion.7), channel_id=1, source_target_pairs={{0,1},{1,0},{2,3},{3,2},{4,5},{5,4},{6,7},{7,6},{8,9},{9,8},{10,11... | collective-permute-start | bytes 1376264 | tf_op jit(solution)/shard_map/ppermute | solution.py:146
  94.6 11.6 %collective-permute-start.29 = (bf16[64,3584]{1,0:T(8,128)(2,1)}, bf16[64,3584]{1,0:T(8,128)(2,1)}, u32[]{:S(2)}, u32[]{:S(2)}) collective-permute-start(bf16[64,3584]{1,0:T(8,128)(2,1)} %add_convert_fusion.1), channel_id=1, source_target_pairs={{0,4},{1,5},{4,6},{5,7},{6,2},{7,3},{2,0},{3,1},{8,12},{9,13},{12,... | collective-permute-start | bytes 1376264 | tf_op jit(solution)/shard_map/ppermute | solution.py:149

commit v5 on v4

--- a/solution.py
+++ b/solution.py
@@ -126,6 +126,26 @@
     )(*blocks, w_gate, w_up, w_down)
 
 
+def add_kernel(*refs):
+    terms, out = refs[:-1], refs[-1]
+    total = terms[0][...].astype(jnp.float32)
+    for term in terms[1:]:
+        total += term[...].astype(jnp.float32)
+    out[...] = total.astype(jnp.bfloat16)
+
+
+def add(*terms):
+    inside = pl.BlockSpec(memory_space=pltpu.VMEM)
+    return pl.pallas_call(
+        add_kernel,
+        out_shape=jax.ShapeDtypeStruct(terms[0].shape, jnp.bfloat16),
+        in_specs=[inside] * len(terms),
+        out_specs=inside,
+        compiler_params=pltpu.CompilerParams(vmem_limit_bytes=4 * 1024 * 1024),
+        cost_estimate=pl.CostEstimate(flops=0, bytes_accessed=0, transcendentals=0),
+    )(*terms)
+
+
 def local(hidden_rows, routes, route_weights, w_gate, w_up, w_down, queries, kv_cache, lengths):
     tokens = hidden_rows.shape[0]
     node_count = lax.axis_size("node")
@@ -166,10 +186,8 @@
         return pair((keep_y[slot].astype(f32) + got_y[slot].astype(f32)).astype(bf16))
 
     def onward(slot, carried):
-        value = keep[slot].astype(f32) + got[slot].astype(f32) + back[slot].astype(f32)
-        if carried is not None:
-            value = value + carried.astype(f32)
-        return value.astype(bf16)
+        terms = [keep[slot], got[slot], back[slot]]
+        return add(*terms) if carried is None else add(*terms, carried)
 
     for slot in range(steps):
         arrived = {"other": core(own[slot])}

time: 108 us -> 107 us (level)
  waiting for transfers between devices: 41 us -> 38.2 us
  Pallas kernels: 33.4 us -> 35 us
  other arithmetic: 4.13 us -> 2.71 us
  matrix products: 3.94 us -> 5.12 us
    convert_element_type x4 -> x0, other arithmetic: 3.4 us -> none  [onward(): return value.astype(bf16)]
    ppermute x7, waiting for transfers between devices: 28.4 us -> 26.3 us  [ring(): return lax.ppermute(value, 'rank', hops)]
    pallas_call x0 -> x4, Pallas kernels: none -> 1.61 us  [add(): pl.pallas_call(add_kernel, out_shape=jax.ShapeDtypeStruct(terms[0].shape,...]
    sub x1, other arithmetic: 0.24 us -> 1.44 us  [attend(): exponent = jnp.exp(scores - row_max)]
  transfers between devices with their start and end apart: 30 -> 30, of which waited for: 14 -> 14; matrix products, arithmetic and copies ran while one was open for 6% -> 7% of each run, Pallas kernels for 28% -> 30%
where the time goes in v5:
time: 107 us; the launch traced here: 106 us
  waiting for transfers between devices  38.2 us (36%)
  Pallas kernels  35 us (33%)
  starting transfers between devices  24.6 us (23%)
  matrix products  5.12 us (5%)
  other arithmetic  2.71 us (3%)
    ppermute x7, waiting for transfers between devices, ring(): return lax.ppermute(value, 'rank', hops)  26.3 us
    pallas_call x4, Pallas kernels, run_expert(): pl.pallas_call(lambda *refs: expert_kernel(experts, *refs), out_shape=[ja...  23.5 us
    ppermute x7, waiting for transfers between devices, pair(): return lax.ppermute(value, 'rank', [(i, i ^ 1) for i in range(rank_count)])  11.9 us
    ppermute x7, starting transfers between devices, ring(): return lax.ppermute(value, 'rank', hops)  11.5 us
    ppermute x7, starting transfers between devices, pair(): return lax.ppermute(value, 'rank', [(i, i ^ 1) for i in range(rank_count)])  9.82 us
    pallas_call x1, Pallas kernels, load_inside(): pl.pallas_call(load_kernel, out_shape=[jax.ShapeDtypeStruct(a.shape, a.dt...  7.34 us
    dot_general x1, matrix products, attend(): jnp.einsum('bhl,blc->bhc', softmax_weights, latent_values, preferred_elem...  3.73 us
    ppermute x16, starting transfers between devices, core(): return lax.ppermute(value, 'node', [(i, 1 - i) for i in range(node_count)])  3.22 us
  transfers between devices with their start and end apart: 30, of which 14 were waited for; matrix products, arithmetic and copies ran while one was open for 7% of the time, Pallas kernels for 30%

profile of v5, /device:TPU:0, one launch (start us, length us, event | category | flops | bytes accessed | tf_op | source)
XLA Modules:
  0.0 106.4 jit_solution(6883020626468478589)
XLA Ops:
  0.6 0.0 copy-start
  0.6 2.6 %shard_map.104.refs_0_ = bf16[64,3712]{1,0:T(8,128)(2,1)} custom-call(bf16[64,3584]{1,0:T(8,128)(2,1)} %refs_0_.1, s32[8,64]{1,0:T(8,128)} %bitcast.12, f32[8,64]{1,0:T(8,128)} %bitcast.13), custom_call_target="tpu_custom_call" | custom-call | bytes 917504 | tf_op jit(solution)/shard_map/pallas_call | solution.py:57
  3.2 0.5 collective-permute-start
  3.7 3.6 %collective-permute-start.1 = (bf16[64,3712]{1,0:T(8,128)(2,1)}, bf16[64,3712]{1,0:T(8,128)(2,1)S(1)}, u32[]{:S(2)}, u32[]{:S(2)}) collective-permute-start(bf16[64,3712]{1,0:T(8,128)(2,1)} %shard_map.104.refs_0_), channel_id=1, source_target_pairs={{0,4},{1,5},{4,6},{5,7},{6,2},{7,3},{2,0},{3,1},{8,12},{9,13},{12,... | collective-permute-start | bytes 1425416 | tf_op jit(solution)/shard_map/ppermute | solution.py:169
  7.4 1.5 %collective-permute-start.2 = (bf16[64,3712]{1,0:T(8,128)(2,1)}, bf16[64,3712]{1,0:T(8,128)(2,1)S(1)}, u32[]{:S(2)}, u32[]{:S(2)}) collective-permute-start(bf16[64,3712]{1,0:T(8,128)(2,1)} %shard_map.104.refs_0_), channel_id=1, source_target_pairs={{0,1},{1,0},{2,3},{3,2},{4,5},{5,4},{6,7},{7,6},{8,9},{9,8},{10,11... | collective-permute-start | bytes 1425416 | tf_op jit(solution)/shard_map/ppermute | solution.py:166
  8.9 7.3 %shard_map.105 = (bf16[3584,1024]{1,0:T(8,128)(2,1)S(1)}, bf16[3584,1024]{1,0:T(8,128)(2,1)S(1)}, bf16[1024,3584]{1,0:T(8,128)(2,1)S(1)}) custom-call(bf16[3584,1024]{1,0:T(8,128)(2,1)} %bitcast.9, bf16[3584,1024]{1,0:T(8,128)(2,1)} %bitcast.10, bf16[1024,3584]{1,0:T(8,128)(2,1)} %bitcast.11), custom_call_target="tpu_custom_call" | custom-call | bytes 22020096 | tf_op jit(solution)/shard_map/pallas_call | solution.py:101
  16.3 0.0 collective-permute-done.refs_1_
  16.3 2.2 %collective-permute-done.1.refs_0_ = bf16[64,3712]{1,0:T(8,128)(2,1)S(1)} collective-permute-done((bf16[64,3712]{1,0:T(8,128)(2,1)}, bf16[64,3712]{1,0:T(8,128)(2,1)S(1)}, u32[]{:S(2)}, u32[]{:S(2)}) %collective-permute-start.1) | collective-permute-done | bytes 475168 | tf_op jit(solution)/shard_map/ppermute | solution.py:169
  18.4 2.1 %collective-permute-done.2.refs_2_ = bf16[64,3712]{1,0:T(8,128)(2,1)S(1)} collective-permute-done((bf16[64,3712]{1,0:T(8,128)(2,1)}, bf16[64,3712]{1,0:T(8,128)(2,1)S(1)}, u32[]{:S(2)}, u32[]{:S(2)}) %collective-permute-start.2) | collective-permute-done | bytes 475168 | tf_op jit(solution)/shard_map/ppermute | solution.py:166
  20.5 0.0 collective-permute-start.3
  20.5 0.5 collective-permute-start.5
  21.1 1.6 %collective-permute-start.6 = (bf16[64,3712]{1,0:T(8,128)(2,1)S(1)}, bf16[64,3712]{1,0:T(8,128)(2,1)S(1)}, u32[]{:S(2)}, u32[]{:S(2)}) collective-permute-start(bf16[64,3712]{1,0:T(8,128)(2,1)S(1)} %collective-permute-done.1.refs_0_), channel_id=1, source_target_pairs={{0,4},{1,5},{4,6},{5,7},{6,2},{7,3},{2,0},{3,1},{8,12},{9,13},{12,... | collective-permute-start | bytes 1425416 | tf_op jit(solution)/shard_map/ppermute | solution.py:169
  22.6 1.5 %collective-permute-start.7 = (bf16[64,3712]{1,0:T(8,128)(2,1)S(1)}, bf16[64,3712]{1,0:T(8,128)(2,1)S(1)}, u32[]{:S(2)}, u32[]{:S(2)}) collective-permute-start(bf16[64,3712]{1,0:T(8,128)(2,1)S(1)} %collective-permute-done.1.refs_0_), channel_id=1, source_target_pairs={{0,1},{1,0},{2,3},{3,2},{4,5},{5,4},{6,7},{7,6},{8,9},{9,8},{10,11... | collective-permute-start | bytes 1425416 | tf_op jit(solution)/shard_map/ppermute | solution.py:166
  24.2 5.9 %shard_map.106 = (bf16[64,3584]{1,0:T(8,128)(2,1)S(1)}, bf16[64,3584]{1,0:T(8,128)(2,1)S(1)}, bf16[64,3584]{1,0:T(8,128)(2,1)S(1)}, bf16[64,3584]{1,0:T(8,128)(2,1)S(1)}) custom-call(bf16[64,3712]{1,0:T(8,128)(2,1)S(1)} %copy-done.1, bf16[64,3712]{1,0:T(8,128)(2,1)S(1)} %collective-permute-done.refs_1_, bf16[64,3712]{1,0:T(8,128)(2,1)S(1)} %collective-permute-done.2.refs_2_, ...), custom_call_target="tpu_custom_call" | custom-call | tf_op jit(solution)/shard_map/pallas_call | solution.py:118
  30.0 3.8 %collective-permute-done.6.refs_0_ = bf16[64,3712]{1,0:T(8,128)(2,1)S(1)} collective-permute-done((bf16[64,3712]{1,0:T(8,128)(2,1)S(1)}, bf16[64,3712]{1,0:T(8,128)(2,1)S(1)}, u32[]{:S(2)}, u32[]{:S(2)}) %collective-permute-start.6) | collective-permute-done | bytes 475168 | tf_op jit(solution)/shard_map/ppermute | solution.py:169
  33.8 1.3 %collective-permute-done.7.refs_2_ = bf16[64,3712]{1,0:T(8,128)(2,1)S(1)} collective-permute-done((bf16[64,3712]{1,0:T(8,128)(2,1)S(1)}, bf16[64,3712]{1,0:T(8,128)(2,1)S(1)}, u32[]{:S(2)}, u32[]{:S(2)}) %collective-permute-start.7) | collective-permute-done | bytes 475168 | tf_op jit(solution)/shard_map/ppermute | solution.py:166
  35.1 0.0 collective-permute-start.10
  35.1 0.5 collective-permute-start.11
  35.6 1.2 %collective-permute-start.12 = (bf16[64,3712]{1,0:T(8,128)(2,1)S(1)}, bf16[64,3712]{1,0:T(8,128)(2,1)S(1)}, u32[]{:S(2)}, u32[]{:S(2)}) collective-permute-start(bf16[64,3712]{1,0:T(8,128)(2,1)S(1)} %collective-permute-done.6.refs_0_), channel_id=1, source_target_pairs={{0,4},{1,5},{4,6},{5,7},{6,2},{7,3},{2,0},{3,1},{8,12},{9,13},{12,... | collective-permute-start | bytes 1425416 | tf_op jit(solution)/shard_map/ppermute | solution.py:169
  36.8 1.5 %collective-permute-start.13 = (bf16[64,3712]{1,0:T(8,128)(2,1)S(1)}, bf16[64,3712]{1,0:T(8,128)(2,1)S(1)}, u32[]{:S(2)}, u32[]{:S(2)}) collective-permute-start(bf16[64,3712]{1,0:T(8,128)(2,1)S(1)} %collective-permute-done.6.refs_0_), channel_id=1, source_target_pairs={{0,1},{1,0},{2,3},{3,2},{4,5},{5,4},{6,7},{7,6},{8,9},{9,8},{10,11... | collective-permute-start | bytes 1425416 | tf_op jit(solution)/shard_map/ppermute | solution.py:166
  38.3 5.9 %shard_map.107 = (bf16[64,3584]{1,0:T(8,128)(2,1)S(1)}, bf16[64,3584]{1,0:T(8,128)(2,1)S(1)}, bf16[64,3584]{1,0:T(8,128)(2,1)S(1)}, bf16[64,3584]{1,0:T(8,128)(2,1)S(1)}) custom-call(bf16[64,3712]{1,0:T(8,128)(2,1)S(1)} %collective-permute-done.1.refs_0_, bf16[64,3712]{1,0:T(8,128)(2,1)S(1)} %collective-permute-done.5.refs_1_, ...), custom_call_target="tpu_custom_call" | custom-call | tf_op jit(solution)/shard_map/pallas_call | solution.py:118
  44.2 0.1 collective-permute-start.14
  44.3 4.1 %collective-permute-done.12.refs_0_ = bf16[64,3712]{1,0:T(8,128)(2,1)S(1)} collective-permute-done((bf16[64,3712]{1,0:T(8,128)(2,1)S(1)}, bf16[64,3712]{1,0:T(8,128)(2,1)S(1)}, u32[]{:S(2)}, u32[]{:S(2)}) %collective-permute-start.12) | collective-permute-done | bytes 475168 | tf_op jit(solution)/shard_map/ppermute | solution.py:169
  48.4 0.9 collective-permute-done.13.refs_2_
  49.3 0.0 collective-permute-start.16
  49.3 1.2 %collective-permute-start.18 = (bf16[64,3712]{1,0:T(8,128)(2,1)S(1)}, bf16[64,3712]{1,0:T(8,128)(2,1)S(1)}, u32[]{:S(2)}, u32[]{:S(2)}) collective-permute-start(bf16[64,3712]{1,0:T(8,128)(2,1)S(1)} %collective-permute-done.13.refs_2_), channel_id=1, source_target_pairs={{0,4},{1,5},{4,6},{5,7},{6,2},{7,3},{2,0},{3,1},{8,12},{9,13},{12,... | collective-permute-start | bytes 1425416 | tf_op jit(solution)/shard_map/ppermute | solution.py:169
  50.5 0.2 collective-permute-start.17
  50.7 0.1 add_convert_fusion.2
  50.8 1.6 %collective-permute-start.15 = (bf16[64,3584]{1,0:T(8,128)(2,1)S(1)}, bf16[64,3584]{1,0:T(8,128)(2,1)S(1)}, u32[]{:S(2)}, u32[]{:S(2)}) collective-permute-start(bf16[64,3584]{1,0:T(8,128)(2,1)S(1)} %add_convert_fusion.2), channel_id=1, source_target_pairs={{0,1},{1,0},{2,3},{3,2},{4,5},{5,4},{6,7},{7,6},{8,9},{9,8},{10,11... | collective-permute-start | bytes 1376264 | tf_op jit(solution)/shard_map/ppermute | solution.py:166
  52.4 0.0 collective-permute-start.23
  52.4 5.9 %shard_map.108 = (bf16[64,3584]{1,0:T(8,128)(2,1)S(1)}, bf16[64,3584]{1,0:T(8,128)(2,1)S(1)}, bf16[64,3584]{1,0:T(8,128)(2,1)S(1)}, bf16[64,3584]{1,0:T(8,128)(2,1)S(1)}) custom-call(bf16[64,3712]{1,0:T(8,128)(2,1)S(1)} %collective-permute-done.6.refs_0_, bf16[64,3712]{1,0:T(8,128)(2,1)S(1)} %collective-permute-done.11.refs_1_, ...), custom_call_target="tpu_custom_call" | custom-call | tf_op jit(solution)/shard_map/pallas_call | solution.py:118
  58.3 0.6 collective-permute-start.21
  58.9 0.0 collective-permute-done.17.refs_1_
  58.9 3.7 %collective-permute-done.18.refs_2_ = bf16[64,3712]{1,0:T(8,128)(2,1)S(1)} collective-permute-done((bf16[64,3712]{1,0:T(8,128)(2,1)S(1)}, bf16[64,3712]{1,0:T(8,128)(2,1)S(1)}, u32[]{:S(2)}, u32[]{:S(2)}) %collective-permute-start.18) | collective-permute-done | bytes 475168 | tf_op jit(solution)/shard_map/ppermute | solution.py:169
  62.6 1.0 collective-permute-done.15.refs_2_
  63.6 0.0 collective-permute-done.23.refs_1_
  63.6 0.2 shard_map.110
  63.8 1.1 %collective-permute-start.24 = (bf16[64,3584]{1,0:T(8,128)(2,1)S(1)}, bf16[64,3584]{1,0:T(8,128)(2,1)S(1)}, u32[]{:S(2)}, u32[]{:S(2)}) collective-permute-start(bf16[64,3584]{1,0:T(8,128)(2,1)S(1)} %shard_map.110), channel_id=1, source_target_pairs={{0,4},{1,5},{4,6},{5,7},{6,2},{7,3},{2,0},{3,1},{8,12},{9,13},{12,... | collective-permute-start | bytes 1376264 | tf_op jit(solution)/shard_map/ppermute | solution.py:169
  64.9 0.1 add_convert_fusion.1
  65.0 1.6 %collective-permute-start.22 = (bf16[64,3584]{1,0:T(8,128)(2,1)S(1)}, bf16[64,3584]{1,0:T(8,128)(2,1)S(1)}, u32[]{:S(2)}, u32[]{:S(2)}) collective-permute-start(bf16[64,3584]{1,0:T(8,128)(2,1)S(1)} %add_convert_fusion.1), channel_id=1, source_target_pairs={{0,1},{1,0},{2,3},{3,2},{4,5},{5,4},{6,7},{7,6},{8,9},{9,8},{10,11... | collective-permute-start | bytes 1376264 | tf_op jit(solution)/shard_map/ppermute | solution.py:166
  66.6 0.2 collective-permute-start.27
  66.9 0.0 collective-permute-done.19.refs_3_
  66.9 5.9 %shard_map.109 = (bf16[64,3584]{1,0:T(8,128)(2,1)S(1)}, bf16[64,3584]{1,0:T(8,128)(2,1)S(1)}, bf16[64,3584]{1,0:T(8,128)(2,1)S(1)}, bf16[64,3584]{1,0:T(8,128)(2,1)S(1)}) custom-call(bf16[64,3712]{1,0:T(8,128)(2,1)S(1)} %collective-permute-done.12.refs_0_, bf16[64,3712]{1,0:T(8,128)(2,1)S(1)} %collective-permute-done.17.refs_1_, ...), custom_call_target="tpu_custom_call" | custom-call | tf_op jit(solution)/shard_map/pallas_call | solution.py:118
  72.7 0.3 collective-permute-start.25
  73.1 0.1 iota_compare_fusion
  73.2 0.2 collective-permute-start.8
  73.4 2.4 %collective-permute-done.24.refs_3_ = bf16[64,3584]{1,0:T(8,128)(2,1)S(1)} collective-permute-done((bf16[64,3584]{1,0:T(8,128)(2,1)S(1)}, bf16[64,3584]{1,0:T(8,128)(2,1)S(1)}, u32[]{:S(2)}, u32[]{:S(2)}) %collective-permute-start.24) | collective-permute-done | bytes 458784 | tf_op jit(solution)/shard_map/ppermute | solution.py:169
  75.7 2.3 %collective-permute-done.22.refs_2_ = bf16[64,3584]{1,0:T(8,128)(2,1)S(1)} collective-permute-done((bf16[64,3584]{1,0:T(8,128)(2,1)S(1)}, bf16[64,3584]{1,0:T(8,128)(2,1)S(1)}, u32[]{:S(2)}, u32[]{:S(2)}) %collective-permute-start.22) | collective-permute-done | bytes 458784 | tf_op jit(solution)/shard_map/ppermute | solution.py:166
  78.0 0.2 shard_map.111
  78.3 1.6 %collective-permute-start.28 = (bf16[64,3584]{1,0:T(8,128)(2,1)S(1)}, bf16[64,3584]{1,0:T(8,128)(2,1)S(1)}, u32[]{:S(2)}, u32[]{:S(2)}) collective-permute-start(bf16[64,3584]{1,0:T(8,128)(2,1)S(1)} %shard_map.111), channel_id=1, source_target_pairs={{0,4},{1,5},{4,6},{5,7},{6,2},{7,3},{2,0},{3,1},{8,12},{9,13},{12,... | collective-permute-start | bytes 1376264 | tf_op jit(solution)/shard_map/ppermute | solution.py:169
  79.8 0.1 add_convert_fusion
  80.0 1.6 %collective-permute-start.26 = (bf16[64,3584]{1,0:T(8,128)(2,1)S(1)}, bf16[64,3584]{1,0:T(8,128)(2,1)S(1)}, u32[]{:S(2)}, u32[]{:S(2)}) collective-permute-start(bf16[64,3584]{1,0:T(8,128)(2,1)S(1)} %add_convert_fusion), channel_id=1, source_target_pairs={{0,1},{1,0},{2,3},{3,2},{4,5},{5,4},{6,7},{7,6},{8,9},{9,8},{10,11... | collective-permute-start | bytes 1376264 | tf_op jit(solution)/shard_map/ppermute | solution.py:166
  81.6 0.9 add_convert_fusion.3
  82.4 0.5 collective-permute-start.9
  82.9 7.5 %collective-permute-done.28.refs_3_ = bf16[64,3584]{1,0:T(8,128)(2,1)S(1)} collective-permute-done((bf16[64,3584]{1,0:T(8,128)(2,1)S(1)}, bf16[64,3584]{1,0:T(8,128)(2,1)S(1)}, u32[]{:S(2)}, u32[]{:S(2)}) %collective-permute-start.28) | collective-permute-done | bytes 458784 | tf_op jit(solution)/shard_map/ppermute | solution.py:169
  90.5 2.9 %collective-permute-done.26.refs_2_ = bf16[64,3584]{1,0:T(8,128)(2,1)S(1)} collective-permute-done((bf16[64,3584]{1,0:T(8,128)(2,1)S(1)}, bf16[64,3584]{1,0:T(8,128)(2,1)S(1)}, u32[]{:S(2)}, u32[]{:S(2)}) %collective-permute-start.26) | collective-permute-done | bytes 458784 | tf_op jit(solution)/shard_map/ppermute | solution.py:166
  93.3 0.2 shard_map.112
  93.6 1.2 %collective-permute-start.29 = (bf16[64,3584]{1,0:T(8,128)(2,1)S(1)}, bf16[64,3584]{1,0:T(8,128)(2,1)S(1)}, u32[]{:S(2)}, u32[]{:S(2)}) collective-permute-start(bf16[64,3584]{1,0:T(8,128)(2,1)S(1)} %shard_map.112), channel_id=1, source_target_pairs={{0,4},{1,5},{4,6},{5,7},{6,2},{7,3},{2,0},{3,1},{8,12},{9,13},{12,... | collective-permute-start | bytes 1376264 | tf_op jit(solution)/shard_map/ppermute | solution.py:169
  94.8 1.4 %fusion.8 = f32[8,64,256]{2,1,0:T(8,128)} fusion(bf16[8,64,576]{2,1,0:T(8,128)(2,1)S(1)} %copy-done, bf16[8,256,576]{1,2,0:T(8,128)(2,1)S(1)} %copy-done.2, pred[8,256]{1,0:T(8,128)(4,1)S(1)} %iota_compare_fusion), kind=kOutput, calls=%fused_computation.7 | convolution fusion | flops 151257088 | bytes 3475456 | tf_op jit(solution)/shard_map/bhc,blc->bhl/dot_general | solution.py:19
  96.2 1.4 %fusion.11 = f32[8,64]{1,0:T(8,128)S(1)} fusion(f32[8,64,256]{2,1,0:T(8,128)} %fusion.8), kind=kOutput, calls=%fused_computation.16 | output fusion | flops 262399 | bytes 526336 | tf_op jit(solution)/shard_map/sub | solution.py:25
  97.6 3.7 %fusion.3 = bf16[8,64,512]{2,1,0:T(8,128)(2,1)} fusion(bf16[8,256,576]{1,2,0:T(8,128)(2,1)} %param.16, f32[8,64]{1,0:T(8,128)S(1)} %fusion.11, f32[8,64,256]{2,1,0:T(8,128)} %fusion.8), kind=kOutput, calls=%fused_computation.3 | convolution fusion | flops 134873856 | bytes 3672064 | tf_op jit(solution)/shard_map/bhl,blc->bhc/dot_general | solution.py:28
  101.4 1.4 %collective-permute-done.9.refs_2_ = bf16[64,3584]{1,0:T(8,128)(2,1)S(1)} collective-permute-done((bf16[64,3584]{1,0:T(8,128)(2,1)}, bf16[64,3584]{1,0:T(8,128)(2,1)S(1)}, u32[]{:S(2)}, u32[]{:S(2)}) %collective-permute-start.9) | collective-permute-done | bytes 458784 | tf_op jit(solution)/shard_map/ppermute | solution.py:166
  102.8 2.6 %collective-permute-done.29.refs_3_ = bf16[64,3584]{1,0:T(8,128)(2,1)S(1)} collective-permute-done((bf16[64,3584]{1,0:T(8,128)(2,1)S(1)}, bf16[64,3584]{1,0:T(8,128)(2,1)S(1)}, u32[]{:S(2)}, u32[]{:S(2)}) %collective-permute-start.29) | collective-permute-done | bytes 458784 | tf_op jit(solution)/shard_map/ppermute | solution.py:169
  105.4 1.0 shard_map.113
  (22 shorter events, 0.1 us)
Async XLA Ops:
  0.6 94.2 %copy-start = (bf16[8,64,576]{2,1,0:T(8,128)(2,1)S(1)}, bf16[8,64,576]{2,1,0:T(8,128)(2,1)}, u32[]{:S(2)}) copy-start(bf16[8,64,576]{2,1,0:T(8,128)(2,1)} %param.15) | copy-start | bytes 1769476
  3.2 13.0 %collective-permute-start = (bf16[64,3712]{1,0:T(8,128)(2,1)}, bf16[64,3712]{1,0:T(8,128)(2,1)S(1)}, u32[]{:S(2)}, u32[]{:S(2)}) collective-permute-start(bf16[64,3712]{1,0:T(8,128)(2,1)} %shard_map.104.refs_0_), channel_id=1, source_target_pairs={{0,8},{8,0},{1,9},{9,1},{2,10},{10,2},{3,11},{11,3},{4,12},{12,4},... | collective-permute-start | bytes 1425416 | tf_op jit(solution)/shard_map/ppermute | solution.py:163
  3.7 14.7 %collective-permute-start.1 = (bf16[64,3712]{1,0:T(8,128)(2,1)}, bf16[64,3712]{1,0:T(8,128)(2,1)S(1)}, u32[]{:S(2)}, u32[]{:S(2)}) collective-permute-start(bf16[64,3712]{1,0:T(8,128)(2,1)} %shard_map.104.refs_0_), channel_id=1, source_target_pairs={{0,4},{1,5},{4,6},{5,7},{6,2},{7,3},{2,0},{3,1},{8,12},{9,13},{12,... | collective-permute-start | bytes 1425416 | tf_op jit(solution)/shard_map/ppermute | solution.py:169
  7.4 13.2 %collective-permute-start.2 = (bf16[64,3712]{1,0:T(8,128)(2,1)}, bf16[64,3712]{1,0:T(8,128)(2,1)S(1)}, u32[]{:S(2)}, u32[]{:S(2)}) collective-permute-start(bf16[64,3712]{1,0:T(8,128)(2,1)} %shard_map.104.refs_0_), channel_id=1, source_target_pairs={{0,1},{1,0},{2,3},{3,2},{4,5},{5,4},{6,7},{7,6},{8,9},{9,8},{10,11... | collective-permute-start | bytes 1425416 | tf_op jit(solution)/shard_map/ppermute | solution.py:166
  8.9 15.2 %copy-start.1 = (bf16[64,3712]{1,0:T(8,128)(2,1)S(1)}, bf16[64,3712]{1,0:T(8,128)(2,1)}, u32[]{:S(2)}) copy-start(bf16[64,3712]{1,0:T(8,128)(2,1)} %shard_map.104.refs_0_) | copy-start | bytes 1425412
  20.5 3.6 %collective-permute-start.3 = (bf16[64,3712]{1,0:T(8,128)(2,1)S(1)}, bf16[64,3712]{1,0:T(8,128)(2,1)S(1)}, u32[]{:S(2)}, u32[]{:S(2)}) collective-permute-start(bf16[64,3712]{1,0:T(8,128)(2,1)S(1)} %collective-permute-done.2.refs_2_), channel_id=1, source_target_pairs={{0,8},{8,0},{1,9},{9,1},{2,10},{10,2},{3,11},{11,3},{4,12},{12,4},... | collective-permute-start | bytes 1425416 | tf_op jit(solution)/shard_map/ppermute | solution.py:163
  20.5 9.5 %collective-permute-start.5 = (bf16[64,3712]{1,0:T(8,128)(2,1)S(1)}, bf16[64,3712]{1,0:T(8,128)(2,1)S(1)}, u32[]{:S(2)}, u32[]{:S(2)}) collective-permute-start(bf16[64,3712]{1,0:T(8,128)(2,1)S(1)} %collective-permute-done.1.refs_0_), channel_id=1, source_target_pairs={{0,8},{8,0},{1,9},{9,1},{2,10},{10,2},{3,11},{11,3},{4,12},{12,4},... | collective-permute-start | bytes 1425416 | tf_op jit(solution)/shard_map/ppermute | solution.py:163
  21.1 12.8 %collective-permute-start.6 = (bf16[64,3712]{1,0:T(8,128)(2,1)S(1)}, bf16[64,3712]{1,0:T(8,128)(2,1)S(1)}, u32[]{:S(2)}, u32[]{:S(2)}) collective-permute-start(bf16[64,3712]{1,0:T(8,128)(2,1)S(1)} %collective-permute-done.1.refs_0_), channel_id=1, source_target_pairs={{0,4},{1,5},{4,6},{5,7},{6,2},{7,3},{2,0},{3,1},{8,12},{9,13},{12,... | collective-permute-start | bytes 1425416 | tf_op jit(solution)/shard_map/ppermute | solution.py:169
  22.6 12.5 %collective-permute-start.7 = (bf16[64,3712]{1,0:T(8,128)(2,1)S(1)}, bf16[64,3712]{1,0:T(8,128)(2,1)S(1)}, u32[]{:S(2)}, u32[]{:S(2)}) collective-permute-start(bf16[64,3712]{1,0:T(8,128)(2,1)S(1)} %collective-permute-done.1.refs_0_), channel_id=1, source_target_pairs={{0,1},{1,0},{2,3},{3,2},{4,5},{5,4},{6,7},{7,6},{8,9},{9,8},{10,11... | collective-permute-start | bytes 1425416 | tf_op jit(solution)/shard_map/ppermute | solution.py:166
  35.1 3.2 %collective-permute-start.10 = (bf16[64,3712]{1,0:T(8,128)(2,1)S(1)}, bf16[64,3712]{1,0:T(8,128)(2,1)S(1)}, u32[]{:S(2)}, u32[]{:S(2)}) collective-permute-start(bf16[64,3712]{1,0:T(8,128)(2,1)S(1)} %collective-permute-done.7.refs_2_), channel_id=1, source_target_pairs={{0,8},{8,0},{1,9},{9,1},{2,10},{10,2},{3,11},{11,3},{4,12},{12,4},... | collective-permute-start | bytes 1425416 | tf_op jit(solution)/shard_map/ppermute | solution.py:163
  35.1 9.2 %collective-permute-start.11 = (bf16[64,3712]{1,0:T(8,128)(2,1)S(1)}, bf16[64,3712]{1,0:T(8,128)(2,1)S(1)}, u32[]{:S(2)}, u32[]{:S(2)}) collective-permute-start(bf16[64,3712]{1,0:T(8,128)(2,1)S(1)} %collective-permute-done.6.refs_0_), channel_id=1, source_target_pairs={{0,8},{8,0},{1,9},{9,1},{2,10},{10,2},{3,11},{11,3},{4,12},{12,4},... | collective-permute-start | bytes 1425416 | tf_op jit(solution)/shard_map/ppermute | solution.py:163
  35.6 12.8 %collective-permute-start.12 = (bf16[64,3712]{1,0:T(8,128)(2,1)S(1)}, bf16[64,3712]{1,0:T(8,128)(2,1)S(1)}, u32[]{:S(2)}, u32[]{:S(2)}) collective-permute-start(bf16[64,3712]{1,0:T(8,128)(2,1)S(1)} %collective-permute-done.6.refs_0_), channel_id=1, source_target_pairs={{0,4},{1,5},{4,6},{5,7},{6,2},{7,3},{2,0},{3,1},{8,12},{9,13},{12,... | collective-permute-start | bytes 1425416 | tf_op jit(solution)/shard_map/ppermute | solution.py:169
  36.8 12.5 %collective-permute-start.13 = (bf16[64,3712]{1,0:T(8,128)(2,1)S(1)}, bf16[64,3712]{1,0:T(8,128)(2,1)S(1)}, u32[]{:S(2)}, u32[]{:S(2)}) collective-permute-start(bf16[64,3712]{1,0:T(8,128)(2,1)S(1)} %collective-permute-done.6.refs_0_), channel_id=1, source_target_pairs={{0,1},{1,0},{2,3},{3,2},{4,5},{5,4},{6,7},{7,6},{8,9},{9,8},{10,11... | collective-permute-start | bytes 1425416 | tf_op jit(solution)/shard_map/ppermute | solution.py:166
  44.2 6.5 %collective-permute-start.14 = (bf16[64,3584]{1,0:T(8,128)(2,1)S(1)}, bf16[64,3584]{1,0:T(8,128)(2,1)S(1)}, u32[]{:S(2)}, u32[]{:S(2)}) collective-permute-start(bf16[64,3584]{1,0:T(8,128)(2,1)S(1)} %get-tuple-element.66), channel_id=1, source_target_pairs={{0,8},{8,0},{1,9},{9,1},{2,10},{10,2},{3,11},{11,3},{4,12},{12,4},... | collective-permute-start | bytes 1376264 | tf_op jit(solution)/shard_map/ppermute | solution.py:163
  49.3 3.1 %collective-permute-start.16 = (bf16[64,3712]{1,0:T(8,128)(2,1)S(1)}, bf16[64,3712]{1,0:T(8,128)(2,1)S(1)}, u32[]{:S(2)}, u32[]{:S(2)}) collective-permute-start(bf16[64,3712]{1,0:T(8,128)(2,1)S(1)} %collective-permute-done.13.refs_2_), channel_id=1, source_target_pairs={{0,8},{8,0},{1,9},{9,1},{2,10},{10,2},{3,11},{11,3},{4,12},{12,4},... | collective-permute-start | bytes 1425416 | tf_op jit(solution)/shard_map/ppermute | solution.py:163
  49.3 13.3 %collective-permute-start.18 = (bf16[64,3712]{1,0:T(8,128)(2,1)S(1)}, bf16[64,3712]{1,0:T(8,128)(2,1)S(1)}, u32[]{:S(2)}, u32[]{:S(2)}) collective-permute-start(bf16[64,3712]{1,0:T(8,128)(2,1)S(1)} %collective-permute-done.13.refs_2_), channel_id=1, source_target_pairs={{0,4},{1,5},{4,6},{5,7},{6,2},{7,3},{2,0},{3,1},{8,12},{9,13},{12,... | collective-permute-start | bytes 1425416 | tf_op jit(solution)/shard_map/ppermute | solution.py:169
  50.5 8.4 %collective-permute-start.17 = (bf16[64,3712]{1,0:T(8,128)(2,1)S(1)}, bf16[64,3712]{1,0:T(8,128)(2,1)S(1)}, u32[]{:S(2)}, u32[]{:S(2)}) collective-permute-start(bf16[64,3712]{1,0:T(8,128)(2,1)S(1)} %collective-permute-done.12.refs_0_), channel_id=1, source_target_pairs={{0,8},{8,0},{1,9},{9,1},{2,10},{10,2},{3,11},{11,3},{4,12},{12,4},... | collective-permute-start | bytes 1425416 | tf_op jit(solution)/shard_map/ppermute | solution.py:163
  50.8 12.8 %collective-permute-start.15 = (bf16[64,3584]{1,0:T(8,128)(2,1)S(1)}, bf16[64,3584]{1,0:T(8,128)(2,1)S(1)}, u32[]{:S(2)}, u32[]{:S(2)}) collective-permute-start(bf16[64,3584]{1,0:T(8,128)(2,1)S(1)} %add_convert_fusion.2), channel_id=1, source_target_pairs={{0,1},{1,0},{2,3},{3,2},{4,5},{5,4},{6,7},{7,6},{8,9},{9,8},{10,11... | collective-permute-start | bytes 1376264 | tf_op jit(solution)/shard_map/ppermute | solution.py:166
  52.4 11.2 %collective-permute-start.23 = (bf16[64,3584]{1,0:T(8,128)(2,1)S(1)}, bf16[64,3584]{1,0:T(8,128)(2,1)S(1)}, u32[]{:S(2)}, u32[]{:S(2)}) collective-permute-start(bf16[64,3584]{1,0:T(8,128)(2,1)S(1)} %get-tuple-element.77), channel_id=1, source_target_pairs={{0,8},{8,0},{1,9},{9,1},{2,10},{10,2},{3,11},{11,3},{4,12},{12,4},... | collective-permute-start | bytes 1376264 | tf_op jit(solution)/shard_map/ppermute | solution.py:163
  58.3 6.6 %collective-permute-start.21 = (bf16[64,3584]{1,0:T(8,128)(2,1)S(1)}, bf16[64,3584]{1,0:T(8,128)(2,1)S(1)}, u32[]{:S(2)}, u32[]{:S(2)}) collective-permute-start(bf16[64,3584]{1,0:T(8,128)(2,1)S(1)} %get-tuple-element.75), channel_id=1, source_target_pairs={{0,8},{8,0},{1,9},{9,1},{2,10},{10,2},{3,11},{11,3},{4,12},{12,4},... | collective-permute-start | bytes 1376264 | tf_op jit(solution)/shard_map/ppermute | solution.py:163
  63.8 11.9 %collective-permute-start.24 = (bf16[64,3584]{1,0:T(8,128)(2,1)S(1)}, bf16[64,3584]{1,0:T(8,128)(2,1)S(1)}, u32[]{:S(2)}, u32[]{:S(2)}) collective-permute-start(bf16[64,3584]{1,0:T(8,128)(2,1)S(1)} %shard_map.110), channel_id=1, source_target_pairs={{0,4},{1,5},{4,6},{5,7},{6,2},{7,3},{2,0},{3,1},{8,12},{9,13},{12,... | collective-permute-start | bytes 1376264 | tf_op jit(solution)/shard_map/ppermute | solution.py:169
  64.9 1.9 %collective-permute-start.19 = (bf16[64,3712]{1,0:T(8,128)(2,1)S(1)}, bf16[64,3712]{1,0:T(8,128)(2,1)S(1)}, u32[]{:S(2)}, u32[]{:S(2)}) collective-permute-start(bf16[64,3712]{1,0:T(8,128)(2,1)S(1)} %collective-permute-done.18.refs_2_), channel_id=1, source_target_pairs={{0,8},{8,0},{1,9},{9,1},{2,10},{10,2},{3,11},{11,3},{4,12},{12,4},... | collective-permute-start | bytes 1425416 | tf_op jit(solution)/shard_map/ppermute | solution.py:163
  65.0 13.0 %collective-permute-start.22 = (bf16[64,3584]{1,0:T(8,128)(2,1)S(1)}, bf16[64,3584]{1,0:T(8,128)(2,1)S(1)}, u32[]{:S(2)}, u32[]{:S(2)}) collective-permute-start(bf16[64,3584]{1,0:T(8,128)(2,1)S(1)} %add_convert_fusion.1), channel_id=1, source_target_pairs={{0,1},{1,0},{2,3},{3,2},{4,5},{5,4},{6,7},{7,6},{8,9},{9,8},{10,11... | collective-permute-start | bytes 1376264 | tf_op jit(solution)/shard_map/ppermute | solution.py:166
  66.6 6.5 %copy-start.3 = (s32[8]{0:T(128)S(1)}, s32[8]{0:T(128)}, u32[]{:S(2)}) copy-start(s32[8]{0:T(128)} %param.17) | copy-start | bytes 100
  66.6 11.4 %collective-permute-start.27 = (bf16[64,3584]{1,0:T(8,128)(2,1)S(1)}, bf16[64,3584]{1,0:T(8,128)(2,1)S(1)}, u32[]{:S(2)}, u32[]{:S(2)}) collective-permute-start(bf16[64,3584]{1,0:T(8,128)(2,1)S(1)} %get-tuple-element.83), channel_id=1, source_target_pairs={{0,8},{8,0},{1,9},{9,1},{2,10},{10,2},{3,11},{11,3},{4,12},{12,4},... | collective-permute-start | bytes 1376264 | tf_op jit(solution)/shard_map/ppermute | solution.py:163
  72.7 7.1 %collective-permute-start.25 = (bf16[64,3584]{1,0:T(8,128)(2,1)S(1)}, bf16[64,3584]{1,0:T(8,128)(2,1)S(1)}, u32[]{:S(2)}, u32[]{:S(2)}) collective-permute-start(bf16[64,3584]{1,0:T(8,128)(2,1)S(1)} %get-tuple-element.81), channel_id=1, source_target_pairs={{0,8},{8,0},{1,9},{9,1},{2,10},{10,2},{3,11},{11,3},{4,12},{12,4},... | collective-permute-start | bytes 1376264 | tf_op jit(solution)/shard_map/ppermute | solution.py:163
  73.2 8.4 %collective-permute-start.8 = (bf16[64,3584]{1,0:T(8,128)(2,1)S(1)}, bf16[64,3584]{1,0:T(8,128)(2,1)S(1)}, u32[]{:S(2)}, u32[]{:S(2)}) collective-permute-start(bf16[64,3584]{1,0:T(8,128)(2,1)S(1)} %get-tuple-element.59), channel_id=1, source_target_pairs={{0,8},{8,0},{1,9},{9,1},{2,10},{10,2},{3,11},{11,3},{4,12},{12,4},... | collective-permute-start | bytes 1376264 | tf_op jit(solution)/shard_map/ppermute | solution.py:163
  75.7 29.6 %collective-permute-start.4 = (bf16[64,3584]{1,0:T(8,128)(2,1)S(1)}, bf16[64,3584]{1,0:T(8,128)(2,1)S(1)}, u32[]{:S(2)}, u32[]{:S(2)}) collective-permute-start(bf16[64,3584]{1,0:T(8,128)(2,1)S(1)} %get-tuple-element.55), channel_id=1, source_target_pairs={{0,8},{8,0},{1,9},{9,1},{2,10},{10,2},{3,11},{11,3},{4,12},{12,4},... | collective-permute-start | bytes 1376264 | tf_op jit(solution)/shard_map/ppermute | solution.py:163
  78.3 12.2 %collective-permute-start.28 = (bf16[64,3584]{1,0:T(8,128)(2,1)S(1)}, bf16[64,3584]{1,0:T(8,128)(2,1)S(1)}, u32[]{:S(2)}, u32[]{:S(2)}) collective-permute-start(bf16[64,3584]{1,0:T(8,128)(2,1)S(1)} %shard_map.111), channel_id=1, source_target_pairs={{0,4},{1,5},{4,6},{5,7},{6,2},{7,3},{2,0},{3,1},{8,12},{9,13},{12,... | collective-permute-start | bytes 1376264 | tf_op jit(solution)/shard_map/ppermute | solution.py:169
  79.8 15.0 %copy-start.2 = (bf16[8,256,576]{1,2,0:T(8,128)(2,1)S(1)}, bf16[8,256,576]{1,2,0:T(8,128)(2,1)}, u32[]{:S(2)}) copy-start(bf16[8,256,576]{1,2,0:T(8,128)(2,1)} %param.16) | copy-start | bytes 7077892
  79.8 13.5 %collective-permute-start.20 = (bf16[64,3584]{1,0:T(8,128)(2,1)S(1)}, bf16[64,3584]{1,0:T(8,128)(2,1)S(1)}, u32[]{:S(2)}, u32[]{:S(2)}) collective-permute-start(bf16[64,3584]{1,0:T(8,128)(2,1)S(1)} %get-tuple-element.73), channel_id=1, source_target_pairs={{0,8},{8,0},{1,9},{9,1},{2,10},{10,2},{3,11},{11,3},{4,12},{12,4},... | collective-permute-start | bytes 1376264 | tf_op jit(solution)/shard_map/ppermute | solution.py:163
  80.0 13.4 %collective-permute-start.26 = (bf16[64,3584]{1,0:T(8,128)(2,1)S(1)}, bf16[64,3584]{1,0:T(8,128)(2,1)S(1)}, u32[]{:S(2)}, u32[]{:S(2)}) collective-permute-start(bf16[64,3584]{1,0:T(8,128)(2,1)S(1)} %add_convert_fusion), channel_id=1, source_target_pairs={{0,1},{1,0},{2,3},{3,2},{4,5},{5,4},{6,7},{7,6},{8,9},{9,8},{10,11... | collective-permute-start | bytes 1376264 | tf_op jit(solution)/shard_map/ppermute | solution.py:166
  82.4 20.4 %collective-permute-start.9 = (bf16[64,3584]{1,0:T(8,128)(2,1)}, bf16[64,3584]{1,0:T(8,128)(2,1)S(1)}, u32[]{:S(2)}, u32[]{:S(2)}) collective-permute-start(bf16[64,3584]{1,0:T(8,128)(2,1)} %add_convert_fusion.3), channel_id=1, source_target_pairs={{0,1},{1,0},{2,3},{3,2},{4,5},{5,4},{6,7},{7,6},{8,9},{9,8},{10,11... | collective-permute-start | bytes 1376264 | tf_op jit(solution)/shard_map/ppermute | solution.py:166
  93.6 11.8 %collective-permute-start.29 = (bf16[64,3584]{1,0:T(8,128)(2,1)S(1)}, bf16[64,3584]{1,0:T(8,128)(2,1)S(1)}, u32[]{:S(2)}, u32[]{:S(2)}) collective-permute-start(bf16[64,3584]{1,0:T(8,128)(2,1)S(1)} %shard_map.112), channel_id=1, source_target_pairs={{0,4},{1,5},{4,6},{5,7},{6,2},{7,3},{2,0},{3,1},{8,12},{9,13},{12,... | collective-permute-start | bytes 1376264 | tf_op jit(solution)/shard_map/ppermute | solution.py:169

commit v6 on v5

--- a/solution.py
+++ b/solution.py
@@ -152,7 +152,6 @@
     rank_count = lax.axis_size("rank")
     experts = node_count * rank_count * w_gate.shape[0]
     steps = rank_count // PAIR
-    f32, bf16 = jnp.float32, jnp.bfloat16
 
     line = list(range(0, steps, 2)) + list(range(1, steps, 2))[::-1]
     hops = [
@@ -183,7 +182,7 @@
         got.append(core(sent))
 
     def away(slot):
-        return pair((keep_y[slot].astype(f32) + got_y[slot].astype(f32)).astype(bf16))
+        return pair(add(keep_y[slot], got_y[slot]))
 
     def onward(slot, carried):
         terms = [keep[slot], got[slot], back[slot]]

time: 107 us -> 105 us (0.981)
  waiting for transfers between devices: 38.2 us -> 35.8 us
  Pallas kernels: 35 us -> 36.2 us
  other arithmetic: 2.71 us -> 1.51 us
    ppermute x7, waiting for transfers between devices: 26.3 us -> 24 us  [ring(): return lax.ppermute(value, 'rank', hops)]
    ppermute x7, waiting for transfers between devices: 11.9 us -> 9.73 us  [pair(): return lax.ppermute(value, 'rank', [(i, i ^ 1) for i in range(rank_count)])]
    ppermute x16, waiting for transfers between devices: 0.04 us -> 2.02 us  [core(): return lax.ppermute(value, 'node', [(i, 1 - i) for i in range(node_count)])]
    convert_element_type x4 -> x0, other arithmetic: 1.2 us -> none  [away(): (keep_y[slot].astype(f32) + got_y[slot].astype(f32)).astype(bf16)]
  transfers between devices with their start and end apart: 30 -> 30, of which waited for: 14 -> 14; matrix products, arithmetic and copies ran while one was open for 7% -> 6% of each run, Pallas kernels for 30% -> 31%
where the time goes in v6:
time: 105 us
  Pallas kernels  36.2 us (34%)
  waiting for transfers between devices  35.8 us (34%)
  starting transfers between devices  25.4 us (24%)
  matrix products  5.12 us (5%)
  other arithmetic  1.51 us (1%)
    pallas_call x4, Pallas kernels, run_expert(): pl.pallas_call(lambda *refs: expert_kernel(experts, *refs), out_shape=[ja...  24.2 us
    ppermute x7, waiting for transfers between devices, ring(): return lax.ppermute(value, 'rank', hops)  24 us
    ppermute x7, starting transfers between devices, ring(): return lax.ppermute(value, 'rank', hops)  11.7 us
    ppermute x7, starting transfers between devices, pair(): return lax.ppermute(value, 'rank', [(i, i ^ 1) for i in range(rank_count)])  9.88 us
    ppermute x7, waiting for transfers between devices, pair(): return lax.ppermute(value, 'rank', [(i, i ^ 1) for i in range(rank_count)])  9.73 us
    pallas_call x1, Pallas kernels, load_inside(): pl.pallas_call(load_kernel, out_shape=[jax.ShapeDtypeStruct(a.shape, a.dt...  7.34 us
    ppermute x16, starting transfers between devices, core(): return lax.ppermute(value, 'node', [(i, 1 - i) for i in range(node_count)])  3.8 us
    dot_general x1, matrix products, attend(): jnp.einsum('bhl,blc->bhc', softmax_weights, latent_values, preferred_elem...  3.73 us
  transfers between devices with their start and end apart: 30, of which 14 were waited for; matrix products, arithmetic and copies ran while one was open for 6% of the time, Pallas kernels for 31%

profile of v6, /device:TPU:0, one launch (start us, length us, event | category | flops | bytes accessed | tf_op | source)
XLA Modules:
  0.0 104.8 jit_solution(6418286086875020768)
XLA Ops:
  0.6 0.0 copy-start
  0.6 2.6 %shard_map.104.refs_0_ = bf16[64,3712]{1,0:T(8,128)(2,1)} custom-call(bf16[64,3584]{1,0:T(8,128)(2,1)} %refs_0_.1, s32[8,64]{1,0:T(8,128)} %bitcast.12, f32[8,64]{1,0:T(8,128)} %bitcast.13), custom_call_target="tpu_custom_call" | custom-call | bytes 917504 | tf_op jit(solution)/shard_map/pallas_call | solution.py:57
  3.2 0.5 collective-permute-start
  3.7 3.6 %collective-permute-start.1 = (bf16[64,3712]{1,0:T(8,128)(2,1)}, bf16[64,3712]{1,0:T(8,128)(2,1)S(1)}, u32[]{:S(2)}, u32[]{:S(2)}) collective-permute-start(bf16[64,3712]{1,0:T(8,128)(2,1)} %shard_map.104.refs_0_), channel_id=1, source_target_pairs={{0,4},{1,5},{4,6},{5,7},{6,2},{7,3},{2,0},{3,1},{8,12},{9,13},{12,... | collective-permute-start | bytes 1425416 | tf_op jit(solution)/shard_map/ppermute | solution.py:168
  7.4 1.5 %collective-permute-start.2 = (bf16[64,3712]{1,0:T(8,128)(2,1)}, bf16[64,3712]{1,0:T(8,128)(2,1)S(1)}, u32[]{:S(2)}, u32[]{:S(2)}) collective-permute-start(bf16[64,3712]{1,0:T(8,128)(2,1)} %shard_map.104.refs_0_), channel_id=1, source_target_pairs={{0,1},{1,0},{2,3},{3,2},{4,5},{5,4},{6,7},{7,6},{8,9},{9,8},{10,11... | collective-permute-start | bytes 1425416 | tf_op jit(solution)/shard_map/ppermute | solution.py:165
  8.9 7.3 %shard_map.105 = (bf16[3584,1024]{1,0:T(8,128)(2,1)S(1)}, bf16[3584,1024]{1,0:T(8,128)(2,1)S(1)}, bf16[1024,3584]{1,0:T(8,128)(2,1)S(1)}) custom-call(bf16[3584,1024]{1,0:T(8,128)(2,1)} %bitcast.9, bf16[3584,1024]{1,0:T(8,128)(2,1)} %bitcast.10, bf16[1024,3584]{1,0:T(8,128)(2,1)} %bitcast.11), custom_call_target="tpu_custom_call" | custom-call | bytes 22020096 | tf_op jit(solution)/shard_map/pallas_call | solution.py:101
  16.3 2.2 %collective-permute-done.1.refs_0_ = bf16[64,3712]{1,0:T(8,128)(2,1)S(1)} collective-permute-done((bf16[64,3712]{1,0:T(8,128)(2,1)}, bf16[64,3712]{1,0:T(8,128)(2,1)S(1)}, u32[]{:S(2)}, u32[]{:S(2)}) %collective-permute-start.1) | collective-permute-done | bytes 475168 | tf_op jit(solution)/shard_map/ppermute | solution.py:168
  18.4 2.1 %collective-permute-done.2.refs_2_ = bf16[64,3712]{1,0:T(8,128)(2,1)S(1)} collective-permute-done((bf16[64,3712]{1,0:T(8,128)(2,1)}, bf16[64,3712]{1,0:T(8,128)(2,1)S(1)}, u32[]{:S(2)}, u32[]{:S(2)}) %collective-permute-start.2) | collective-permute-done | bytes 475168 | tf_op jit(solution)/shard_map/ppermute | solution.py:165
  20.5 0.0 collective-permute-start.3
  20.5 0.5 collective-permute-start.5
  21.1 1.6 %collective-permute-start.6 = (bf16[64,3712]{1,0:T(8,128)(2,1)S(1)}, bf16[64,3712]{1,0:T(8,128)(2,1)S(1)}, u32[]{:S(2)}, u32[]{:S(2)}) collective-permute-start(bf16[64,3712]{1,0:T(8,128)(2,1)S(1)} %collective-permute-done.1.refs_0_), channel_id=1, source_target_pairs={{0,4},{1,5},{4,6},{5,7},{6,2},{7,3},{2,0},{3,1},{8,12},{9,13},{12,... | collective-permute-start | bytes 1425416 | tf_op jit(solution)/shard_map/ppermute | solution.py:168
  22.6 1.5 %collective-permute-start.7 = (bf16[64,3712]{1,0:T(8,128)(2,1)S(1)}, bf16[64,3712]{1,0:T(8,128)(2,1)S(1)}, u32[]{:S(2)}, u32[]{:S(2)}) collective-permute-start(bf16[64,3712]{1,0:T(8,128)(2,1)S(1)} %collective-permute-done.1.refs_0_), channel_id=1, source_target_pairs={{0,1},{1,0},{2,3},{3,2},{4,5},{5,4},{6,7},{7,6},{8,9},{9,8},{10,11... | collective-permute-start | bytes 1425416 | tf_op jit(solution)/shard_map/ppermute | solution.py:165
  24.1 0.0 collective-permute-done.3.refs_3_
  24.2 6.6 %shard_map.106 = (bf16[64,3584]{1,0:T(8,128)(2,1)S(1)}, bf16[64,3584]{1,0:T(8,128)(2,1)S(1)}, bf16[64,3584]{1,0:T(8,128)(2,1)}, bf16[64,3584]{1,0:T(8,128)(2,1)S(1)}) custom-call(bf16[64,3712]{1,0:T(8,128)(2,1)S(1)} %copy-done.1, bf16[64,3712]{1,0:T(8,128)(2,1)S(1)} %collective-permute-done.refs_1_, bf16[64,3712]{1,0:T(8,128)(2,1)S(1)} %collective-permute-done.2.refs_2_, ...), custom_call_target="tpu_custom_call" | custom-call | tf_op jit(solution)/shard_map/pallas_call | solution.py:118
  30.8 0.0 collective-permute-done.5.refs_1_
  30.8 3.0 %collective-permute-done.6.refs_0_ = bf16[64,3712]{1,0:T(8,128)(2,1)S(1)} collective-permute-done((bf16[64,3712]{1,0:T(8,128)(2,1)S(1)}, bf16[64,3712]{1,0:T(8,128)(2,1)S(1)}, u32[]{:S(2)}, u32[]{:S(2)}) %collective-permute-start.6) | collective-permute-done | bytes 475168 | tf_op jit(solution)/shard_map/ppermute | solution.py:168
  33.8 1.3 %collective-permute-done.7.refs_2_ = bf16[64,3712]{1,0:T(8,128)(2,1)S(1)} collective-permute-done((bf16[64,3712]{1,0:T(8,128)(2,1)S(1)}, bf16[64,3712]{1,0:T(8,128)(2,1)S(1)}, u32[]{:S(2)}, u32[]{:S(2)}) %collective-permute-start.7) | collective-permute-done | bytes 475168 | tf_op jit(solution)/shard_map/ppermute | solution.py:165
  35.1 0.0 collective-permute-start.10
  35.1 0.5 collective-permute-start.11
  35.6 1.2 %collective-permute-start.12 = (bf16[64,3712]{1,0:T(8,128)(2,1)S(1)}, bf16[64,3712]{1,0:T(8,128)(2,1)S(1)}, u32[]{:S(2)}, u32[]{:S(2)}) collective-permute-start(bf16[64,3712]{1,0:T(8,128)(2,1)S(1)} %collective-permute-done.6.refs_0_), channel_id=1, source_target_pairs={{0,4},{1,5},{4,6},{5,7},{6,2},{7,3},{2,0},{3,1},{8,12},{9,13},{12,... | collective-permute-start | bytes 1425416 | tf_op jit(solution)/shard_map/ppermute | solution.py:168
  36.8 1.5 %collective-permute-start.13 = (bf16[64,3712]{1,0:T(8,128)(2,1)S(1)}, bf16[64,3712]{1,0:T(8,128)(2,1)S(1)}, u32[]{:S(2)}, u32[]{:S(2)}) collective-permute-start(bf16[64,3712]{1,0:T(8,128)(2,1)S(1)} %collective-permute-done.6.refs_0_), channel_id=1, source_target_pairs={{0,1},{1,0},{2,3},{3,2},{4,5},{5,4},{6,7},{7,6},{8,9},{9,8},{10,11... | collective-permute-start | bytes 1425416 | tf_op jit(solution)/shard_map/ppermute | solution.py:165
  38.3 5.9 %shard_map.108 = (bf16[64,3584]{1,0:T(8,128)(2,1)S(1)}, bf16[64,3584]{1,0:T(8,128)(2,1)S(1)}, bf16[64,3584]{1,0:T(8,128)(2,1)S(1)}, bf16[64,3584]{1,0:T(8,128)(2,1)S(1)}) custom-call(bf16[64,3712]{1,0:T(8,128)(2,1)S(1)} %collective-permute-done.1.refs_0_, bf16[64,3712]{1,0:T(8,128)(2,1)S(1)} %collective-permute-done.5.refs_1_, ...), custom_call_target="tpu_custom_call" | custom-call | tf_op jit(solution)/shard_map/pallas_call | solution.py:118
  44.2 0.1 collective-permute-start.14
  44.3 4.1 %collective-permute-done.12.refs_0_ = bf16[64,3712]{1,0:T(8,128)(2,1)S(1)} collective-permute-done((bf16[64,3712]{1,0:T(8,128)(2,1)S(1)}, bf16[64,3712]{1,0:T(8,128)(2,1)S(1)}, u32[]{:S(2)}, u32[]{:S(2)}) %collective-permute-start.12) | collective-permute-done | bytes 475168 | tf_op jit(solution)/shard_map/ppermute | solution.py:168
  48.4 0.9 collective-permute-done.13.refs_2_
  49.3 0.0 collective-permute-start.16
  49.3 0.5 collective-permute-start.17
  49.8 1.2 %collective-permute-start.18 = (bf16[64,3712]{1,0:T(8,128)(2,1)S(1)}, bf16[64,3712]{1,0:T(8,128)(2,1)S(1)}, u32[]{:S(2)}, u32[]{:S(2)}) collective-permute-start(bf16[64,3712]{1,0:T(8,128)(2,1)S(1)} %collective-permute-done.13.refs_2_), channel_id=1, source_target_pairs={{0,4},{1,5},{4,6},{5,7},{6,2},{7,3},{2,0},{3,1},{8,12},{9,13},{12,... | collective-permute-start | bytes 1425416 | tf_op jit(solution)/shard_map/ppermute | solution.py:168
  51.0 0.1 shard_map.109
  51.1 1.6 %collective-permute-start.15 = (bf16[64,3584]{1,0:T(8,128)(2,1)S(1)}, bf16[64,3584]{1,0:T(8,128)(2,1)S(1)}, u32[]{:S(2)}, u32[]{:S(2)}) collective-permute-start(bf16[64,3584]{1,0:T(8,128)(2,1)S(1)} %shard_map.109), channel_id=1, source_target_pairs={{0,1},{1,0},{2,3},{3,2},{4,5},{5,4},{6,7},{7,6},{8,9},{9,8},{10,11... | collective-permute-start | bytes 1376264 | tf_op jit(solution)/shard_map/ppermute | solution.py:165
  52.7 5.9 %shard_map.110 = (bf16[64,3584]{1,0:T(8,128)(2,1)S(1)}, bf16[64,3584]{1,0:T(8,128)(2,1)S(1)}, bf16[64,3584]{1,0:T(8,128)(2,1)S(1)}, bf16[64,3584]{1,0:T(8,128)(2,1)S(1)}) custom-call(bf16[64,3712]{1,0:T(8,128)(2,1)S(1)} %collective-permute-done.6.refs_0_, bf16[64,3712]{1,0:T(8,128)(2,1)S(1)} %collective-permute-done.11.refs_1_, ...), custom_call_target="tpu_custom_call" | custom-call | tf_op jit(solution)/shard_map/pallas_call | solution.py:118
  58.6 4.0 %collective-permute-done.18.refs_2_ = bf16[64,3712]{1,0:T(8,128)(2,1)S(1)} collective-permute-done((bf16[64,3712]{1,0:T(8,128)(2,1)S(1)}, bf16[64,3712]{1,0:T(8,128)(2,1)S(1)}, u32[]{:S(2)}, u32[]{:S(2)}) %collective-permute-start.18) | collective-permute-done | bytes 475168 | tf_op jit(solution)/shard_map/ppermute | solution.py:168
  62.6 0.7 collective-permute-done.15.refs_2_
  63.3 0.5 collective-permute-start.23
  63.9 0.0 collective-permute-start.21
  63.9 2.0 %collective-permute-done.23.refs_1_ = bf16[64,3584]{1,0:T(8,128)(2,1)S(1)} collective-permute-done((bf16[64,3584]{1,0:T(8,128)(2,1)S(1)}, bf16[64,3584]{1,0:T(8,128)(2,1)S(1)}, u32[]{:S(2)}, u32[]{:S(2)}) %collective-permute-start.23) | collective-permute-done | bytes 458784 | tf_op jit(solution)/shard_map/ppermute | solution.py:162
  65.8 0.2 shard_map.113
  66.0 1.4 %collective-permute-start.24 = (bf16[64,3584]{1,0:T(8,128)(2,1)S(1)}, bf16[64,3584]{1,0:T(8,128)(2,1)S(1)}, u32[]{:S(2)}, u32[]{:S(2)}) collective-permute-start(bf16[64,3584]{1,0:T(8,128)(2,1)S(1)} %shard_map.113), channel_id=1, source_target_pairs={{0,4},{1,5},{4,6},{5,7},{6,2},{7,3},{2,0},{3,1},{8,12},{9,13},{12,... | collective-permute-start | bytes 1376264 | tf_op jit(solution)/shard_map/ppermute | solution.py:168
  67.4 0.1 shard_map.112
  67.5 1.6 %collective-permute-start.22 = (bf16[64,3584]{1,0:T(8,128)(2,1)S(1)}, bf16[64,3584]{1,0:T(8,128)(2,1)S(1)}, u32[]{:S(2)}, u32[]{:S(2)}) collective-permute-start(bf16[64,3584]{1,0:T(8,128)(2,1)S(1)} %shard_map.112), channel_id=1, source_target_pairs={{0,1},{1,0},{2,3},{3,2},{4,5},{5,4},{6,7},{7,6},{8,9},{9,8},{10,11... | collective-permute-start | bytes 1376264 | tf_op jit(solution)/shard_map/ppermute | solution.py:165
  69.1 5.9 %shard_map.111 = (bf16[64,3584]{1,0:T(8,128)(2,1)S(1)}, bf16[64,3584]{1,0:T(8,128)(2,1)S(1)}, bf16[64,3584]{1,0:T(8,128)(2,1)S(1)}, bf16[64,3584]{1,0:T(8,128)(2,1)S(1)}) custom-call(bf16[64,3712]{1,0:T(8,128)(2,1)S(1)} %collective-permute-done.12.refs_0_, bf16[64,3712]{1,0:T(8,128)(2,1)S(1)} %collective-permute-done.17.refs_1_, ...), custom_call_target="tpu_custom_call" | custom-call | tf_op jit(solution)/shard_map/pallas_call | solution.py:118
  75.0 0.0 copy-start.3
  75.0 0.6 collective-permute-start.25
  75.6 0.1 collective-permute-start.8
  75.7 3.0 %collective-permute-done.24.refs_3_ = bf16[64,3584]{1,0:T(8,128)(2,1)S(1)} collective-permute-done((bf16[64,3584]{1,0:T(8,128)(2,1)S(1)}, bf16[64,3584]{1,0:T(8,128)(2,1)S(1)}, u32[]{:S(2)}, u32[]{:S(2)}) %collective-permute-start.24) | collective-permute-done | bytes 458784 | tf_op jit(solution)/shard_map/ppermute | solution.py:168
  78.6 1.3 %collective-permute-done.22.refs_2_ = bf16[64,3584]{1,0:T(8,128)(2,1)S(1)} collective-permute-done((bf16[64,3584]{1,0:T(8,128)(2,1)S(1)}, bf16[64,3584]{1,0:T(8,128)(2,1)S(1)}, u32[]{:S(2)}, u32[]{:S(2)}) %collective-permute-start.22) | collective-permute-done | bytes 458784 | tf_op jit(solution)/shard_map/ppermute | solution.py:165
  79.9 0.2 shard_map.115
  80.1 0.0 copy-start.2
  80.1 1.3 %collective-permute-start.28 = (bf16[64,3584]{1,0:T(8,128)(2,1)S(1)}, bf16[64,3584]{1,0:T(8,128)(2,1)S(1)}, u32[]{:S(2)}, u32[]{:S(2)}) collective-permute-start(bf16[64,3584]{1,0:T(8,128)(2,1)S(1)} %shard_map.115), channel_id=1, source_target_pairs={{0,4},{1,5},{4,6},{5,7},{6,2},{7,3},{2,0},{3,1},{8,12},{9,13},{12,... | collective-permute-start | bytes 1376264 | tf_op jit(solution)/shard_map/ppermute | solution.py:168
  81.4 0.1 shard_map.114
  81.5 1.6 %collective-permute-start.26 = (bf16[64,3584]{1,0:T(8,128)(2,1)S(1)}, bf16[64,3584]{1,0:T(8,128)(2,1)S(1)}, u32[]{:S(2)}, u32[]{:S(2)}) collective-permute-start(bf16[64,3584]{1,0:T(8,128)(2,1)S(1)} %shard_map.114), channel_id=1, source_target_pairs={{0,1},{1,0},{2,3},{3,2},{4,5},{5,4},{6,7},{7,6},{8,9},{9,8},{10,11... | collective-permute-start | bytes 1376264 | tf_op jit(solution)/shard_map/ppermute | solution.py:165
  83.1 0.1 iota_compare_fusion
  83.2 0.5 collective-permute-start.4
  83.7 0.1 shard_map.107
  83.8 0.6 collective-permute-start.9
  84.4 7.2 %collective-permute-done.28.refs_3_ = bf16[64,3584]{1,0:T(8,128)(2,1)S(1)} collective-permute-done((bf16[64,3584]{1,0:T(8,128)(2,1)S(1)}, bf16[64,3584]{1,0:T(8,128)(2,1)S(1)}, u32[]{:S(2)}, u32[]{:S(2)}) %collective-permute-start.28) | collective-permute-done | bytes 458784 | tf_op jit(solution)/shard_map/ppermute | solution.py:168
  91.6 3.5 %collective-permute-done.26.refs_2_ = bf16[64,3584]{1,0:T(8,128)(2,1)S(1)} collective-permute-done((bf16[64,3584]{1,0:T(8,128)(2,1)S(1)}, bf16[64,3584]{1,0:T(8,128)(2,1)S(1)}, u32[]{:S(2)}, u32[]{:S(2)}) %collective-permute-start.26) | collective-permute-done | bytes 458784 | tf_op jit(solution)/shard_map/ppermute | solution.py:165
  95.0 0.2 shard_map.116
  95.3 1.4 %collective-permute-start.29 = (bf16[64,3584]{1,0:T(8,128)(2,1)S(1)}, bf16[64,3584]{1,0:T(8,128)(2,1)S(1)}, u32[]{:S(2)}, u32[]{:S(2)}) collective-permute-start(bf16[64,3584]{1,0:T(8,128)(2,1)S(1)} %shard_map.116), channel_id=1, source_target_pairs={{0,4},{1,5},{4,6},{5,7},{6,2},{7,3},{2,0},{3,1},{8,12},{9,13},{12,... | collective-permute-start | bytes 1376264 | tf_op jit(solution)/shard_map/ppermute | solution.py:168
  96.7 1.4 %fusion.8 = f32[8,64,256]{2,1,0:T(8,128)} fusion(bf16[8,64,576]{2,1,0:T(8,128)(2,1)S(1)} %copy-done, bf16[8,256,576]{1,2,0:T(8,128)(2,1)S(1)} %copy-done.2, pred[8,256]{1,0:T(8,128)(4,1)S(1)} %iota_compare_fusion), kind=kOutput, calls=%fused_computation.7 | convolution fusion | flops 151257088 | bytes 3475456 | tf_op jit(solution)/shard_map/bhc,blc->bhl/dot_general | solution.py:19
  98.1 1.4 %fusion.11 = f32[8,64]{1,0:T(8,128)S(1)} fusion(f32[8,64,256]{2,1,0:T(8,128)} %fusion.8), kind=kOutput, calls=%fused_computation.12 | output fusion | flops 262399 | bytes 526336 | tf_op jit(solution)/shard_map/sub | solution.py:25
  99.5 3.7 %fusion.3 = bf16[8,64,512]{2,1,0:T(8,128)(2,1)} fusion(bf16[8,256,576]{1,2,0:T(8,128)(2,1)} %param.16, f32[8,64]{1,0:T(8,128)S(1)} %fusion.11, f32[8,64,256]{2,1,0:T(8,128)} %fusion.8), kind=kOutput, calls=%fused_computation.3 | convolution fusion | flops 134873856 | bytes 3672064 | tf_op jit(solution)/shard_map/bhl,blc->bhc/dot_general | solution.py:28
  103.2 0.6 collective-permute-done.29.refs_3_
  103.8 1.0 shard_map.117
  (22 shorter events, 0.1 us)
Async XLA Ops:
  0.6 96.1 %copy-start = (bf16[8,64,576]{2,1,0:T(8,128)(2,1)S(1)}, bf16[8,64,576]{2,1,0:T(8,128)(2,1)}, u32[]{:S(2)}) copy-start(bf16[8,64,576]{2,1,0:T(8,128)(2,1)} %param.15) | copy-start | bytes 1769476
  3.2 13.0 %collective-permute-start = (bf16[64,3712]{1,0:T(8,128)(2,1)}, bf16[64,3712]{1,0:T(8,128)(2,1)S(1)}, u32[]{:S(2)}, u32[]{:S(2)}) collective-permute-start(bf16[64,3712]{1,0:T(8,128)(2,1)} %shard_map.104.refs_0_), channel_id=1, source_target_pairs={{0,8},{8,0},{1,9},{9,1},{2,10},{10,2},{3,11},{11,3},{4,12},{12,4},... | collective-permute-start | bytes 1425416 | tf_op jit(solution)/shard_map/ppermute | solution.py:162
  3.7 14.7 %collective-permute-start.1 = (bf16[64,3712]{1,0:T(8,128)(2,1)}, bf16[64,3712]{1,0:T(8,128)(2,1)S(1)}, u32[]{:S(2)}, u32[]{:S(2)}) collective-permute-start(bf16[64,3712]{1,0:T(8,128)(2,1)} %shard_map.104.refs_0_), channel_id=1, source_target_pairs={{0,4},{1,5},{4,6},{5,7},{6,2},{7,3},{2,0},{3,1},{8,12},{9,13},{12,... | collective-permute-start | bytes 1425416 | tf_op jit(solution)/shard_map/ppermute | solution.py:168
  7.4 13.2 %collective-permute-start.2 = (bf16[64,3712]{1,0:T(8,128)(2,1)}, bf16[64,3712]{1,0:T(8,128)(2,1)S(1)}, u32[]{:S(2)}, u32[]{:S(2)}) collective-permute-start(bf16[64,3712]{1,0:T(8,128)(2,1)} %shard_map.104.refs_0_), channel_id=1, source_target_pairs={{0,1},{1,0},{2,3},{3,2},{4,5},{5,4},{6,7},{7,6},{8,9},{9,8},{10,11... | collective-permute-start | bytes 1425416 | tf_op jit(solution)/shard_map/ppermute | solution.py:165
  8.9 15.2 %copy-start.1 = (bf16[64,3712]{1,0:T(8,128)(2,1)S(1)}, bf16[64,3712]{1,0:T(8,128)(2,1)}, u32[]{:S(2)}) copy-start(bf16[64,3712]{1,0:T(8,128)(2,1)} %shard_map.104.refs_0_) | copy-start | bytes 1425412
  20.5 3.6 %collective-permute-start.3 = (bf16[64,3712]{1,0:T(8,128)(2,1)S(1)}, bf16[64,3712]{1,0:T(8,128)(2,1)S(1)}, u32[]{:S(2)}, u32[]{:S(2)}) collective-permute-start(bf16[64,3712]{1,0:T(8,128)(2,1)S(1)} %collective-permute-done.2.refs_2_), channel_id=1, source_target_pairs={{0,8},{8,0},{1,9},{9,1},{2,10},{10,2},{3,11},{11,3},{4,12},{12,4},... | collective-permute-start | bytes 1425416 | tf_op jit(solution)/shard_map/ppermute | solution.py:162
  20.5 10.2 %collective-permute-start.5 = (bf16[64,3712]{1,0:T(8,128)(2,1)S(1)}, bf16[64,3712]{1,0:T(8,128)(2,1)S(1)}, u32[]{:S(2)}, u32[]{:S(2)}) collective-permute-start(bf16[64,3712]{1,0:T(8,128)(2,1)S(1)} %collective-permute-done.1.refs_0_), channel_id=1, source_target_pairs={{0,8},{8,0},{1,9},{9,1},{2,10},{10,2},{3,11},{11,3},{4,12},{12,4},... | collective-permute-start | bytes 1425416 | tf_op jit(solution)/shard_map/ppermute | solution.py:162
  21.1 12.8 %collective-permute-start.6 = (bf16[64,3712]{1,0:T(8,128)(2,1)S(1)}, bf16[64,3712]{1,0:T(8,128)(2,1)S(1)}, u32[]{:S(2)}, u32[]{:S(2)}) collective-permute-start(bf16[64,3712]{1,0:T(8,128)(2,1)S(1)} %collective-permute-done.1.refs_0_), channel_id=1, source_target_pairs={{0,4},{1,5},{4,6},{5,7},{6,2},{7,3},{2,0},{3,1},{8,12},{9,13},{12,... | collective-permute-start | bytes 1425416 | tf_op jit(solution)/shard_map/ppermute | solution.py:168
  22.6 12.5 %collective-permute-start.7 = (bf16[64,3712]{1,0:T(8,128)(2,1)S(1)}, bf16[64,3712]{1,0:T(8,128)(2,1)S(1)}, u32[]{:S(2)}, u32[]{:S(2)}) collective-permute-start(bf16[64,3712]{1,0:T(8,128)(2,1)S(1)} %collective-permute-done.1.refs_0_), channel_id=1, source_target_pairs={{0,1},{1,0},{2,3},{3,2},{4,5},{5,4},{6,7},{7,6},{8,9},{9,8},{10,11... | collective-permute-start | bytes 1425416 | tf_op jit(solution)/shard_map/ppermute | solution.py:165
  35.1 3.2 %collective-permute-start.10 = (bf16[64,3712]{1,0:T(8,128)(2,1)S(1)}, bf16[64,3712]{1,0:T(8,128)(2,1)S(1)}, u32[]{:S(2)}, u32[]{:S(2)}) collective-permute-start(bf16[64,3712]{1,0:T(8,128)(2,1)S(1)} %collective-permute-done.7.refs_2_), channel_id=1, source_target_pairs={{0,8},{8,0},{1,9},{9,1},{2,10},{10,2},{3,11},{11,3},{4,12},{12,4},... | collective-permute-start | bytes 1425416 | tf_op jit(solution)/shard_map/ppermute | solution.py:162
  35.1 9.2 %collective-permute-start.11 = (bf16[64,3712]{1,0:T(8,128)(2,1)S(1)}, bf16[64,3712]{1,0:T(8,128)(2,1)S(1)}, u32[]{:S(2)}, u32[]{:S(2)}) collective-permute-start(bf16[64,3712]{1,0:T(8,128)(2,1)S(1)} %collective-permute-done.6.refs_0_), channel_id=1, source_target_pairs={{0,8},{8,0},{1,9},{9,1},{2,10},{10,2},{3,11},{11,3},{4,12},{12,4},... | collective-permute-start | bytes 1425416 | tf_op jit(solution)/shard_map/ppermute | solution.py:162
  35.6 12.8 %collective-permute-start.12 = (bf16[64,3712]{1,0:T(8,128)(2,1)S(1)}, bf16[64,3712]{1,0:T(8,128)(2,1)S(1)}, u32[]{:S(2)}, u32[]{:S(2)}) collective-permute-start(bf16[64,3712]{1,0:T(8,128)(2,1)S(1)} %collective-permute-done.6.refs_0_), channel_id=1, source_target_pairs={{0,4},{1,5},{4,6},{5,7},{6,2},{7,3},{2,0},{3,1},{8,12},{9,13},{12,... | collective-permute-start | bytes 1425416 | tf_op jit(solution)/shard_map/ppermute | solution.py:168
  36.8 12.5 %collective-permute-start.13 = (bf16[64,3712]{1,0:T(8,128)(2,1)S(1)}, bf16[64,3712]{1,0:T(8,128)(2,1)S(1)}, u32[]{:S(2)}, u32[]{:S(2)}) collective-permute-start(bf16[64,3712]{1,0:T(8,128)(2,1)S(1)} %collective-permute-done.6.refs_0_), channel_id=1, source_target_pairs={{0,1},{1,0},{2,3},{3,2},{4,5},{5,4},{6,7},{7,6},{8,9},{9,8},{10,11... | collective-permute-start | bytes 1425416 | tf_op jit(solution)/shard_map/ppermute | solution.py:165
  44.2 6.8 %collective-permute-start.14 = (bf16[64,3584]{1,0:T(8,128)(2,1)S(1)}, bf16[64,3584]{1,0:T(8,128)(2,1)S(1)}, u32[]{:S(2)}, u32[]{:S(2)}) collective-permute-start(bf16[64,3584]{1,0:T(8,128)(2,1)S(1)} %get-tuple-element.66), channel_id=1, source_target_pairs={{0,8},{8,0},{1,9},{9,1},{2,10},{10,2},{3,11},{11,3},{4,12},{12,4},... | collective-permute-start | bytes 1376264 | tf_op jit(solution)/shard_map/ppermute | solution.py:162
  49.3 3.4 %collective-permute-start.16 = (bf16[64,3712]{1,0:T(8,128)(2,1)S(1)}, bf16[64,3712]{1,0:T(8,128)(2,1)S(1)}, u32[]{:S(2)}, u32[]{:S(2)}) collective-permute-start(bf16[64,3712]{1,0:T(8,128)(2,1)S(1)} %collective-permute-done.13.refs_2_), channel_id=1, source_target_pairs={{0,8},{8,0},{1,9},{9,1},{2,10},{10,2},{3,11},{11,3},{4,12},{12,4},... | collective-permute-start | bytes 1425416 | tf_op jit(solution)/shard_map/ppermute | solution.py:162
  49.3 9.3 %collective-permute-start.17 = (bf16[64,3712]{1,0:T(8,128)(2,1)S(1)}, bf16[64,3712]{1,0:T(8,128)(2,1)S(1)}, u32[]{:S(2)}, u32[]{:S(2)}) collective-permute-start(bf16[64,3712]{1,0:T(8,128)(2,1)S(1)} %collective-permute-done.12.refs_0_), channel_id=1, source_target_pairs={{0,8},{8,0},{1,9},{9,1},{2,10},{10,2},{3,11},{11,3},{4,12},{12,4},... | collective-permute-start | bytes 1425416 | tf_op jit(solution)/shard_map/ppermute | solution.py:162
  49.8 12.8 %collective-permute-start.18 = (bf16[64,3712]{1,0:T(8,128)(2,1)S(1)}, bf16[64,3712]{1,0:T(8,128)(2,1)S(1)}, u32[]{:S(2)}, u32[]{:S(2)}) collective-permute-start(bf16[64,3712]{1,0:T(8,128)(2,1)S(1)} %collective-permute-done.13.refs_2_), channel_id=1, source_target_pairs={{0,4},{1,5},{4,6},{5,7},{6,2},{7,3},{2,0},{3,1},{8,12},{9,13},{12,... | collective-permute-start | bytes 1425416 | tf_op jit(solution)/shard_map/ppermute | solution.py:168
  51.1 12.2 %collective-permute-start.15 = (bf16[64,3584]{1,0:T(8,128)(2,1)S(1)}, bf16[64,3584]{1,0:T(8,128)(2,1)S(1)}, u32[]{:S(2)}, u32[]{:S(2)}) collective-permute-start(bf16[64,3584]{1,0:T(8,128)(2,1)S(1)} %shard_map.109), channel_id=1, source_target_pairs={{0,1},{1,0},{2,3},{3,2},{4,5},{5,4},{6,7},{7,6},{8,9},{9,8},{10,11... | collective-permute-start | bytes 1376264 | tf_op jit(solution)/shard_map/ppermute | solution.py:165
  63.3 5.8 %collective-permute-start.19 = (bf16[64,3712]{1,0:T(8,128)(2,1)S(1)}, bf16[64,3712]{1,0:T(8,128)(2,1)S(1)}, u32[]{:S(2)}, u32[]{:S(2)}) collective-permute-start(bf16[64,3712]{1,0:T(8,128)(2,1)S(1)} %collective-permute-done.18.refs_2_), channel_id=1, source_target_pairs={{0,8},{8,0},{1,9},{9,1},{2,10},{10,2},{3,11},{11,3},{4,12},{12,4},... | collective-permute-start | bytes 1425416 | tf_op jit(solution)/shard_map/ppermute | solution.py:162
  63.3 2.5 %collective-permute-start.23 = (bf16[64,3584]{1,0:T(8,128)(2,1)S(1)}, bf16[64,3584]{1,0:T(8,128)(2,1)S(1)}, u32[]{:S(2)}, u32[]{:S(2)}) collective-permute-start(bf16[64,3584]{1,0:T(8,128)(2,1)S(1)} %get-tuple-element.77), channel_id=1, source_target_pairs={{0,8},{8,0},{1,9},{9,1},{2,10},{10,2},{3,11},{11,3},{4,12},{12,4},... | collective-permute-start | bytes 1376264 | tf_op jit(solution)/shard_map/ppermute | solution.py:162
  63.9 3.6 %collective-permute-start.21 = (bf16[64,3584]{1,0:T(8,128)(2,1)S(1)}, bf16[64,3584]{1,0:T(8,128)(2,1)S(1)}, u32[]{:S(2)}, u32[]{:S(2)}) collective-permute-start(bf16[64,3584]{1,0:T(8,128)(2,1)S(1)} %get-tuple-element.75), channel_id=1, source_target_pairs={{0,8},{8,0},{1,9},{9,1},{2,10},{10,2},{3,11},{11,3},{4,12},{12,4},... | collective-permute-start | bytes 1376264 | tf_op jit(solution)/shard_map/ppermute | solution.py:162
  66.0 12.6 %collective-permute-start.24 = (bf16[64,3584]{1,0:T(8,128)(2,1)S(1)}, bf16[64,3584]{1,0:T(8,128)(2,1)S(1)}, u32[]{:S(2)}, u32[]{:S(2)}) collective-permute-start(bf16[64,3584]{1,0:T(8,128)(2,1)S(1)} %shard_map.113), channel_id=1, source_target_pairs={{0,4},{1,5},{4,6},{5,7},{6,2},{7,3},{2,0},{3,1},{8,12},{9,13},{12,... | collective-permute-start | bytes 1376264 | tf_op jit(solution)/shard_map/ppermute | solution.py:168
  67.5 12.3 %collective-permute-start.22 = (bf16[64,3584]{1,0:T(8,128)(2,1)S(1)}, bf16[64,3584]{1,0:T(8,128)(2,1)S(1)}, u32[]{:S(2)}, u32[]{:S(2)}) collective-permute-start(bf16[64,3584]{1,0:T(8,128)(2,1)S(1)} %shard_map.112), channel_id=1, source_target_pairs={{0,1},{1,0},{2,3},{3,2},{4,5},{5,4},{6,7},{7,6},{8,9},{9,8},{10,11... | collective-permute-start | bytes 1376264 | tf_op jit(solution)/shard_map/ppermute | solution.py:165
  69.1 10.8 %collective-permute-start.27 = (bf16[64,3584]{1,0:T(8,128)(2,1)S(1)}, bf16[64,3584]{1,0:T(8,128)(2,1)S(1)}, u32[]{:S(2)}, u32[]{:S(2)}) collective-permute-start(bf16[64,3584]{1,0:T(8,128)(2,1)S(1)} %get-tuple-element.83), channel_id=1, source_target_pairs={{0,8},{8,0},{1,9},{9,1},{2,10},{10,2},{3,11},{11,3},{4,12},{12,4},... | collective-permute-start | bytes 1376264 | tf_op jit(solution)/shard_map/ppermute | solution.py:162
  75.0 8.1 %copy-start.3 = (s32[8]{0:T(128)S(1)}, s32[8]{0:T(128)}, u32[]{:S(2)}) copy-start(s32[8]{0:T(128)} %param.17) | copy-start | bytes 100
  75.0 6.4 %collective-permute-start.25 = (bf16[64,3584]{1,0:T(8,128)(2,1)S(1)}, bf16[64,3584]{1,0:T(8,128)(2,1)S(1)}, u32[]{:S(2)}, u32[]{:S(2)}) collective-permute-start(bf16[64,3584]{1,0:T(8,128)(2,1)S(1)} %get-tuple-element.81), channel_id=1, source_target_pairs={{0,8},{8,0},{1,9},{9,1},{2,10},{10,2},{3,11},{11,3},{4,12},{12,4},... | collective-permute-start | bytes 1376264 | tf_op jit(solution)/shard_map/ppermute | solution.py:162
  75.6 8.1 %collective-permute-start.8 = (bf16[64,3584]{1,0:T(8,128)(2,1)S(1)}, bf16[64,3584]{1,0:T(8,128)(2,1)S(1)}, u32[]{:S(2)}, u32[]{:S(2)}) collective-permute-start(bf16[64,3584]{1,0:T(8,128)(2,1)S(1)} %get-tuple-element.59), channel_id=1, source_target_pairs={{0,8},{8,0},{1,9},{9,1},{2,10},{10,2},{3,11},{11,3},{4,12},{12,4},... | collective-permute-start | bytes 1376264 | tf_op jit(solution)/shard_map/ppermute | solution.py:162
  80.1 16.6 %copy-start.2 = (bf16[8,256,576]{1,2,0:T(8,128)(2,1)S(1)}, bf16[8,256,576]{1,2,0:T(8,128)(2,1)}, u32[]{:S(2)}) copy-start(bf16[8,256,576]{1,2,0:T(8,128)(2,1)} %param.16) | copy-start | bytes 7077892
  80.1 11.5 %collective-permute-start.28 = (bf16[64,3584]{1,0:T(8,128)(2,1)S(1)}, bf16[64,3584]{1,0:T(8,128)(2,1)S(1)}, u32[]{:S(2)}, u32[]{:S(2)}) collective-permute-start(bf16[64,3584]{1,0:T(8,128)(2,1)S(1)} %shard_map.115), channel_id=1, source_target_pairs={{0,4},{1,5},{4,6},{5,7},{6,2},{7,3},{2,0},{3,1},{8,12},{9,13},{12,... | collective-permute-start | bytes 1376264 | tf_op jit(solution)/shard_map/ppermute | solution.py:168
  81.5 13.5 %collective-permute-start.26 = (bf16[64,3584]{1,0:T(8,128)(2,1)S(1)}, bf16[64,3584]{1,0:T(8,128)(2,1)S(1)}, u32[]{:S(2)}, u32[]{:S(2)}) collective-permute-start(bf16[64,3584]{1,0:T(8,128)(2,1)S(1)} %shard_map.114), channel_id=1, source_target_pairs={{0,1},{1,0},{2,3},{3,2},{4,5},{5,4},{6,7},{7,6},{8,9},{9,8},{10,11... | collective-permute-start | bytes 1376264 | tf_op jit(solution)/shard_map/ppermute | solution.py:165
  83.1 11.9 %collective-permute-start.20 = (bf16[64,3584]{1,0:T(8,128)(2,1)S(1)}, bf16[64,3584]{1,0:T(8,128)(2,1)S(1)}, u32[]{:S(2)}, u32[]{:S(2)}) collective-permute-start(bf16[64,3584]{1,0:T(8,128)(2,1)S(1)} %get-tuple-element.73), channel_id=1, source_target_pairs={{0,8},{8,0},{1,9},{9,1},{2,10},{10,2},{3,11},{11,3},{4,12},{12,4},... | collective-permute-start | bytes 1376264 | tf_op jit(solution)/shard_map/ppermute | solution.py:162
  83.2 20.6 %collective-permute-start.4 = (bf16[64,3584]{1,0:T(8,128)(2,1)}, bf16[64,3584]{1,0:T(8,128)(2,1)S(1)}, u32[]{:S(2)}, u32[]{:S(2)}) collective-permute-start(bf16[64,3584]{1,0:T(8,128)(2,1)} %get-tuple-element.55), channel_id=1, source_target_pairs={{0,8},{8,0},{1,9},{9,1},{2,10},{10,2},{3,11},{11,3},{4,12},{12,4},... | collective-permute-start | bytes 1376264 | tf_op jit(solution)/shard_map/ppermute | solution.py:162
  83.8 19.4 %collective-permute-start.9 = (bf16[64,3584]{1,0:T(8,128)(2,1)S(1)}, bf16[64,3584]{1,0:T(8,128)(2,1)S(1)}, u32[]{:S(2)}, u32[]{:S(2)}) collective-permute-start(bf16[64,3584]{1,0:T(8,128)(2,1)S(1)} %shard_map.107), channel_id=1, source_target_pairs={{0,1},{1,0},{2,3},{3,2},{4,5},{5,4},{6,7},{7,6},{8,9},{9,8},{10,11... | collective-permute-start | bytes 1376264 | tf_op jit(solution)/shard_map/ppermute | solution.py:165
  95.3 8.5 %collective-permute-start.29 = (bf16[64,3584]{1,0:T(8,128)(2,1)S(1)}, bf16[64,3584]{1,0:T(8,128)(2,1)S(1)}, u32[]{:S(2)}, u32[]{:S(2)}) collective-permute-start(bf16[64,3584]{1,0:T(8,128)(2,1)S(1)} %shard_map.116), channel_id=1, source_target_pairs={{0,4},{1,5},{4,6},{5,7},{6,2},{7,3},{2,0},{3,1},{8,12},{9,13},{12,... | collective-permute-start | bytes 1376264 | tf_op jit(solution)/shard_map/ppermute | solution.py:168
